TPU v7x, 32 devices: a whole 2x2x4 slice. The times are simulated.
32 devices in a mesh: gx: 8 (over z, y), gz: 4 (over x, core).
Axes of the slice: x: 2, y: 2, z: 4, core: 2. Of those that a mesh axis runs over, the one named last changes fastest.
Arguments:
- solid_state: float32 [9, 20, 8192], P(None, None, ('gx', 'gz')), may hold values from -6 to 6
- jacobians: float32 [3, 9, 9, 8192], P(None, None, None, ('gx', 'gz')), may hold values from -2 to 2
- flux_solvers: float32 [4, 9, 9, 8192], P(None, None, None, ('gx', 'gz')), may hold values from -2 to 2
- stiffness: float32 [3, 20, 20], replicated, may hold values from -1.25 to 1.25
- trace_matrix: float32 [4, 10, 20], replicated, may hold values from -1.25 to 1.25
- lift_matrix: float32 [4, 20, 10], replicated, may hold values from -2 to 2
- neighbours: int32 [4, 8192], P(None, ('gx', 'gz')), may hold values from 0 to 1575, as said below
- send_faces: int32 [4, 4096], P(None, ('gx', 'gz')), may hold values from 0 to 1023, as said below
- surface_map: int32 [3, 5, 256], P(None, None, ('gx', 'gz')), may hold values from 0 to 16383, as said below
- surface_normals: float32 [3, 5, 256], P(None, None, ('gx', 'gz')), may hold values from -1 to 1
- air_state: float32 [4, 64, 64, 128], P(None, 'gx', 'gz'), may hold values from -6 to 6
- wind_field: float32 [3, 64, 64, 128], P(None, 'gx', 'gz'), may hold values from -0.3 to 0.3
- air_medium: float32 [2, 64, 64, 128], P(None, 'gx', 'gz'), may hold values from 0.05 to 0.25
Outputs:
- solid_next: float32 [9, 20, 8192], P(None, None, ('gx', 'gz'))
- air_next: float32 [4, 64, 64, 128], P(None, 'gx', 'gz')
Inputs may be any that keep to these rules, and one draw needn't show every extreme that they name: `neighbours`: entry [f, e] of a partition names what lies across face f of its tetrahedron e: below 1024 a face slot of the same partition (such slots name each other in pairs), from 1024 the slot 1024 + d * 128 + k of the k-th face shared in direction d, from 1536 the surface slot r * 8 + k. `send_faces`: the entries of a partition are distinct face slots; the face slot in [d, k] has neighbour entry 1024 + d * 128 + k. `surface_map`: row 0 holds distinct face slots, none of them in send_faces, whose neighbour entry is their surface slot; row 1 a cell index below 16384; row 2 is 1 for coupled slots and 0 otherwise. The coupled slots of one r are the lowest k; slots whose target strip lies outside 0 to 7 are uncoupled; the slots with r = 2 are all coupled.
All inputs are finite; a program needn't handle non-finite values.
Results may differ from a plain program's by a relative error of at most 0.0003.
Values sent between devices are 32-bit elements; how exact they have to be, the bound alone decides.
No kernel may reach another device: no remote copies, remote signals or barrier semaphores. Data moves between devices by JAX's collectives and lax.ppermute only.
A program may use at most 128 MiB of HBM per device.

v0:
```python
import functools

import jax
import jax.numpy as jnp
from jax import lax
from jax.experimental import pallas as pl
from jax.experimental.pallas import tpu as pltpu
from jax.sharding import PartitionSpec as P

ORDERS = 4
RADIUS = 4
SUBSTEPS = 3
ZRIM = 8
LANES = 128
HEAD = 8
FACE_ROWS = 10
K = 32
TIME_STEP = 0.5
STENCIL_WEIGHTS = (0.8, -0.2, 4.0 / 105.0, -1.0 / 280.0)
F32 = jnp.float32
BF16 = jnp.bfloat16


def call(kernel, name, outs, ins, scratch=(), flops=1_000_000, after=()):
    count, skip = len(ins), len(after)
    nbytes = 4 * sum(x.size for x in ins) + 4 * sum(functools.reduce(lambda m, n: m * n, s, 1) for s in outs)

    def body(*refs):
        kernel(*refs[:count], *refs[count + skip:])

    return pl.pallas_call(
        body,
        out_shape=[jax.ShapeDtypeStruct(s, F32) for s in outs],
        in_specs=[pl.BlockSpec(memory_space=pltpu.VMEM) for _ in ins]
        + [pl.BlockSpec(memory_space=pl.ANY) for _ in after],
        out_specs=[pl.BlockSpec(memory_space=pltpu.VMEM) for _ in outs],
        scratch_shapes=[pltpu.VMEM(s, F32) for s in scratch],
        compiler_params=pltpu.CompilerParams(vmem_limit_bytes=8 * 1024 * 1024),
        cost_estimate=pl.CostEstimate(flops=flops, bytes_accessed=nbytes, transcendentals=0),
        name=name,
    )(*ins, *after)


def swap(values, axis, odd, by=1):
    count = lax.axis_size(axis)
    pairs = []
    for i in range(count - by):
        if i // by % 2 == odd:
            pairs += [(i, i + by), (i + by, i)]
    return lax.ppermute(values, axis, pairs)


def exchange(xb, zb, xa, za):
    return swap(xb, "gx", 1), swap(zb, "gz", 1), swap(xa, "gx", 0), swap(za, "gz", 0)


def sides(axis, by=1):
    parity = (lax.axis_index(axis) // by) & 1
    return 1 - parity, parity


def by_side(pair, axis, by=1):
    first = sides(axis, by)[0]
    return jnp.where(first == 0, pair[0], pair[1]), jnp.where(first == 1, pair[0], pair[1])


def halves(values):
    high = values.astype(BF16)
    return high, (values - high.astype(F32)).astype(BF16)


def stacked_left(matrix):
    spread = matrix + pltpu.roll(matrix, K, 1) + pltpu.roll(matrix, 2 * K, 1)
    high = spread.astype(BF16).astype(F32)
    lane = lax.broadcasted_iota(jnp.int32, spread.shape, 1)
    return jnp.where(lane < 2 * K, high, spread - high).astype(BF16)[:, 0:3 * K]


def dot3(left, right):
    high, low = halves(right)
    return jnp.dot(left, jnp.concatenate([high, low, high], axis=0), preferred_element_type=F32)


def dot_exact(left, right, dims=(((1,), (0,)), ((), ()))):
    return lax.dot_general(
        left, right, dims, precision=lax.Precision.HIGHEST, preferred_element_type=F32
    )


def flat_slots(table, spread):
    rows, fields, slots = table.shape
    lane = lax.broadcasted_iota(jnp.int32, (8, LANES), 1)
    for r in range(rows):
        spread[r, 0:fields, 0:slots] = table[r].astype(F32)
    flat = jnp.zeros((8, LANES), F32)
    for r in range(rows):
        got = jnp.take_along_axis(spread[r], lane % slots, axis=1, mode="promise_in_bounds")
        flat = jnp.where(lane // slots == r, got, flat)
    return flat


def pack_x(out, at, source, side):
    fields, nx, nz, ny = source.shape
    start = side * (nx - RADIUS)
    rows = fields * RADIUS * nz
    at = HEAD + at * RADIUS * nz
    out[at:at + rows, :] = source[:, pl.ds(start, RADIUS)].reshape(rows, ny)


def pack_z(out, at, source, side):
    fields, nz = source.shape[0], source.shape[2]
    out[at:at + fields] = jnp.where(side == 1, source[:, :, nz - RADIUS:, :], source[:, :, 0:RADIUS, :])


def widen(ext, center, xb, zb, xa, za, first=0):
    fields, nx, nz, ny = center.shape
    ext[:, RADIUS:RADIUS + nx, ZRIM:ZRIM + nz] = center[...]
    for got, side in zip((xa, xb), sides("gx")):
        place = pl.ds(side * (nx + RADIUS), RADIUS)
        if len(got.shape) == 4:
            rows = got[first:first + fields]
        else:
            rows = got[HEAD:HEAD + fields * RADIUS * nz, :].reshape(fields, RADIUS, nz, ny)
        ext[:, place, ZRIM:ZRIM + nz] = rows
    low, high = by_side([got[first:first + fields] for got in (za, zb)], "gz")
    ext[:, RADIUS:RADIUS + nx, ZRIM - RADIUS:ZRIM] = low
    ext[:, RADIUS:RADIUS + nx, ZRIM + nz:ZRIM + nz + RADIUS] = high


def d1(load, x, lo, hi):
    total = None
    for m, w in enumerate(STENCIL_WEIGHTS, 1):
        term = w * (load(x + m, lo, hi) - load(x - m, lo, hi))
        total = term if total is None else total + term
    return total


def d2(load, x, lo, hi):
    total = None
    for m, w in enumerate(STENCIL_WEIGHTS, 1):
        term = w * (load(x, lo + m, hi + m) - load(x, lo - m, hi - m))
        total = term if total is None else total + term
    return total


def d3(values):
    width = values.shape[1]
    lane = lax.broadcasted_iota(jnp.int32, (1, width), 1)
    total = None
    for m, w in enumerate(STENCIL_WEIGHTS, 1):
        ahead = jnp.where(lane < width - m, w, 0.0) * pltpu.roll(values, width - m, 1)
        behind = jnp.where(lane >= m, w, 0.0) * pltpu.roll(values, m, 1)
        term = ahead - behind
        total = term if total is None else total + term
    return total


def field(ref, c):
    return lambda x, lo, hi: ref[c, x, lo:hi, :]


def plane(ref):
    return lambda x, lo, hi: ref[x, lo:hi, :]


def arrived(table, strip, band, n_gx, n_gz, reach, slots):
    lane = lax.broadcasted_iota(jnp.int32, (1, LANES), 1)
    got = jnp.zeros((1, LANES), F32)
    inside = (strip >= 0) & (strip < n_gx) & (band >= 0) & (band < n_gz)
    for r in range(reach):
        source = strip - (r - reach // 2)
        valid = inside & (source >= 0) & (source < n_gx)
        row = table[pl.ds(jnp.where(valid, source * n_gz + band, 0), 1), :]
        here = ((lane & (LANES // 2 - 1)) // slots == r) & valid
        got = jnp.where(here, row, got)
    turned = pltpu.roll(got, LANES // 2, 1)
    speed = jnp.where(lane < LANES // 2, got, turned)
    high = speed.astype(BF16).astype(F32)
    return jnp.where(lane < LANES // 2, high, speed - high), jnp.where(lane < LANES // 2, turned, got)


def cell_masks(cells, rows):
    cells = cells.astype(jnp.int32)
    place = lax.broadcasted_iota(jnp.int32, (rows, LANES), 0)
    third = lax.broadcasted_iota(jnp.int32, (LANES, LANES), 0)
    return cells // LANES == place, cells % LANES == third


def raw_rims_kernel(air, wind, xb, zb, xa, za):
    fields, nx = air.shape[:2]
    for out, side in zip((xa, xb), sides("gx")):
        rows = pl.ds(side * (nx - RADIUS), RADIUS)
        out[0:fields] = air[:, rows]
        out[fields:] = wind[:, rows]
    for out, side in zip((za, zb), sides("gz")):
        pack_z(out, 0, air, side)
        pack_z(out, fields, wind, side)


def lanes(at):
    return pl.ds(at if isinstance(at, int) else pl.multiple_of(at, LANES), LANES)


def jacobian_step(load, rot, emit, quants, dims, width):
    rows = rot.shape[0] // dims

    def half(h, carry):
        at = h * LANES
        acc = [None] * quants
        for d in range(dims):
            for q in range(quants):
                turned = rot[d * rows:(d + 1) * rows, lanes(q * width + at)].reshape(rows // 8, 8, LANES)
                for p in range(quants):
                    term = load(p, q, d, lanes(at)) * turned
                    acc[p] = term if acc[p] is None else acc[p] + term
        for p in range(quants):
            emit(p, at, acc[p].reshape(rows, LANES))
        return carry

    lax.fori_loop(0, width // LANES, half, 0)


def rotate(rot, left, source, quants, width):
    for q in range(quants):
        cut = slice(q * width, (q + 1) * width)
        rot[:, cut] = dot3(left, source[:, cut])


def take_slots(tiles, index):
    low = index % LANES
    high = index // LANES
    got = None
    for s, tile in enumerate(tiles):
        picked = jnp.take_along_axis(tile, low, axis=1, mode="promise_in_bounds")
        got = picked if got is None else jnp.where(high == s, picked, got)
    return got


def predict_kernel(
    state, jac, stiff, trace,
    integral, traces, kept,
    cur, rot, sp, tp,
):
    quants, basis, width = state.shape
    pad = sp.shape[0] // stiff.shape[0]
    face_basis, faces = trace.shape[:2]
    dims = stiff.shape[0]
    sp[...] = jnp.zeros_like(sp)
    tp[...] = jnp.zeros_like(tp)
    cur[...] = jnp.zeros_like(cur)
    for d in range(dims):
        sp[d * pad:d * pad + basis, 0:basis] = stiff[d]
    for f in range(faces):
        for j in range(face_basis):
            tp[f * 16 + j:f * 16 + j + 1, 0:basis] = trace[j, f:f + 1, :]
    for q in range(quants):
        cur[0:basis, q * width:(q + 1) * width] = state[q]
    kept[...] = state[...]
    integral[...] = TIME_STEP * cur[...]
    left = stacked_left(sp[...])

    def degree(k, weight):
        weight = jnp.where(k == 1, TIME_STEP**2 / 2, jnp.where(k == 2, TIME_STEP**3 / 6, TIME_STEP**4 / 24))
        rotate(rot, left, cur, quants, width)

        def emit(p, at, value):
            cut = lanes(p * width + at)
            cur[0:pad, cut] = -value
            integral[0:pad, cut] = integral[0:pad, cut] - weight * value

        jacobian_step(lambda p, q, d, cut: jac[p, q, d:d + 1, cut], rot, emit, quants, dims, width)
        return weight

    lax.fori_loop(1, ORDERS, degree, F32(0))
    restrict = stacked_left(tp[...])
    for q in range(quants):
        cut = slice(q * width, (q + 1) * width)
        done = dot3(restrict, integral[:, cut])
        for f in range(faces):
            traces[q, :, f * width:(f + 1) * width] = done[f * 16:(f + 1) * 16]


def own_list_kernel(traces, smap, normals, own, rows, spread):
    quants, _, all_slots = traces.shape
    slots = flat_slots(smap, spread)
    wanted = jnp.broadcast_to(slots[0:1].astype(jnp.int32), (16, LANES))

    def gather(q, carry):
        own[q] = take_slots([traces[q, :, s * LANES:(s + 1) * LANES] for s in range(all_slots // LANES)], wanted)
        return carry

    lax.fori_loop(0, quants, gather, 0)
    normal = flat_slots(normals, spread)
    speed = jnp.zeros((1, LANES), F32)
    for c in range(3):
        mean = jnp.sum(own[6 + c, 0:FACE_ROWS, :], axis=0, keepdims=True) * (1.0 / FACE_ROWS)
        speed = speed + normal[c:c + 1] * mean
    lane = lax.broadcasted_iota(jnp.int32, (1, LANES), 1)
    cells = pltpu.roll(slots[1:2], LANES // 2, 1)
    rows[...] = jnp.broadcast_to(jnp.where(lane < LANES // 2, slots[2:3] * speed, cells), rows.shape)


def outgoing_kernel(traces, sends, xa, xb, za, zb, picked):
    quants, _, slots = traces.shape
    rows = sent_rows(quants, FACE_ROWS)
    wanted = [jnp.broadcast_to(sends[d:d + 1, :], (16, LANES)) for d in range(4)]

    def gather(q, carry):
        tiles = [traces[q, :, s * LANES:(s + 1) * LANES] for s in range(slots // LANES)]
        for d in range(4):
            picked[d, q] = take_slots(tiles, wanted[d])
        return carry

    lax.fori_loop(0, quants, gather, 0)
    rest = FACE_ROWS - 8
    for axis, base, outs in (("gx", 0, (xa, xb)), ("gz", 2, (za, zb))):
        for out, side in zip(outs, sides(axis)):
            for q in range(quants):
                out[q * 8:q * 8 + 8, :] = picked[base + side, q, 0:8, :]
                at = quants * 8 + q * rest
                out[at:at + rest, :] = picked[base + side, q, 8:FACE_ROWS, :]
            out[quants * FACE_ROWS:, :] = jnp.zeros((rows - quants * FACE_ROWS, LANES), F32)


def pressure_rows(ext, wind, medium, x, nz):
    lo, hi = ZRIM, ZRIM + nz
    xe = x + RADIUS
    pressure = field(ext, 0)
    here = pressure(xe, lo, hi)
    divergence = d1(field(ext, 1), xe, lo, hi) + d2(field(ext, 2), xe, lo, hi) + d3(ext[3, xe, lo:hi, :])
    moved = (
        wind[0, x] * d1(pressure, xe, lo, hi)
        + wind[1, x] * d2(pressure, xe, lo, hi)
        + wind[2, x] * d3(here)
    )
    return here - medium[0, x] * divergence - moved


def pack_pressure(center, xs, zs):
    nx, nz, ny = center.shape[1:]
    for out, side in zip(xs, sides("gx")):
        start = side * (nx - RADIUS)
        out[HEAD:HEAD + RADIUS * nz, :] = center[0, pl.ds(start, RADIUS)].reshape(RADIUS * nz, ny)
    for out, side in zip(zs, sides("gz")):
        start = pl.multiple_of(side * (nz - ZRIM), ZRIM)
        out[HEAD:HEAD + nx * ZRIM, :] = center[0, :, pl.ds(start, ZRIM), :].reshape(nx * ZRIM, ny)


def widen_pressure(ext, center, xb, zb, xa, za):
    nx, nz, ny = center.shape
    ext[RADIUS:RADIUS + nx, ZRIM:ZRIM + nz] = center[...]
    for got, side in zip((xa, xb), sides("gx")):
        ext[pl.ds(side * (nx + RADIUS), RADIUS), ZRIM:ZRIM + nz] = got[HEAD:HEAD + RADIUS * nz, :].reshape(RADIUS, nz, ny)
    for got, side in zip((za, zb), sides("gz")):
        start = pl.multiple_of(side * (nz + ZRIM), ZRIM)
        ext[RADIUS:RADIUS + nx, pl.ds(start, ZRIM)] = got[HEAD:HEAD + nx * ZRIM, :].reshape(nx, ZRIM, ny)


def raw_pressure_kernel(
    air, wind, medium, xb, zb, xa, za, txa, txb, tza, tzb, pressure, oxb, ozb, oxa, oza, ext
):
    nx, nz, ny = air.shape[1:]
    widen(ext, air, xb, zb, xa, za)
    for x in range(nx):
        pressure[0, x] = pressure_rows(ext, wind, medium, x, nz)
    pack_pressure(pressure, (oxa, oxb), (oza, ozb))
    for out, sent in zip((oxa, oxb, oza, ozb), (txa, txb, tza, tzb)):
        out[0:HEAD, :] = jnp.zeros((HEAD, LANES), F32)
        out[out.shape[0] - sent.shape[0]:, :] = sent[...]


def put_rows(rows):
    place = lax.broadcasted_iota(jnp.int32, (HEAD, LANES), 0)
    out = jnp.zeros((HEAD, LANES), F32)
    for at, row in enumerate(rows):
        out = jnp.where(place == at, row, out)
    return out


def advection_kernel(air, wind, xb, zb, xa, za, moved, ext):
    nx, nz, ny = air.shape[1:]
    widen(ext, air, xb, zb, xa, za)
    lo, hi = ZRIM, ZRIM + nz
    for x in range(nx):
        xe = x + RADIUS
        for c in range(3):
            load = field(ext, 1 + c)
            moved[c, x] = (
                wind[0, x] * d1(load, xe, lo, hi)
                + wind[1, x] * d2(load, xe, lo, hi)
                + wind[2, x] * d3(load(xe, lo, hi))
            )


def velocities(out, center, moved, medium, wide, nx, nz):
    lo, hi = ZRIM, ZRIM + nz
    load = plane(wide)
    for x in range(nx):
        xe = x + RADIUS
        slopes = (d1(load, xe, lo, hi), d2(load, xe, lo, hi), d3(load(xe, lo, hi)))
        out[0, x] = load(xe, lo, hi)
        for c in range(3):
            out[1 + c, x] = center[1 + c, x] - medium[1, x] * slopes[c] - moved[c, x]


def pack_air(out, xb, zb, xa, za):
    for rim, side in zip((xa, xb), sides("gx")):
        pack_x(rim, 0, out, side)
    for rim, side in zip((za, zb), sides("gz")):
        pack_z(rim, 0, out, side)


def injected_kernel(
    n_gx, n_gz, air, wind, medium, raw, moved, wxb, wzb, wxa, wza, pxb, pzb, pxa, pza, table, smap,
    out, oxb, ozb, oxa, oza, answer, spread, wide, wide_wind,
):
    nx, nz, ny = air.shape[1:]
    reach, _, slots = smap.shape
    strip, band = lax.axis_index("gx"), lax.axis_index("gz")
    mul = functools.partial(
        lax.dot_general, dimension_numbers=(((1,), (1,)), ((), ())), preferred_element_type=F32
    )
    for da in range(3):
        for db in range(3):
            speed, cells = arrived(table, strip + da - 1, band + db - 1, n_gx, n_gz, reach, slots)
            row_mask, third_mask = cell_masks(cells, nx * nz)
            columns = jnp.where(third_mask, 1.0, 0.0).astype(BF16)
            if da == 1 and db == 1:
                seen, rest = halves(air[0].reshape(nx * nz, ny))
                looked = jnp.dot(seen, columns, preferred_element_type=F32)
                looked = looked + jnp.dot(rest, columns, preferred_element_type=F32)
                answer[...] = jnp.sum(jnp.where(row_mask, looked, 0.0), axis=0, keepdims=True)
            block = mul(jnp.where(row_mask, speed, 0.0).astype(BF16), columns)
            spread[da * nx:(da + 1) * nx, db * nz:(db + 1) * nz] = block.reshape(nx, nz, ny)
    widen(wide_wind, wind, wxb, wzb, wxa, wza, first=air.shape[0])
    widen_pressure(wide, raw.at[0], pxb, pzb, pxa, pza)
    load = plane(spread)
    for x in range(nx + 2 * RADIUS):
        xs = x + nx - RADIUS
        if RADIUS <= x < RADIUS + nx:
            lo, hi = 0, nz + 2 * ZRIM
        else:
            lo, hi = ZRIM, ZRIM + nz
        slo, shi = lo + nz - ZRIM, hi + nz - ZRIM
        here = load(xs, slo, shi)
        turned = (
            wide_wind[0, x, lo:hi, :] * d1(load, xs, slo, shi)
            + wide_wind[1, x, lo:hi, :] * d2(load, xs, slo, shi)
            + wide_wind[2, x, lo:hi, :] * d3(here)
        )
        wide[x, lo:hi, :] = wide[x, lo:hi, :] + (here - turned)
    velocities(out, air, moved, medium, wide, nx, nz)
    pack_air(out, oxb, ozb, oxa, oza)
    for rim in (oxa, oxb):
        rim[0:HEAD, :] = put_rows((answer[...],))


def pressure_kernel(air, wind, medium, xb, zb, xa, za, answer, pressure, oxb, ozb, oxa, oza, ext):
    nx, nz, ny = air.shape[1:]
    widen(ext, air, xb, zb, xa, za)
    for x in range(nx):
        pressure[0, x] = pressure_rows(ext, wind, medium, x, nz)
    pack_pressure(pressure, (oxa, oxb), (oza, ozb))
    low, high = by_side((xa[0:1, :], xb[0:1, :]), "gx")
    for rim in (oxa, oxb):
        rim[0:HEAD, :] = put_rows((answer[...], low, high))
    for rim in (oza, ozb):
        rim[0:HEAD, :] = jnp.zeros((HEAD, LANES), F32)


def velocity_kernel(air, pressure, medium, moved, xb, zb, xa, za, out, *rest):
    nx, nz, ny = air.shape[1:]
    wide = rest[-1]
    widen_pressure(wide, pressure.at[0], xb, zb, xa, za)
    velocities(out, air, moved, medium, wide, nx, nz)
    if len(rest) > 1:
        pack_air(out, *rest[:-1])
        for rim in (rest[0], rest[2]):
            rim[0:HEAD, :] = jnp.zeros((HEAD, LANES), F32)


def volume_kernel(state, integral, jac, stiff, out, token, rot, sp):
    quants, basis, width = state.shape
    dims = stiff.shape[0]
    pad = sp.shape[0] // dims
    token[...] = jnp.zeros_like(token)
    sp[...] = jnp.zeros_like(sp)
    place = lax.broadcasted_iota(jnp.int32, (basis, basis), 0)
    other = lax.broadcasted_iota(jnp.int32, (basis, basis), 1)
    unit = jnp.where(place == other, 1.0, 0.0).astype(F32)
    for d in range(dims):
        sp[d * pad:d * pad + basis, 0:basis] = dot_exact(unit, stiff[d], (((1,), (1,)), ((), ())))
    rotate(rot, stacked_left(sp[...]), integral, quants, width)

    def emit(p, at, value):
        out[p, :, lanes(at)] = state[p, :, lanes(at)] + value[0:basis]

    jacobian_step(lambda p, q, d, cut: jac[p, q, d:d + 1, cut], rot, emit, quants, dims, width)


def flux_kernel(
    first, faces, base, traces, own, solvers, lift, neighbours, xb, zb, xa, za,
    out, token, tiles, flux, lp,
):
    token[...] = jnp.zeros_like(token)
    quants, basis, width = base.shape
    face_basis = lift.shape[0]
    skip = xa.shape[0] - sent_rows(quants, face_basis)
    for axis, base_tile, gots in (("gx", 0, (xa, xb)), ("gz", 2, (za, zb))):
        for got, side in zip(gots, sides(axis)):
            for q in range(quants):
                tiles[q, base_tile + side, 0:8, :] = got[skip + q * 8:skip + q * 8 + 8, :]
                at = skip + quants * 8 + q * 2
                tiles[q, base_tile + side, 8:face_basis, :] = got[at:at + 2, :]
                tiles[q, base_tile + side, face_basis:, :] = jnp.zeros((16 - face_basis, LANES), F32)
    for q in range(quants):
        tiles[q, 4] = -own[q] if q < 3 else own[q]
    lp[...] = jnp.zeros_like(lp)
    for f in range(faces):
        for j in range(face_basis):
            lp[f * 16 + j:f * 16 + j + 1, 0:basis] = lift[j, first + f:first + f + 1, :]
    unit = lax.broadcasted_iota(jnp.int32, (lp.shape[1], lp.shape[1]), 0) == lax.broadcasted_iota(
        jnp.int32, (lp.shape[1], lp.shape[1]), 1
    )
    lifted = stacked_left(dot_exact(jnp.where(unit, 1.0, 0.0).astype(F32), lp[...], (((1,), (1,)), ((), ()))))
    local = traces.shape[2] // LANES
    halves_in = width // LANES

    def one(h, carry):
        at = h * LANES
        for f in range(faces):
            index = jnp.broadcast_to(neighbours[first + f:first + f + 1, lanes(at)], (16, LANES))
            acc = [None] * quants
            for q in range(quants):
                pool = [traces[q, :, s * LANES:(s + 1) * LANES] for s in range(local)]
                pool += [tiles[q, s] for s in range(5)]
                mine = traces[q, :, lanes((first + f) * width + at)]
                jump = take_slots(pool, index) - mine
                for p in range(quants):
                    term = solvers[p, q, first + f:first + f + 1, lanes(at)] * jump
                    acc[p] = term if acc[p] is None else acc[p] + term
            for p in range(quants):
                flux[f * 16:(f + 1) * 16, lanes(p * width + at)] = acc[p]
        return carry

    lax.fori_loop(0, halves_in, one, 0)
    for p in range(quants):
        cut = slice(p * width, (p + 1) * width)
        out[p] = base[p] + dot3(lifted, flux[:, cut])[0:basis]


def replies_kernel(base, solvers, lift, neighbours, smap, answer, rxb, rxa, out, slot_spread):
    quants, basis, width = base.shape
    face_basis, faces = lift.shape[:2]
    slots = smap.shape[2]
    low, high = by_side((rxa[0:HEAD, :], rxb[0:HEAD, :]), "gx")
    lane = lax.broadcasted_iota(jnp.int32, (1, LANES), 1)
    replies = jnp.zeros((1, LANES), F32)
    for r, row in enumerate((low[1:2], low[0:1], answer[...], high[0:1], high[2:3])):
        replies = jnp.where(lane // slots == r, row, replies)
    replies = jnp.broadcast_to(-2.0 * replies * flat_slots(smap, slot_spread)[2:3], (8, LANES))
    begin = faces * width + 4 * LANES
    square = lax.broadcasted_iota(jnp.int32, (basis, basis), 0) == lax.broadcasted_iota(
        jnp.int32, (basis, basis), 1
    )
    columns = []
    for f in range(faces):
        column = lift[0, f:f + 1, :]
        for j in range(1, face_basis):
            column = column + lift[j, f:f + 1, :]
        columns.append(jnp.sum(jnp.where(square, column, 0.0), axis=1, keepdims=True))
    for h in range(width // LANES):
        cut = slice(h * LANES, (h + 1) * LANES)
        spread = []
        for f in range(faces):
            index = jnp.broadcast_to(neighbours[f:f + 1, cut], (8, LANES))
            found = jnp.take_along_axis(replies, index % LANES, axis=1, mode="promise_in_bounds")
            spread.append(columns[f] * jnp.where(index >= begin, found, 0.0)[0:1])
        for p in range(quants):
            stress = solvers[p, 0, :, cut] + solvers[p, 1, :, cut] + solvers[p, 2, :, cut]
            total = base[p, :, cut]
            for f in range(faces):
                total = total + stress[f:f + 1] * spread[f]
            out[p, :, cut] = total


def sent_rows(quants, face_basis):
    return -(-quants * face_basis // 8) * 8


def shards(
    solid_state, jacobians, flux_solvers, stiffness, trace_matrix, lift_matrix,
    neighbours, send_faces, surface_map, surface_normals, air_state, wind_field, air_medium,
):
    quants, basis, width = solid_state.shape
    faces, face_basis = trace_matrix.shape[0], trace_matrix.shape[1]
    dims = stiffness.shape[0]
    nx, nz, ny = air_state.shape[1:]
    n_gx, n_gz = lax.axis_size("gx"), lax.axis_size("gz")
    jacobians = jnp.transpose(jacobians, (1, 2, 0, 3))
    flux_solvers = jnp.transpose(flux_solvers, (1, 2, 0, 3))
    trace_matrix = jnp.transpose(trace_matrix, (1, 0, 2))
    lift_matrix = jnp.transpose(lift_matrix, (2, 0, 1))
    surface_map = jnp.transpose(surface_map, (1, 0, 2))
    surface_normals = jnp.transpose(surface_normals, (1, 0, 2))
    pad = -(-basis // 8) * 8
    rim_z = (7, nx, RADIUS, ny)
    rim_x = (7, RADIUS, nz, ny)
    ext = (4, nx + 2 * RADIUS, nz + 2 * ZRIM, ny)
    wide = ext[1:]
    block = (1, nx, nz, ny)
    tile = (8, LANES)

    rims = exchange(
        *call(
            raw_rims_kernel, "raw_rims", [rim_x, rim_z, rim_x, rim_z], [air_state, wind_field],
        )
    )

    sent = (sent_rows(quants, face_basis), LANES)
    integral, traces, state = call(
        predict_kernel, "predict",
        [(K, quants * width), (quants, 16, faces * width), solid_state.shape],
        [solid_state, jacobians, stiffness, trace_matrix],
        [(K, quants * width), (dims * pad, quants * width), (dims * pad, LANES), (faces * 16, LANES)],
        flops=40_000_000,
    )
    own, rows = call(
        own_list_kernel, "own_list", [(quants, 16, LANES), (n_gx * n_gz, LANES)],
        [traces, surface_map, surface_normals], [(surface_map.shape[0], 8, LANES)], after=[rims[3]],
    )
    lists = lax.all_to_all(rows, ("gx", "gz"), split_axis=0, concat_axis=0, tiled=True)
    sent_four = call(
        outgoing_kernel, "outgoing", [sent, sent, sent, sent], [traces, send_faces],
        [(4, quants, 16, LANES)], flops=10_000_000, after=[rows],
    )
    pressure_x = (HEAD + RADIUS * nz, ny)
    pressure_z = (HEAD + nx * ZRIM, ny)
    both_x = (pressure_x[0] + sent[0], LANES)
    both_z = (pressure_z[0] + sent[0], LANES)
    raw, xb, zb, xa, za = call(
        raw_pressure_kernel, "raw_pressure", [block, both_x, both_z, both_x, both_z],
        [air_state, wind_field, air_medium, *rims, *sent_four], [ext],
    )
    both = exchange(xb, zb, xa, za)
    (moved,) = call(
        advection_kernel, "advection", [(3, nx, nz, ny)],
        [air_state, wind_field, *rims], [ext], flops=10_000_000, after=[xa],
    )
    volume, token = call(
        volume_kernel, "volume", [solid_state.shape, tile], [state, integral, jacobians, stiffness],
        [(dims * pad, quants * width), (dims * pad, LANES)], flops=10_000_000, after=[xa],
    )

    rim_x = (HEAD + 4 * RADIUS * nz, ny)
    rim_z = (4, nx, RADIUS, ny)
    air, xb, zb, xa, za, answer = call(
        functools.partial(injected_kernel, n_gx, n_gz), "injected",
        [air_state.shape, rim_x, rim_z, rim_x, rim_z, (1, LANES)],
        [air_state, wind_field, air_medium, raw, moved, *rims, *both, lists, surface_map],
        [(3 * nx, 3 * nz, ny), wide, (3,) + wide], after=[token],
    )
    half = faces // 2
    solid = volume
    for substep in range(1, SUBSTEPS):
        rims = exchange(xb, zb, xa, za)
        solid, token = call(
            functools.partial(flux_kernel, (substep - 1) * half, half), "flux", [solid_state.shape, tile],
            [solid, traces, own, flux_solvers, lift_matrix, neighbours, *both],
            [(quants, 5, 16, LANES), (half * 16, quants * width), (LANES, pad)], flops=20_000_000,
            after=[xa],
        )
        pressure, xb, zb, xa, za = call(
            pressure_kernel, "pressure", [block, pressure_x, pressure_z, pressure_x, pressure_z],
            [air, wind_field, air_medium, *rims, answer], [ext], after=[token],
        )
        rises = exchange(xb, zb, xa, za)
        if substep == 1:
            replies = [answer, rises[0], rises[2]]
        (moved,) = call(
            advection_kernel, "advection", [(3, nx, nz, ny)],
            [air, wind_field, *rims], [ext], flops=10_000_000, after=[xa],
        )
        last = substep == SUBSTEPS - 1
        if last:
            (solid,) = call(
                replies_kernel, "replies", [solid_state.shape],
                [solid, flux_solvers, lift_matrix, neighbours, surface_map, *replies],
                [(surface_map.shape[0], 8, LANES)], after=[moved],
            )
        outs = [air_state.shape] + ([] if last else [rim_x, rim_z, rim_x, rim_z])
        done = call(
            velocity_kernel, "velocity", outs, [air, pressure, air_medium, moved, *rises], [wide]
        )
        air = done[0]
        if not last:
            xb, zb, xa, za = done[1:]
    return (solid, air)


def solution(mesh):
    in_specs = (
        P(None, None, ("gx", "gz")),
        P(None, None, None, ("gx", "gz")),
        P(None, None, None, ("gx", "gz")),
        P(),
        P(),
        P(),
        P(None, ("gx", "gz")),
        P(None, ("gx", "gz")),
        P(None, None, ("gx", "gz")),
        P(None, None, ("gx", "gz")),
        P(None, "gx", "gz", None),
        P(None, "gx", "gz", None),
        P(None, "gx", "gz", None),
    )
    out_specs = (P(None, None, ("gx", "gz")), P(None, "gx", "gz", None))
    return jax.shard_map(shards, mesh=mesh, in_specs=in_specs, out_specs=out_specs, check_vma=False)
```

profile of v0, /device:TPU:0, one launch (start us, length us, event | category | flops | bytes accessed | tf_op | source)
XLA Modules:
  0.0 83.8 jit_solution(2249856723960928470)
XLA Ops:
  0.6 0.9 %copy-done = f32[3,8,16,128]{3,2,1,0:T(8,128)S(1)} copy-done((f32[3,8,16,128]{3,2,1,0:T(8,128)S(1)}, f32[3,8,16,128]{3,2,1,0:T(8,128)}, u32[]{:S(2)}) %copy-start) | copy-done | bytes 196632
  1.6 0.9 %copy-done.3 = f32[4,8,16,128]{3,2,1,0:T(8,128)S(1)} copy-done((f32[4,8,16,128]{3,2,1,0:T(8,128)S(1)}, f32[4,8,16,128]{3,2,1,0:T(8,128)}, u32[]{:S(2)}) %copy-start.3) | copy-done | bytes 262168
  2.6 0.8 collective-permute-start
  3.4 5.8 %collective-permute-start.2 = (f32[7,4,16,128]{3,2,1,0:T(8,128)S(1)}, f32[7,4,16,128]{3,2,1,0:T(8,128)S(1)}, u32[]{:S(2)}, u32[]{:S(2)}) collective-permute-start(f32[7,4,16,128]{3,2,1,0:T(8,128)S(1)} %get-tuple-element.51), channel_id=1, source_target_pairs={{0,4},{4,0},{8,12},{12,8},{16,20},{20,16},{24,28},{28,24},{1,5},{5... | collective-permute-start | bytes 688136 | tf_op jit(solution)/shard_map/ppermute | solution.py:50
  9.9 0.9 %copy-done.7 = f32[9,20,256]{2,1,0:T(8,128)S(1)} copy-done((f32[9,20,256]{2,1,0:T(8,128)S(1)}, f32[9,20,256]{2,1,0:T(8,128)}, u32[]{:S(2)}) %copy-start.7) | copy-done | bytes 184344
  10.8 2.5 %predict.1 = (f32[32,2304]{1,0:T(8,128)S(1)}, f32[9,16,1024]{2,1,0:T(8,128)S(1)}, f32[9,20,256]{2,1,0:T(8,128)S(1)}) custom-call(f32[9,20,256]{2,1,0:T(8,128)S(1)} %copy-done.7, f32[9,9,3,256]{3,2,1,0:T(4,128)S(1)} %bitcast.13, f32[3,20,20]{2,1,0:T(8,128)S(1)} %copy-done.9, f32[10,4,20]{2,1,0:T(4,128)S(1)} %bitcast.22), custom_call_target="tpu_custom_call" | custom-call | flops 40000000 | bytes 1510208 | tf_op jit(solution)/shard_map/predict/pallas_call | solution.py:31
  13.4 1.6 %own_list.1 = (f32[9,16,128]{2,1,0:T(8,128)S(1)}, f32[32,128]{1,0:T(8,128)}) custom-call(f32[9,16,1024]{2,1,0:T(8,128)S(1)} %get-tuple-element.53.refs_0_.refs_1_, s32[5,3,8]{2,1,0:T(4,128)S(1)} %bitcast.18, f32[5,3,8]{2,1,0:T(4,128)S(1)} %bitcast.23, f32[7,8,4,128]{3,2,1,0:T(4,128)S(1)} %collective-permute-done.3.refs_3_.refs_6_.refs_5_.refs_8_), custom_call_target="tpu_custom_call" | custom-call | flops 1000000 | bytes 680896 | tf_op jit(solution)/shard_map/own_list/pallas_call | solution.py:31
  15.0 1.5 %outgoing.1 = (f32[96,128]{1,0:T(8,128)S(1)}, f32[96,128]{1,0:T(8,128)S(1)}, f32[96,128]{1,0:T(8,128)S(1)}, f32[96,128]{1,0:T(8,128)S(1)}) custom-call(f32[9,16,1024]{2,1,0:T(8,128)S(1)} %get-tuple-element.53.refs_0_.refs_1_, s32[4,128]{1,0:T(4,128)S(1)} %copy-done.16, f32[32,128]{1,0:T(8,128)} %get-tuple-element.54.refs_2_), custom_call_target="tpu_custom_call" | custom-call | flops 10000000 | bytes 788480 | tf_op jit(solution)/shard_map/outgoing/pallas_call | solution.py:31
  16.4 1.8 %collective-permute-done.2.refs_5_.refs_4_.refs_7_ = f32[7,4,16,128]{3,2,1,0:T(8,128)S(1)} collective-permute-done((f32[7,4,16,128]{3,2,1,0:T(8,128)S(1)}, f32[7,4,16,128]{3,2,1,0:T(8,128)S(1)}, u32[]{:S(2)}, u32[]{:S(2)}) %collective-permute-start.2) | collective-permute-done | bytes 229408 | tf_op jit(solution)/shard_map/ppermute | solution.py:50
  18.3 1.1 %raw_pressure.1 = (f32[1,8,16,128]{3,2,1,0:T(8,128)S(1)}, f32[168,128]{1,0:T(8,128)}, f32[168,128]{1,0:T(8,128)}, f32[168,128]{1,0:T(8,128)S(1)}, f32[168,128]{1,0:T(8,128)}) custom-call(f32[4,8,16,128]{3,2,1,0:T(8,128)S(1)} %copy-done.4, f32[3,8,16,128]{3,2,1,0:T(8,128)S(1)} %copy-done.1, f32[2,8,16,128]{3,2,1,0:T(8,128)S(1)} %copy-done.2, ...), custom_call_target="tpu_custom_call" | custom-call | flops 1000000 | bytes 1884160 | tf_op jit(solution)/shard_map/raw_pressure/pallas_call | solution.py:31
  20.6 0.7 collective-permute-start.5
  21.3 3.0 %collective-permute-start.7 = (f32[168,128]{1,0:T(8,128)}, f32[168,128]{1,0:T(8,128)S(1)}, u32[]{:S(2)}, u32[]{:S(2)}) collective-permute-start(f32[168,128]{1,0:T(8,128)} %get-tuple-element.64), channel_id=1, source_target_pairs={{0,1},{1,0},{2,3},{3,2},{4,5},{5,4},{6,7},{7,6},{8,9},{9,8},{10,11... | collective-permute-start | bytes 258056 | tf_op jit(solution)/shard_map/ppermute | solution.py:50
  24.3 5.1 %collective-permute-start.6 = (f32[168,128]{1,0:T(8,128)S(1)}, f32[168,128]{1,0:T(8,128)S(1)}, u32[]{:S(2)}, u32[]{:S(2)}) collective-permute-start(f32[168,128]{1,0:T(8,128)S(1)} %get-tuple-element.59.refs_4_.refs_6_), channel_id=1, source_target_pairs={{0,4},{4,0},{8,12},{12,8},{16,20},{20,16},{24,28},{28,24},{1,5},{5... | collective-permute-start | bytes 258056 | tf_op jit(solution)/shard_map/ppermute | solution.py:50
  29.5 3.8 %all-to-all-start = ((f32[32,1,128]{2,1,0:T(1,128)}), f32[32,1,128]{2,1,0:T(1,128)S(1)}, u32[]{:S(2)}, u32[]{:S(2)}) async-start(f32[32,1,128]{2,1,0:T(1,128)} %bitcast.7), calls=%async_computation | async-start | bytes 32768 | tf_op jit(solution)/shard_map/all_to_all | solution.py:632
  33.3 1.1 %volume.1 = (f32[9,20,256]{2,1,0:T(8,128)S(1)}, f32[8,128]{1,0:T(8,128)S(1)}) custom-call(f32[9,20,256]{2,1,0:T(8,128)S(1)} %get-tuple-element.47.refs_0_, f32[32,2304]{1,0:T(8,128)S(1)} %get-tuple-element.48.refs_1_, f32[9,9,3,256]{3,2,1,0:T(4,128)S(1)} %bitcast.14, f32[3,20,20]{2,1,0:T(8,128)S(1)} %copy-done.9, ...), custom_call_target="tpu_custom_call" | custom-call | flops 10000000 | bytes 921280 | tf_op jit(solution)/shard_map/volume/pallas_call | solution.py:31
  34.9 5.5 %all-to-all-done = f32[32,1,128]{2,1,0:T(1,128)S(1)} async-done(((f32[32,1,128]{2,1,0:T(1,128)}), f32[32,1,128]{2,1,0:T(1,128)S(1)}, u32[]{:S(2)}, u32[]{:S(2)}) %all-to-all-start) | async-done | bytes 16416 | tf_op jit(solution)/shard_map/all_to_all | solution.py:632
  40.5 1.1 %injected.1 = (f32[4,8,16,128]{3,2,1,0:T(8,128)S(1)}, f32[264,128]{1,0:T(8,128)S(1)}, f32[4,8,4,128]{3,2,1,0:T(4,128)S(1)}, f32[264,128]{1,0:T(8,128)S(1)}, f32[...) custom-call(f32[4,8,16,128]{3,2,1,0:T(8,128)S(1)} %copy-done.4, f32[3,8,16,128]{3,2,1,0:T(8,128)S(1)} %copy-done.1, ...), custom_call_target="tpu_custom_call" | custom-call | flops 1000000 | bytes 2565088 | tf_op jit(solution)/shard_map/injected/pallas_call | solution.py:31
  42.2 3.3 %collective-permute-start.10 = (f32[264,128]{1,0:T(8,128)S(1)}, f32[264,128]{1,0:T(8,128)S(1)}, u32[]{:S(2)}, u32[]{:S(2)}) collective-permute-start(f32[264,128]{1,0:T(8,128)S(1)} %get-tuple-element.67.refs_10_), channel_id=1, source_target_pairs={{0,4},{4,0},{8,12},{12,8},{16,20},{20,16},{24,28},{28,24},{1,5},{5... | collective-permute-start | bytes 405512 | tf_op jit(solution)/shard_map/ppermute | solution.py:50
  46.3 2.0 %collective-permute-start.11 = (f32[4,8,4,128]{3,2,1,0:T(4,128)S(1)}, f32[4,8,4,128]{3,2,1,0:T(4,128)S(1)}, u32[]{:S(2)}, u32[]{:S(2)}) collective-permute-start(f32[4,8,4,128]{3,2,1,0:T(4,128)S(1)} %get-tuple-element.72), channel_id=1, source_target_pairs={{0,1},{1,0},{2,3},{3,2},{4,5},{5,4},{6,7},{7,6},{8,9},{9,8},{10,11... | collective-permute-start | bytes 196616 | tf_op jit(solution)/shard_map/ppermute | solution.py:50
  48.2 1.8 %flux.2 = (f32[9,20,256]{2,1,0:T(8,128)S(1)}, f32[8,128]{1,0:T(8,128)S(1)}) custom-call(f32[9,20,256]{2,1,0:T(8,128)S(1)} %get-tuple-element.60.refs_0_, f32[9,16,1024]{2,1,0:T(8,128)S(1)} %get-tuple-element.53.refs_0_.refs_1_, f32[9,16,128]{2,1,0:T(8,128)S(1)} %get-tuple-element.61.refs_2_, f32[9,9,4,256]{3,2,1,0:T(4,128)S(1)} %bitcast.10, ...), custom_call_target="tpu_custom_call" | custom-call | flops 20000000 | bytes 1719424 | tf_op jit(solution)/shard_map/flux/pallas_call | solution.py:31
  51.0 0.7 collective-permute-start.12
  52.3 2.5 %collective-permute-start.15 = (f32[72,128]{1,0:T(8,128)S(1)}, f32[72,128]{1,0:T(8,128)S(1)}, u32[]{:S(2)}, u32[]{:S(2)}) collective-permute-start(f32[72,128]{1,0:T(8,128)S(1)} %get-tuple-element.79), channel_id=1, source_target_pairs={{0,1},{1,0},{2,3},{3,2},{4,5},{5,4},{6,7},{7,6},{8,9},{9,8},{10,11... | collective-permute-start | bytes 110600 | tf_op jit(solution)/shard_map/ppermute | solution.py:50
  54.8 4.7 %collective-permute-start.14 = (f32[72,128]{1,0:T(8,128)S(1)}, f32[72,128]{1,0:T(8,128)S(1)}, u32[]{:S(2)}, u32[]{:S(2)}) collective-permute-start(f32[72,128]{1,0:T(8,128)S(1)} %get-tuple-element.76.refs_6_), channel_id=1, source_target_pairs={{0,4},{4,0},{8,12},{12,8},{16,20},{20,16},{24,28},{28,24},{1,5},{5... | collective-permute-start | bytes 110600 | tf_op jit(solution)/shard_map/ppermute | solution.py:50
  60.1 1.4 %collective-permute-done.14.refs_6_.refs_7_ = f32[72,128]{1,0:T(8,128)S(1)} collective-permute-done((f32[72,128]{1,0:T(8,128)S(1)}, f32[72,128]{1,0:T(8,128)S(1)}, u32[]{:S(2)}, u32[]{:S(2)}) %collective-permute-start.14) | collective-permute-done | bytes 36896 | tf_op jit(solution)/shard_map/ppermute | solution.py:50
  61.8 0.7 collective-permute-start.16
  62.5 4.7 %collective-permute-start.18 = (f32[264,128]{1,0:T(8,128)S(1)}, f32[264,128]{1,0:T(8,128)S(1)}, u32[]{:S(2)}, u32[]{:S(2)}) collective-permute-start(f32[264,128]{1,0:T(8,128)S(1)} %get-tuple-element.80.refs_10_), channel_id=1, source_target_pairs={{0,4},{4,0},{8,12},{12,8},{16,20},{20,16},{24,28},{28,24},{1,5},{5... | collective-permute-start | bytes 405512 | tf_op jit(solution)/shard_map/ppermute | solution.py:50
  67.9 2.2 %collective-permute-start.19 = (f32[4,8,4,128]{3,2,1,0:T(4,128)S(1)}, f32[4,8,4,128]{3,2,1,0:T(4,128)S(1)}, u32[]{:S(2)}, u32[]{:S(2)}) collective-permute-start(f32[4,8,4,128]{3,2,1,0:T(4,128)S(1)} %get-tuple-element.85), channel_id=1, source_target_pairs={{0,1},{1,0},{2,3},{3,2},{4,5},{5,4},{6,7},{7,6},{8,9},{9,8},{10,11... | collective-permute-start | bytes 196616 | tf_op jit(solution)/shard_map/ppermute | solution.py:50
  70.1 1.8 %flux.3 = (f32[9,20,256]{2,1,0:T(8,128)S(1)}, f32[8,128]{1,0:T(8,128)S(1)}) custom-call(f32[9,20,256]{2,1,0:T(8,128)S(1)} %get-tuple-element.68.refs_0_, f32[9,16,1024]{2,1,0:T(8,128)S(1)} %get-tuple-element.53.refs_0_.refs_1_, f32[9,16,128]{2,1,0:T(8,128)S(1)} %get-tuple-element.61.refs_2_, f32[9,9,4,256]{3,2,1,0:T(4,128)S(1)} %bitcast.11, ...), custom_call_target="tpu_custom_call" | custom-call | flops 20000000 | bytes 1719424 | tf_op jit(solution)/shard_map/flux/pallas_call | solution.py:31
  73.7 3.1 %collective-permute-start.23 = (f32[72,128]{1,0:T(8,128)S(1)}, f32[72,128]{1,0:T(8,128)S(1)}, u32[]{:S(2)}, u32[]{:S(2)}) collective-permute-start(f32[72,128]{1,0:T(8,128)S(1)} %get-tuple-element.91), channel_id=1, source_target_pairs={{0,1},{1,0},{2,3},{3,2},{4,5},{5,4},{6,7},{7,6},{8,9},{9,8},{10,11... | collective-permute-start | bytes 110600 | tf_op jit(solution)/shard_map/ppermute | solution.py:50
  76.7 4.1 %collective-permute-start.22 = (f32[72,128]{1,0:T(8,128)S(1)}, f32[72,128]{1,0:T(8,128)S(1)}, u32[]{:S(2)}, u32[]{:S(2)}) collective-permute-start(f32[72,128]{1,0:T(8,128)S(1)} %get-tuple-element.87.refs_6_), channel_id=1, source_target_pairs={{0,4},{4,0},{8,12},{12,8},{16,20},{20,16},{24,28},{28,24},{1,5},{5... | collective-permute-start | bytes 110600 | tf_op jit(solution)/shard_map/ppermute | solution.py:50
  81.4 0.9 %replies.1 = f32[9,20,256]{2,1,0:T(8,128)} custom-call(f32[9,20,256]{2,1,0:T(8,128)S(1)} %get-tuple-element.81.refs_0_, f32[9,9,4,256]{3,2,1,0:T(4,128)S(1)} %bitcast.12, f32[10,4,20]{2,1,0:T(4,128)S(1)} %bitcast.17, s32[4,256]{1,0:T(4,128)S(1)} %copy-done.13, s32[5,3,8]{2,1,0:T(4,128)S(1)} %bitcast.20, f32[1,128]{1,0:T(1,128)S(1)} %get-tuple-element.73.refs_7_.refs_5_, ...), custom_call_target="tpu_custom_call" | custom-call | flops 1000000 | bytes 782432 | tf_op jit(solution)/shard_map/replies/pallas_call | solution.py:31
  82.8 1.0 %velocity.3 = f32[4,8,16,128]{3,2,1,0:T(8,128)} custom-call(f32[4,8,16,128]{3,2,1,0:T(8,128)S(1)} %get-tuple-element.82.refs_0_, f32[1,8,16,128]{3,2,1,0:T(8,128)S(1)} %get-tuple-element.88.refs_1_, f32[2,8,16,128]{3,2,1,0:T(8,128)S(1)} %copy-done.2, f32[3,8,16,128]{3,2,1,0:T(8,128)S(1)} %advection.5.refs_8_.refs_3_, ...), custom_call_target="tpu_custom_call" | custom-call | flops 1000000 | bytes 1064960 | tf_op jit(solution)/shard_map/velocity/pallas_call | solution.py:31
  (69 shorter events, 9.7 us)
Async XLA Ops:
  2.5 7.3 %copy-start.6 = (f32[3,9,9,256]{3,0,2,1:T(4,128)S(1)}, f32[3,9,9,256]{3,0,2,1:T(4,128)}, u32[]{:S(2)}) copy-start(f32[3,9,9,256]{3,0,2,1:T(4,128)} %param.14) | copy-start | bytes 746500
  2.5 7.4 %copy-start.9 = (f32[3,20,20]{2,1,0:T(8,128)S(1)}, f32[3,20,20]{2,1,0:T(8,128)}, u32[]{:S(2)}) copy-start(f32[3,20,20]{2,1,0:T(8,128)} %refs_3_.2) | copy-start | bytes 14404
  2.5 7.4 %copy-start.14 = (f32[4,10,20]{2,0,1:T(4,128)S(1)}, f32[4,10,20]{2,0,1:T(4,128)}, u32[]{:S(2)}) copy-start(f32[4,10,20]{2,0,1:T(4,128)} %param.17) | copy-start | bytes 9604
  2.6 13.8 %collective-permute-start = (f32[7,4,16,128]{3,2,1,0:T(8,128)S(1)}, f32[7,4,16,128]{3,2,1,0:T(8,128)S(1)}, u32[]{:S(2)}, u32[]{:S(2)}) collective-permute-start(f32[7,4,16,128]{3,2,1,0:T(8,128)S(1)} %get-tuple-element.49), channel_id=1, source_target_pairs={{4,8},{8,4},{12,16},{16,12},{20,24},{24,20},{5,9},{9,5},{13,17},{1... | collective-permute-start | bytes 688136 | tf_op jit(solution)/shard_map/ppermute | solution.py:50
  3.4 14.9 %collective-permute-start.2 = (f32[7,4,16,128]{3,2,1,0:T(8,128)S(1)}, f32[7,4,16,128]{3,2,1,0:T(8,128)S(1)}, u32[]{:S(2)}, u32[]{:S(2)}) collective-permute-start(f32[7,4,16,128]{3,2,1,0:T(8,128)S(1)} %get-tuple-element.51), channel_id=1, source_target_pairs={{0,4},{4,0},{8,12},{12,8},{16,20},{20,16},{24,28},{28,24},{1,5},{5... | collective-permute-start | bytes 688136 | tf_op jit(solution)/shard_map/ppermute | solution.py:50
  9.2 4.2 %collective-permute-start.3 = (f32[7,8,4,128]{3,2,1,0:T(4,128)S(1)}, f32[7,8,4,128]{3,2,1,0:T(4,128)S(1)}, u32[]{:S(2)}, u32[]{:S(2)}) collective-permute-start(f32[7,8,4,128]{3,2,1,0:T(4,128)S(1)} %get-tuple-element.52), channel_id=1, source_target_pairs={{0,1},{1,0},{2,3},{3,2},{4,5},{5,4},{6,7},{7,6},{8,9},{9,8},{10,11... | collective-permute-start | bytes 344072 | tf_op jit(solution)/shard_map/ppermute | solution.py:50
  9.2 7.2 %collective-permute-start.1 = (f32[7,8,4,128]{3,2,1,0:T(4,128)S(1)}, f32[7,8,4,128]{3,2,1,0:T(4,128)S(1)}, u32[]{:S(2)}, u32[]{:S(2)}) collective-permute-start(f32[7,8,4,128]{3,2,1,0:T(4,128)S(1)} %get-tuple-element.50), channel_id=1, source_target_pairs={{1,2},{2,1},{5,6},{6,5},{9,10},{10,9},{13,14},{14,13},{17,18},{18,... | collective-permute-start | bytes 344072 | tf_op jit(solution)/shard_map/ppermute | solution.py:50
  15.0 3.3 %copy-start.4 = (f32[4,8,16,128]{3,2,1,0:T(8,128)S(1)}, f32[4,8,16,128]{3,2,1,0:T(8,128)}, u32[]{:S(2)}) copy-start(f32[4,8,16,128]{3,2,1,0:T(8,128)} %refs_0_.9) | copy-start | bytes 786436
  20.0 20.5 %collective-permute-start.4 = (f32[168,128]{1,0:T(8,128)}, f32[168,128]{1,0:T(8,128)S(1)}, u32[]{:S(2)}, u32[]{:S(2)}) collective-permute-start(f32[168,128]{1,0:T(8,128)} %get-tuple-element.62), channel_id=1, source_target_pairs={{4,8},{8,4},{12,16},{16,12},{20,24},{24,20},{5,9},{9,5},{13,17},{1... | collective-permute-start | bytes 258056 | tf_op jit(solution)/shard_map/ppermute | solution.py:50
  20.6 19.8 %collective-permute-start.5 = (f32[168,128]{1,0:T(8,128)}, f32[168,128]{1,0:T(8,128)S(1)}, u32[]{:S(2)}, u32[]{:S(2)}) collective-permute-start(f32[168,128]{1,0:T(8,128)} %get-tuple-element.63), channel_id=1, source_target_pairs={{1,2},{2,1},{5,6},{6,5},{9,10},{10,9},{13,14},{14,13},{17,18},{18,... | collective-permute-start | bytes 258056 | tf_op jit(solution)/shard_map/ppermute | solution.py:50
  21.3 19.1 %collective-permute-start.7 = (f32[168,128]{1,0:T(8,128)}, f32[168,128]{1,0:T(8,128)S(1)}, u32[]{:S(2)}, u32[]{:S(2)}) collective-permute-start(f32[168,128]{1,0:T(8,128)} %get-tuple-element.64), channel_id=1, source_target_pairs={{0,1},{1,0},{2,3},{3,2},{4,5},{5,4},{6,7},{7,6},{8,9},{9,8},{10,11... | collective-permute-start | bytes 258056 | tf_op jit(solution)/shard_map/ppermute | solution.py:50
  24.3 16.1 %collective-permute-start.6 = (f32[168,128]{1,0:T(8,128)S(1)}, f32[168,128]{1,0:T(8,128)S(1)}, u32[]{:S(2)}, u32[]{:S(2)}) collective-permute-start(f32[168,128]{1,0:T(8,128)S(1)} %get-tuple-element.59.refs_4_.refs_6_), channel_id=1, source_target_pairs={{0,4},{4,0},{8,12},{12,8},{16,20},{20,16},{24,28},{28,24},{1,5},{5... | collective-permute-start | bytes 258056 | tf_op jit(solution)/shard_map/ppermute | solution.py:50
  29.5 10.9 %all-to-all-start = ((f32[32,1,128]{2,1,0:T(1,128)}), f32[32,1,128]{2,1,0:T(1,128)S(1)}, u32[]{:S(2)}, u32[]{:S(2)}) async-start(f32[32,1,128]{2,1,0:T(1,128)} %bitcast.7), calls=%async_computation | async-start | bytes 32768 | tf_op jit(solution)/shard_map/all_to_all | solution.py:632
  34.4 6.1 %copy-start.12 = (f32[1,8,16,128]{3,2,1,0:T(8,128)S(1)}, f32[1,8,16,128]{3,2,1,0:T(8,128)}, u32[]{:S(2)}) copy-start(f32[1,8,16,128]{3,2,1,0:T(8,128)} %copy-done.11) | copy-start | bytes 196612
  40.5 7.7 %copy-start.5 = (f32[4,9,9,256]{3,0,2,1:T(4,128)S(1)}, f32[4,9,9,256]{3,0,2,1:T(4,128)}, u32[]{:S(2)}) copy-start(f32[4,9,9,256]{3,0,2,1:T(4,128)} %param.15) | copy-start | bytes 995332
  40.5 7.7 %copy-start.8 = (f32[4,20,10]{1,0,2:T(4,128)S(1)}, f32[4,20,10]{1,0,2:T(4,128)}, u32[]{:S(2)}) copy-start(f32[4,20,10]{1,0,2:T(4,128)} %param.18) | copy-start | bytes 9604
  41.6 8.5 %collective-permute-start.8 = (f32[264,128]{1,0:T(8,128)S(1)}, f32[264,128]{1,0:T(8,128)S(1)}, u32[]{:S(2)}, u32[]{:S(2)}) collective-permute-start(f32[264,128]{1,0:T(8,128)S(1)} %get-tuple-element.70), channel_id=1, source_target_pairs={{4,8},{8,4},{12,16},{16,12},{20,24},{24,20},{5,9},{9,5},{13,17},{1... | collective-permute-start | bytes 405512 | tf_op jit(solution)/shard_map/ppermute | solution.py:50
  42.2 8.4 %collective-permute-start.10 = (f32[264,128]{1,0:T(8,128)S(1)}, f32[264,128]{1,0:T(8,128)S(1)}, u32[]{:S(2)}, u32[]{:S(2)}) collective-permute-start(f32[264,128]{1,0:T(8,128)S(1)} %get-tuple-element.67.refs_10_), channel_id=1, source_target_pairs={{0,4},{4,0},{8,12},{12,8},{16,20},{20,16},{24,28},{28,24},{1,5},{5... | collective-permute-start | bytes 405512 | tf_op jit(solution)/shard_map/ppermute | solution.py:50
  45.6 4.4 %collective-permute-start.9 = (f32[4,8,4,128]{3,2,1,0:T(4,128)S(1)}, f32[4,8,4,128]{3,2,1,0:T(4,128)S(1)}, u32[]{:S(2)}, u32[]{:S(2)}) collective-permute-start(f32[4,8,4,128]{3,2,1,0:T(4,128)S(1)} %get-tuple-element.71), channel_id=1, source_target_pairs={{1,2},{2,1},{5,6},{6,5},{9,10},{10,9},{13,14},{14,13},{17,18},{18,... | collective-permute-start | bytes 196616 | tf_op jit(solution)/shard_map/ppermute | solution.py:50
  46.3 3.8 %collective-permute-start.11 = (f32[4,8,4,128]{3,2,1,0:T(4,128)S(1)}, f32[4,8,4,128]{3,2,1,0:T(4,128)S(1)}, u32[]{:S(2)}, u32[]{:S(2)}) collective-permute-start(f32[4,8,4,128]{3,2,1,0:T(4,128)S(1)} %get-tuple-element.72), channel_id=1, source_target_pairs={{0,1},{1,0},{2,3},{3,2},{4,5},{5,4},{6,7},{7,6},{8,9},{9,8},{10,11... | collective-permute-start | bytes 196616 | tf_op jit(solution)/shard_map/ppermute | solution.py:50
  51.0 9.1 %collective-permute-start.12 = (f32[72,128]{1,0:T(8,128)S(1)}, f32[72,128]{1,0:T(8,128)S(1)}, u32[]{:S(2)}, u32[]{:S(2)}) collective-permute-start(f32[72,128]{1,0:T(8,128)S(1)} %get-tuple-element.77), channel_id=1, source_target_pairs={{4,8},{8,4},{12,16},{16,12},{20,24},{24,20},{5,9},{9,5},{13,17},{1... | collective-permute-start | bytes 110600 | tf_op jit(solution)/shard_map/ppermute | solution.py:50
  51.7 8.4 %collective-permute-start.13 = (f32[72,128]{1,0:T(8,128)S(1)}, f32[72,128]{1,0:T(8,128)S(1)}, u32[]{:S(2)}, u32[]{:S(2)}) collective-permute-start(f32[72,128]{1,0:T(8,128)S(1)} %get-tuple-element.78), channel_id=1, source_target_pairs={{1,2},{2,1},{5,6},{6,5},{9,10},{10,9},{13,14},{14,13},{17,18},{18,... | collective-permute-start | bytes 110600 | tf_op jit(solution)/shard_map/ppermute | solution.py:50
  52.3 7.8 %collective-permute-start.15 = (f32[72,128]{1,0:T(8,128)S(1)}, f32[72,128]{1,0:T(8,128)S(1)}, u32[]{:S(2)}, u32[]{:S(2)}) collective-permute-start(f32[72,128]{1,0:T(8,128)S(1)} %get-tuple-element.79), channel_id=1, source_target_pairs={{0,1},{1,0},{2,3},{3,2},{4,5},{5,4},{6,7},{7,6},{8,9},{9,8},{10,11... | collective-permute-start | bytes 110600 | tf_op jit(solution)/shard_map/ppermute | solution.py:50
  54.8 6.7 %collective-permute-start.14 = (f32[72,128]{1,0:T(8,128)S(1)}, f32[72,128]{1,0:T(8,128)S(1)}, u32[]{:S(2)}, u32[]{:S(2)}) collective-permute-start(f32[72,128]{1,0:T(8,128)S(1)} %get-tuple-element.76.refs_6_), channel_id=1, source_target_pairs={{0,4},{4,0},{8,12},{12,8},{16,20},{20,16},{24,28},{28,24},{1,5},{5... | collective-permute-start | bytes 110600 | tf_op jit(solution)/shard_map/ppermute | solution.py:50
  61.8 10.1 %collective-permute-start.16 = (f32[264,128]{1,0:T(8,128)S(1)}, f32[264,128]{1,0:T(8,128)S(1)}, u32[]{:S(2)}, u32[]{:S(2)}) collective-permute-start(f32[264,128]{1,0:T(8,128)S(1)} %get-tuple-element.83), channel_id=1, source_target_pairs={{4,8},{8,4},{12,16},{16,12},{20,24},{24,20},{5,9},{9,5},{13,17},{1... | collective-permute-start | bytes 405512 | tf_op jit(solution)/shard_map/ppermute | solution.py:50
  62.5 9.4 %collective-permute-start.18 = (f32[264,128]{1,0:T(8,128)S(1)}, f32[264,128]{1,0:T(8,128)S(1)}, u32[]{:S(2)}, u32[]{:S(2)}) collective-permute-start(f32[264,128]{1,0:T(8,128)S(1)} %get-tuple-element.80.refs_10_), channel_id=1, source_target_pairs={{0,4},{4,0},{8,12},{12,8},{16,20},{20,16},{24,28},{28,24},{1,5},{5... | collective-permute-start | bytes 405512 | tf_op jit(solution)/shard_map/ppermute | solution.py:50
  67.2 4.7 %collective-permute-start.17 = (f32[4,8,4,128]{3,2,1,0:T(4,128)S(1)}, f32[4,8,4,128]{3,2,1,0:T(4,128)S(1)}, u32[]{:S(2)}, u32[]{:S(2)}) collective-permute-start(f32[4,8,4,128]{3,2,1,0:T(4,128)S(1)} %get-tuple-element.84), channel_id=1, source_target_pairs={{1,2},{2,1},{5,6},{6,5},{9,10},{10,9},{13,14},{14,13},{17,18},{18,... | collective-permute-start | bytes 196616 | tf_op jit(solution)/shard_map/ppermute | solution.py:50
  67.9 4.0 %collective-permute-start.19 = (f32[4,8,4,128]{3,2,1,0:T(4,128)S(1)}, f32[4,8,4,128]{3,2,1,0:T(4,128)S(1)}, u32[]{:S(2)}, u32[]{:S(2)}) collective-permute-start(f32[4,8,4,128]{3,2,1,0:T(4,128)S(1)} %get-tuple-element.85), channel_id=1, source_target_pairs={{0,1},{1,0},{2,3},{3,2},{4,5},{5,4},{6,7},{7,6},{8,9},{9,8},{10,11... | collective-permute-start | bytes 196616 | tf_op jit(solution)/shard_map/ppermute | solution.py:50
  72.3 10.0 %collective-permute-start.20 = (f32[72,128]{1,0:T(8,128)S(1)}, f32[72,128]{1,0:T(8,128)S(1)}, u32[]{:S(2)}, u32[]{:S(2)}) collective-permute-start(f32[72,128]{1,0:T(8,128)S(1)} %get-tuple-element.89), channel_id=1, source_target_pairs={{4,8},{8,4},{12,16},{16,12},{20,24},{24,20},{5,9},{9,5},{13,17},{1... | collective-permute-start | bytes 110600 | tf_op jit(solution)/shard_map/ppermute | solution.py:50
  73.0 9.3 %collective-permute-start.21 = (f32[72,128]{1,0:T(8,128)S(1)}, f32[72,128]{1,0:T(8,128)S(1)}, u32[]{:S(2)}, u32[]{:S(2)}) collective-permute-start(f32[72,128]{1,0:T(8,128)S(1)} %get-tuple-element.90), channel_id=1, source_target_pairs={{1,2},{2,1},{5,6},{6,5},{9,10},{10,9},{13,14},{14,13},{17,18},{18,... | collective-permute-start | bytes 110600 | tf_op jit(solution)/shard_map/ppermute | solution.py:50
  73.7 8.6 %collective-permute-start.23 = (f32[72,128]{1,0:T(8,128)S(1)}, f32[72,128]{1,0:T(8,128)S(1)}, u32[]{:S(2)}, u32[]{:S(2)}) collective-permute-start(f32[72,128]{1,0:T(8,128)S(1)} %get-tuple-element.91), channel_id=1, source_target_pairs={{0,1},{1,0},{2,3},{3,2},{4,5},{5,4},{6,7},{7,6},{8,9},{9,8},{10,11... | collective-permute-start | bytes 110600 | tf_op jit(solution)/shard_map/ppermute | solution.py:50
  76.7 6.1 %collective-permute-start.22 = (f32[72,128]{1,0:T(8,128)S(1)}, f32[72,128]{1,0:T(8,128)S(1)}, u32[]{:S(2)}, u32[]{:S(2)}) collective-permute-start(f32[72,128]{1,0:T(8,128)S(1)} %get-tuple-element.87.refs_6_), channel_id=1, source_target_pairs={{0,4},{4,0},{8,12},{12,8},{16,20},{20,16},{24,28},{28,24},{1,5},{5... | collective-permute-start | bytes 110600 | tf_op jit(solution)/shard_map/ppermute | solution.py:50
  (10 other events, 18.7 us)
where the time goes:
time: 84.3 us; the launch traced here: 83.8 us
  starting transfers between devices  52.5 us (62%)
  Pallas kernels  16.9 us (20%)
  waiting for transfers between devices  9.9 us (12%)
  local copies, waits for them, and re-layouts  3.49 us (4%)
  between operations  1.05 us (1%)
    ppermute x24, starting transfers between devices, swap(): return lax.ppermute(values, axis, pairs)  48.7 us
    pallas_call x17, Pallas kernels, call(): pl.pallas_call(body, out_shape=[jax.ShapeDtypeStruct(s, F32) for s in out...  16.9 us
    all_to_all x1, waiting for transfers between devices, shards(): lax.all_to_all(rows, ('gx', 'gz'), split_axis=0, concat_axis=0, tiled=True)  5.53 us
    ppermute x24, waiting for transfers between devices, swap(): return lax.ppermute(values, axis, pairs)  4.37 us
    all_to_all x1, starting transfers between devices, shards(): lax.all_to_all(rows, ('gx', 'gz'), split_axis=0, concat_axis=0, tiled=True)  3.79 us
    unnamed x34, local copies, waits for them, and re-layouts  3.49 us
  transfers between devices with their start and end apart: 25, of which 5 were waited for; matrix products, arithmetic and copies ran while one was open for 0% of the time, Pallas kernels for 15%

commit v1 on v0

--- a/solution.py
+++ b/solution.py
@@ -170,7 +170,8 @@
     for r in range(reach):
         source = strip - (r - reach // 2)
         valid = inside & (source >= 0) & (source < n_gx)
-        row = table[pl.ds(jnp.where(valid, source * n_gz + band, 0), 1), :]
+        at = jnp.where(valid, source * n_gz + band, 0) * 8
+        row = table[pl.ds(pl.multiple_of(at, 8), 8), :][0:1]
         here = ((lane & (LANES // 2 - 1)) // slots == r) & valid
         got = jnp.where(here, row, got)
     turned = pltpu.roll(got, LANES // 2, 1)
@@ -626,13 +627,21 @@
         flops=40_000_000,
     )
     own, rows = call(
-        own_list_kernel, "own_list", [(quants, 16, LANES), (n_gx * n_gz, LANES)],
+        own_list_kernel, "own_list", [(quants, 16, LANES), (n_gx * n_gz * 8, LANES)],
         [traces, surface_map, surface_normals], [(surface_map.shape[0], 8, LANES)], after=[rims[3]],
     )
     lists = lax.all_to_all(rows, ("gx", "gz"), split_axis=0, concat_axis=0, tiled=True)
     sent_four = call(
         outgoing_kernel, "outgoing", [sent, sent, sent, sent], [traces, send_faces],
         [(4, quants, 16, LANES)], flops=10_000_000, after=[rows],
+    )
+    (moved,) = call(
+        advection_kernel, "advection", [(3, nx, nz, ny)],
+        [air_state, wind_field, *rims], [ext], flops=10_000_000, after=[rows],
+    )
+    volume, token = call(
+        volume_kernel, "volume", [solid_state.shape, tile], [state, integral, jacobians, stiffness],
+        [(dims * pad, quants * width), (dims * pad, LANES)], flops=10_000_000, after=[rows],
     )
     pressure_x = (HEAD + RADIUS * nz, ny)
     pressure_z = (HEAD + nx * ZRIM, ny)
@@ -640,18 +649,9 @@
     both_z = (pressure_z[0] + sent[0], LANES)
     raw, xb, zb, xa, za = call(
         raw_pressure_kernel, "raw_pressure", [block, both_x, both_z, both_x, both_z],
-        [air_state, wind_field, air_medium, *rims, *sent_four], [ext],
+        [air_state, wind_field, air_medium, *rims, *sent_four], [ext], after=[moved, token],
     )
     both = exchange(xb, zb, xa, za)
-    (moved,) = call(
-        advection_kernel, "advection", [(3, nx, nz, ny)],
-        [air_state, wind_field, *rims], [ext], flops=10_000_000, after=[xa],
-    )
-    volume, token = call(
-        volume_kernel, "volume", [solid_state.shape, tile], [state, integral, jacobians, stiffness],
-        [(dims * pad, quants * width), (dims * pad, LANES)], flops=10_000_000, after=[xa],
-    )
-
     rim_x = (HEAD + 4 * RADIUS * nz, ny)
     rim_z = (4, nx, RADIUS, ny)
     air, xb, zb, xa, za, answer = call(

time: 84.3 us -> 82.2 us (0.975)
  waiting for transfers between devices: 9.9 us -> 3.01 us
  starting transfers between devices: 52.5 us -> 57.5 us
    all_to_all x1, waiting for transfers between devices: 5.53 us -> 0.01 us  [shards(): lax.all_to_all(rows, ('gx', 'gz'), split_axis=0, concat_axis=0, tiled=True)]
    ppermute x24, starting transfers between devices: 48.7 us -> 52.7 us  [swap(): return lax.ppermute(values, axis, pairs)]
    ppermute x24, waiting for transfers between devices: 4.37 us -> 3.01 us  [swap(): return lax.ppermute(values, axis, pairs)]
    all_to_all x1, starting transfers between devices: 3.79 us -> 4.73 us  [shards(): lax.all_to_all(rows, ('gx', 'gz'), split_axis=0, concat_axis=0, tiled=True)]
    unnamed x34 -> x30, local copies, waits for them, and re-layouts: 3.49 us -> 3.2 us
  transfers between devices with their start and end apart: 25 -> 25, of which waited for: 5 -> 4; matrix products, arithmetic and copies ran while one was open for 0% -> 0% of each run, Pallas kernels for 15% -> 16%
where the time goes in v1:
time: 82.2 us; the launch traced here: 81.6 us
  starting transfers between devices  57.5 us (70%)
  Pallas kernels  16.9 us (21%)
  local copies, waits for them, and re-layouts  3.2 us (4%)
  waiting for transfers between devices  3.01 us (4%)
  between operations  1.03 us (1%)
    ppermute x24, starting transfers between devices, swap(): return lax.ppermute(values, axis, pairs)  52.7 us
    pallas_call x17, Pallas kernels, call(): pl.pallas_call(body, out_shape=[jax.ShapeDtypeStruct(s, F32) for s in out...  16.9 us
    all_to_all x1, starting transfers between devices, shards(): lax.all_to_all(rows, ('gx', 'gz'), split_axis=0, concat_axis=0, tiled=True)  4.73 us
    unnamed x30, local copies, waits for them, and re-layouts  3.2 us
    ppermute x24, waiting for transfers between devices, swap(): return lax.ppermute(values, axis, pairs)  3.01 us
  transfers between devices with their start and end apart: 25, of which 4 were waited for; matrix products, arithmetic and copies ran while one was open for 0% of the time, Pallas kernels for 16%

profile of v1, /device:TPU:0, one launch (start us, length us, event | category | flops | bytes accessed | tf_op | source)
XLA Modules:
  0.0 81.6 jit_solution(11697542936386708129)
XLA Ops:
  0.6 0.9 %copy-done = f32[3,8,16,128]{3,2,1,0:T(8,128)S(1)} copy-done((f32[3,8,16,128]{3,2,1,0:T(8,128)S(1)}, f32[3,8,16,128]{3,2,1,0:T(8,128)}, u32[]{:S(2)}) %copy-start) | copy-done | bytes 196632
  1.6 0.9 %copy-done.3 = f32[4,8,16,128]{3,2,1,0:T(8,128)S(1)} copy-done((f32[4,8,16,128]{3,2,1,0:T(8,128)S(1)}, f32[4,8,16,128]{3,2,1,0:T(8,128)}, u32[]{:S(2)}) %copy-start.3) | copy-done | bytes 262168
  2.5 0.8 raw_rims.1
  4.4 5.3 %collective-permute-start.3 = (f32[7,4,16,128]{3,2,1,0:T(8,128)S(1)}, f32[7,4,16,128]{3,2,1,0:T(8,128)S(1)}, u32[]{:S(2)}, u32[]{:S(2)}) collective-permute-start(f32[7,4,16,128]{3,2,1,0:T(8,128)S(1)} %get-tuple-element.56), channel_id=1, source_target_pairs={{0,4},{4,0},{8,12},{12,8},{16,20},{20,16},{24,28},{28,24},{1,5},{5... | collective-permute-start | bytes 688136 | tf_op jit(solution)/shard_map/ppermute | solution.py:50
  9.7 0.9 %copy-done.7 = f32[9,20,256]{2,1,0:T(8,128)S(1)} copy-done((f32[9,20,256]{2,1,0:T(8,128)S(1)}, f32[9,20,256]{2,1,0:T(8,128)}, u32[]{:S(2)}) %copy-start.7) | copy-done | bytes 184344
  10.7 2.5 %predict.1 = (f32[32,2304]{1,0:T(8,128)S(1)}, f32[9,16,1024]{2,1,0:T(8,128)S(1)}, f32[9,20,256]{2,1,0:T(8,128)S(1)}) custom-call(f32[9,20,256]{2,1,0:T(8,128)S(1)} %copy-done.7, f32[9,9,3,256]{3,2,1,0:T(4,128)S(1)} %bitcast.11, f32[3,20,20]{2,1,0:T(8,128)S(1)} %copy-done.9, f32[10,4,20]{2,1,0:T(4,128)S(1)} %bitcast.20), custom_call_target="tpu_custom_call" | custom-call | flops 40000000 | bytes 1510208 | tf_op jit(solution)/shard_map/predict/pallas_call | solution.py:31
  13.2 1.6 %own_list.1 = (f32[9,16,128]{2,1,0:T(8,128)S(1)}, f32[256,128]{1,0:T(8,128)}) custom-call(f32[9,16,1024]{2,1,0:T(8,128)S(1)} %get-tuple-element.49.refs_0_.refs_1_, s32[5,3,8]{2,1,0:T(4,128)S(1)} %bitcast.17, f32[5,3,8]{2,1,0:T(4,128)S(1)} %bitcast.21, f32[7,8,4,128]{3,2,1,0:T(4,128)S(1)} %collective-permute-done.refs_3_.refs_5_.refs_6_.refs_8_), custom_call_target="tpu_custom_call" | custom-call | flops 1000000 | bytes 795584 | tf_op jit(solution)/shard_map/own_list/pallas_call | solution.py:31
  14.8 4.7 %all-to-all-start = ((f32[32,8,128]{2,1,0:T(8,128)}), f32[32,8,128]{2,1,0:T(8,128)S(1)}, u32[]{:S(2)}, u32[]{:S(2)}) async-start(f32[32,8,128]{2,1,0:T(8,128)} %bitcast.6), calls=%async_computation | async-start | bytes 262144 | tf_op jit(solution)/shard_map/all_to_all | solution.py:633
  19.6 0.7 collective-permute-start.2
  20.3 1.5 %outgoing.1 = (f32[96,128]{1,0:T(8,128)S(1)}, f32[96,128]{1,0:T(8,128)S(1)}, f32[96,128]{1,0:T(8,128)S(1)}, f32[96,128]{1,0:T(8,128)S(1)}) custom-call(f32[9,16,1024]{2,1,0:T(8,128)S(1)} %get-tuple-element.49.refs_0_.refs_1_, s32[4,128]{1,0:T(4,128)S(1)} %copy-done.14, f32[256,128]{1,0:T(8,128)} %get-tuple-element.51.refs_4_.refs_2_.refs_6_), custom_call_target="tpu_custom_call" | custom-call | flops 10000000 | bytes 788480 | tf_op jit(solution)/shard_map/outgoing/pallas_call | solution.py:31
  21.8 1.1 %volume.1 = (f32[9,20,256]{2,1,0:T(8,128)S(1)}, f32[8,128]{1,0:T(8,128)S(1)}) custom-call(f32[9,20,256]{2,1,0:T(8,128)S(1)} %get-tuple-element.47.refs_0_, f32[32,2304]{1,0:T(8,128)S(1)} %get-tuple-element.48.refs_1_, f32[9,9,3,256]{3,2,1,0:T(4,128)S(1)} %bitcast.12, f32[3,20,20]{2,1,0:T(8,128)S(1)} %copy-done.9, ...), custom_call_target="tpu_custom_call" | custom-call | flops 10000000 | bytes 921280 | tf_op jit(solution)/shard_map/volume/pallas_call | solution.py:31
  24.1 0.7 collective-permute-start.4
  24.8 0.7 collective-permute-start.5
  25.5 4.5 %collective-permute-start.6 = (f32[168,128]{1,0:T(8,128)S(1)}, f32[168,128]{1,0:T(8,128)S(1)}, u32[]{:S(2)}, u32[]{:S(2)}) collective-permute-start(f32[168,128]{1,0:T(8,128)S(1)} %get-tuple-element.64), channel_id=1, source_target_pairs={{0,4},{4,0},{8,12},{12,8},{16,20},{20,16},{24,28},{28,24},{1,5},{5... | collective-permute-start | bytes 258056 | tf_op jit(solution)/shard_map/ppermute | solution.py:50
  30.0 5.1 %collective-permute-start.7 = (f32[168,128]{1,0:T(8,128)S(1)}, f32[168,128]{1,0:T(8,128)S(1)}, u32[]{:S(2)}, u32[]{:S(2)}) collective-permute-start(f32[168,128]{1,0:T(8,128)S(1)} %get-tuple-element.65), channel_id=1, source_target_pairs={{0,1},{1,0},{2,3},{3,2},{4,5},{5,4},{6,7},{7,6},{8,9},{9,8},{10,11... | collective-permute-start | bytes 258056 | tf_op jit(solution)/shard_map/ppermute | solution.py:50
  35.2 0.9 %collective-permute-done.7.refs_12_.refs_9_ = f32[168,128]{1,0:T(8,128)S(1)} collective-permute-done((f32[168,128]{1,0:T(8,128)S(1)}, f32[168,128]{1,0:T(8,128)S(1)}, u32[]{:S(2)}, u32[]{:S(2)}) %collective-permute-start.7) | collective-permute-done | bytes 86048 | tf_op jit(solution)/shard_map/ppermute | solution.py:50
  36.1 1.1 %injected.1 = (f32[4,8,16,128]{3,2,1,0:T(8,128)S(1)}, f32[264,128]{1,0:T(8,128)S(1)}, f32[4,8,4,128]{3,2,1,0:T(4,128)S(1)}, f32[264,128]{1,0:T(8,128)S(1)}, f32[...) custom-call(f32[4,8,16,128]{3,2,1,0:T(8,128)S(1)} %copy-done.4, f32[3,8,16,128]{3,2,1,0:T(8,128)S(1)} %copy-done.1, ...), custom_call_target="tpu_custom_call" | custom-call | flops 1000000 | bytes 2679776 | tf_op jit(solution)/shard_map/injected/pallas_call | solution.py:31
  37.2 0.7 collective-permute-start.8
  37.8 4.1 %collective-permute-start.10 = (f32[264,128]{1,0:T(8,128)S(1)}, f32[264,128]{1,0:T(8,128)S(1)}, u32[]{:S(2)}, u32[]{:S(2)}) collective-permute-start(f32[264,128]{1,0:T(8,128)S(1)} %get-tuple-element.67.refs_10_), channel_id=1, source_target_pairs={{0,4},{4,0},{8,12},{12,8},{16,20},{20,16},{24,28},{28,24},{1,5},{5... | collective-permute-start | bytes 405512 | tf_op jit(solution)/shard_map/ppermute | solution.py:50
  42.6 4.3 %collective-permute-start.11 = (f32[4,8,4,128]{3,2,1,0:T(4,128)S(1)}, f32[4,8,4,128]{3,2,1,0:T(4,128)S(1)}, u32[]{:S(2)}, u32[]{:S(2)}) collective-permute-start(f32[4,8,4,128]{3,2,1,0:T(4,128)S(1)} %get-tuple-element.72), channel_id=1, source_target_pairs={{0,1},{1,0},{2,3},{3,2},{4,5},{5,4},{6,7},{7,6},{8,9},{9,8},{10,11... | collective-permute-start | bytes 196616 | tf_op jit(solution)/shard_map/ppermute | solution.py:50
  47.0 1.8 %flux.2 = (f32[9,20,256]{2,1,0:T(8,128)S(1)}, f32[8,128]{1,0:T(8,128)S(1)}) custom-call(f32[9,20,256]{2,1,0:T(8,128)S(1)} %get-tuple-element.52.refs_0_, f32[9,16,1024]{2,1,0:T(8,128)S(1)} %get-tuple-element.49.refs_0_.refs_1_, f32[9,16,128]{2,1,0:T(8,128)S(1)} %get-tuple-element.53.refs_2_, f32[9,9,4,256]{3,2,1,0:T(4,128)S(1)} %bitcast.8, ...), custom_call_target="tpu_custom_call" | custom-call | flops 20000000 | bytes 1719424 | tf_op jit(solution)/shard_map/flux/pallas_call | solution.py:31
  50.5 3.1 %collective-permute-start.15 = (f32[72,128]{1,0:T(8,128)S(1)}, f32[72,128]{1,0:T(8,128)S(1)}, u32[]{:S(2)}, u32[]{:S(2)}) collective-permute-start(f32[72,128]{1,0:T(8,128)S(1)} %get-tuple-element.79), channel_id=1, source_target_pairs={{0,1},{1,0},{2,3},{3,2},{4,5},{5,4},{6,7},{7,6},{8,9},{9,8},{10,11... | collective-permute-start | bytes 110600 | tf_op jit(solution)/shard_map/ppermute | solution.py:50
  53.6 3.8 %collective-permute-start.14 = (f32[72,128]{1,0:T(8,128)S(1)}, f32[72,128]{1,0:T(8,128)S(1)}, u32[]{:S(2)}, u32[]{:S(2)}) collective-permute-start(f32[72,128]{1,0:T(8,128)S(1)} %get-tuple-element.76.refs_6_), channel_id=1, source_target_pairs={{0,4},{4,0},{8,12},{12,8},{16,20},{20,16},{24,28},{28,24},{1,5},{5... | collective-permute-start | bytes 110600 | tf_op jit(solution)/shard_map/ppermute | solution.py:50
  57.9 1.4 %collective-permute-done.14.refs_6_.refs_7_ = f32[72,128]{1,0:T(8,128)S(1)} collective-permute-done((f32[72,128]{1,0:T(8,128)S(1)}, f32[72,128]{1,0:T(8,128)S(1)}, u32[]{:S(2)}, u32[]{:S(2)}) %collective-permute-start.14) | collective-permute-done | bytes 36896 | tf_op jit(solution)/shard_map/ppermute | solution.py:50
  59.6 0.7 collective-permute-start.16
  60.3 4.2 %collective-permute-start.18 = (f32[264,128]{1,0:T(8,128)S(1)}, f32[264,128]{1,0:T(8,128)S(1)}, u32[]{:S(2)}, u32[]{:S(2)}) collective-permute-start(f32[264,128]{1,0:T(8,128)S(1)} %get-tuple-element.80.refs_10_), channel_id=1, source_target_pairs={{0,4},{4,0},{8,12},{12,8},{16,20},{20,16},{24,28},{28,24},{1,5},{5... | collective-permute-start | bytes 405512 | tf_op jit(solution)/shard_map/ppermute | solution.py:50
  65.2 2.1 %collective-permute-start.19 = (f32[4,8,4,128]{3,2,1,0:T(4,128)S(1)}, f32[4,8,4,128]{3,2,1,0:T(4,128)S(1)}, u32[]{:S(2)}, u32[]{:S(2)}) collective-permute-start(f32[4,8,4,128]{3,2,1,0:T(4,128)S(1)} %get-tuple-element.85), channel_id=1, source_target_pairs={{0,1},{1,0},{2,3},{3,2},{4,5},{5,4},{6,7},{7,6},{8,9},{9,8},{10,11... | collective-permute-start | bytes 196616 | tf_op jit(solution)/shard_map/ppermute | solution.py:50
  67.3 1.8 %flux.3 = (f32[9,20,256]{2,1,0:T(8,128)S(1)}, f32[8,128]{1,0:T(8,128)S(1)}) custom-call(f32[9,20,256]{2,1,0:T(8,128)S(1)} %get-tuple-element.68.refs_0_, f32[9,16,1024]{2,1,0:T(8,128)S(1)} %get-tuple-element.49.refs_0_.refs_1_, f32[9,16,128]{2,1,0:T(8,128)S(1)} %get-tuple-element.53.refs_2_, f32[9,9,4,256]{3,2,1,0:T(4,128)S(1)} %bitcast.9, ...), custom_call_target="tpu_custom_call" | custom-call | flops 20000000 | bytes 1719424 | tf_op jit(solution)/shard_map/flux/pallas_call | solution.py:31
  71.0 2.9 %collective-permute-start.23 = (f32[72,128]{1,0:T(8,128)S(1)}, f32[72,128]{1,0:T(8,128)S(1)}, u32[]{:S(2)}, u32[]{:S(2)}) collective-permute-start(f32[72,128]{1,0:T(8,128)S(1)} %get-tuple-element.91), channel_id=1, source_target_pairs={{0,1},{1,0},{2,3},{3,2},{4,5},{5,4},{6,7},{7,6},{8,9},{9,8},{10,11... | collective-permute-start | bytes 110600 | tf_op jit(solution)/shard_map/ppermute | solution.py:50
  74.0 4.7 %collective-permute-start.22 = (f32[72,128]{1,0:T(8,128)S(1)}, f32[72,128]{1,0:T(8,128)S(1)}, u32[]{:S(2)}, u32[]{:S(2)}) collective-permute-start(f32[72,128]{1,0:T(8,128)S(1)} %get-tuple-element.87.refs_6_), channel_id=1, source_target_pairs={{0,4},{4,0},{8,12},{12,8},{16,20},{20,16},{24,28},{28,24},{1,5},{5... | collective-permute-start | bytes 110600 | tf_op jit(solution)/shard_map/ppermute | solution.py:50
  79.2 0.9 %replies.1 = f32[9,20,256]{2,1,0:T(8,128)} custom-call(f32[9,20,256]{2,1,0:T(8,128)S(1)} %get-tuple-element.81.refs_0_, f32[9,9,4,256]{3,2,1,0:T(4,128)S(1)} %bitcast.10, f32[10,4,20]{2,1,0:T(4,128)S(1)} %bitcast.16, s32[4,256]{1,0:T(4,128)S(1)} %copy-done.11, s32[5,3,8]{2,1,0:T(4,128)S(1)} %bitcast.19, f32[1,128]{1,0:T(1,128)S(1)} %get-tuple-element.73.refs_7_.refs_5_, ...), custom_call_target="tpu_custom_call" | custom-call | flops 1000000 | bytes 782432 | tf_op jit(solution)/shard_map/replies/pallas_call | solution.py:31
  80.6 0.9 %velocity.3 = f32[4,8,16,128]{3,2,1,0:T(8,128)} custom-call(f32[4,8,16,128]{3,2,1,0:T(8,128)S(1)} %get-tuple-element.82.refs_0_, f32[1,8,16,128]{3,2,1,0:T(8,128)S(1)} %get-tuple-element.88.refs_1_, f32[2,8,16,128]{3,2,1,0:T(8,128)S(1)} %copy-done.2, f32[3,8,16,128]{3,2,1,0:T(8,128)S(1)} %advection.5.refs_8_.refs_3_, ...), custom_call_target="tpu_custom_call" | custom-call | flops 1000000 | bytes 1064960 | tf_op jit(solution)/shard_map/velocity/pallas_call | solution.py:31
  (65 shorter events, 9.1 us)
Async XLA Ops:
  2.5 7.2 %copy-start.6 = (f32[3,9,9,256]{3,0,2,1:T(4,128)S(1)}, f32[3,9,9,256]{3,0,2,1:T(4,128)}, u32[]{:S(2)}) copy-start(f32[3,9,9,256]{3,0,2,1:T(4,128)} %param.14) | copy-start | bytes 746500
  2.5 7.2 %copy-start.9 = (f32[3,20,20]{2,1,0:T(8,128)S(1)}, f32[3,20,20]{2,1,0:T(8,128)}, u32[]{:S(2)}) copy-start(f32[3,20,20]{2,1,0:T(8,128)} %refs_3_.2) | copy-start | bytes 14404
  2.5 7.2 %copy-start.12 = (f32[4,10,20]{2,0,1:T(4,128)S(1)}, f32[4,10,20]{2,0,1:T(4,128)}, u32[]{:S(2)}) copy-start(f32[4,10,20]{2,0,1:T(4,128)} %param.17) | copy-start | bytes 9604
  3.3 9.9 %collective-permute-start = (f32[7,8,4,128]{3,2,1,0:T(4,128)S(1)}, f32[7,8,4,128]{3,2,1,0:T(4,128)S(1)}, u32[]{:S(2)}, u32[]{:S(2)}) collective-permute-start(f32[7,8,4,128]{3,2,1,0:T(4,128)S(1)} %get-tuple-element.50), channel_id=1, source_target_pairs={{0,1},{1,0},{2,3},{3,2},{4,5},{5,4},{6,7},{7,6},{8,9},{9,8},{10,11... | collective-permute-start | bytes 344072 | tf_op jit(solution)/shard_map/ppermute | solution.py:50
  3.7 19.2 %collective-permute-start.1 = (f32[7,4,16,128]{3,2,1,0:T(8,128)}, f32[7,4,16,128]{3,2,1,0:T(8,128)S(1)}, u32[]{:S(2)}, u32[]{:S(2)}) collective-permute-start(f32[7,4,16,128]{3,2,1,0:T(8,128)} %get-tuple-element.54), channel_id=1, source_target_pairs={{4,8},{8,4},{12,16},{16,12},{20,24},{24,20},{5,9},{9,5},{13,17},{1... | collective-permute-start | bytes 688136 | tf_op jit(solution)/shard_map/ppermute | solution.py:50
  4.4 18.5 %collective-permute-start.3 = (f32[7,4,16,128]{3,2,1,0:T(8,128)S(1)}, f32[7,4,16,128]{3,2,1,0:T(8,128)S(1)}, u32[]{:S(2)}, u32[]{:S(2)}) collective-permute-start(f32[7,4,16,128]{3,2,1,0:T(8,128)S(1)} %get-tuple-element.56), channel_id=1, source_target_pairs={{0,4},{4,0},{8,12},{12,8},{16,20},{20,16},{24,28},{28,24},{1,5},{5... | collective-permute-start | bytes 688136 | tf_op jit(solution)/shard_map/ppermute | solution.py:50
  14.8 5.4 %copy-start.14 = (s32[4,128]{1,0:T(4,128)S(1)}, s32[4,128]{1,0:T(4,128)}, u32[]{:S(2)}) copy-start(s32[4,128]{1,0:T(4,128)} %refs_1_.10) | copy-start | bytes 6148
  14.8 21.3 %all-to-all-start = ((f32[32,8,128]{2,1,0:T(8,128)}), f32[32,8,128]{2,1,0:T(8,128)S(1)}, u32[]{:S(2)}, u32[]{:S(2)}) async-start(f32[32,8,128]{2,1,0:T(8,128)} %bitcast.6), calls=%async_computation | async-start | bytes 262144 | tf_op jit(solution)/shard_map/all_to_all | solution.py:633
  19.6 3.3 %collective-permute-start.2 = (f32[7,8,4,128]{3,2,1,0:T(4,128)S(1)}, f32[7,8,4,128]{3,2,1,0:T(4,128)S(1)}, u32[]{:S(2)}, u32[]{:S(2)}) collective-permute-start(f32[7,8,4,128]{3,2,1,0:T(4,128)S(1)} %get-tuple-element.55), channel_id=1, source_target_pairs={{1,2},{2,1},{5,6},{6,5},{9,10},{10,9},{13,14},{14,13},{17,18},{18,... | collective-permute-start | bytes 344072 | tf_op jit(solution)/shard_map/ppermute | solution.py:50
  24.1 11.0 %collective-permute-start.4 = (f32[168,128]{1,0:T(8,128)S(1)}, f32[168,128]{1,0:T(8,128)S(1)}, u32[]{:S(2)}, u32[]{:S(2)}) collective-permute-start(f32[168,128]{1,0:T(8,128)S(1)} %get-tuple-element.62), channel_id=1, source_target_pairs={{4,8},{8,4},{12,16},{16,12},{20,24},{24,20},{5,9},{9,5},{13,17},{1... | collective-permute-start | bytes 258056 | tf_op jit(solution)/shard_map/ppermute | solution.py:50
  24.8 10.4 %collective-permute-start.5 = (f32[168,128]{1,0:T(8,128)S(1)}, f32[168,128]{1,0:T(8,128)S(1)}, u32[]{:S(2)}, u32[]{:S(2)}) collective-permute-start(f32[168,128]{1,0:T(8,128)S(1)} %get-tuple-element.63), channel_id=1, source_target_pairs={{1,2},{2,1},{5,6},{6,5},{9,10},{10,9},{13,14},{14,13},{17,18},{18,... | collective-permute-start | bytes 258056 | tf_op jit(solution)/shard_map/ppermute | solution.py:50
  25.5 9.7 %collective-permute-start.6 = (f32[168,128]{1,0:T(8,128)S(1)}, f32[168,128]{1,0:T(8,128)S(1)}, u32[]{:S(2)}, u32[]{:S(2)}) collective-permute-start(f32[168,128]{1,0:T(8,128)S(1)} %get-tuple-element.64), channel_id=1, source_target_pairs={{0,4},{4,0},{8,12},{12,8},{16,20},{20,16},{24,28},{28,24},{1,5},{5... | collective-permute-start | bytes 258056 | tf_op jit(solution)/shard_map/ppermute | solution.py:50
  30.0 6.1 %collective-permute-start.7 = (f32[168,128]{1,0:T(8,128)S(1)}, f32[168,128]{1,0:T(8,128)S(1)}, u32[]{:S(2)}, u32[]{:S(2)}) collective-permute-start(f32[168,128]{1,0:T(8,128)S(1)} %get-tuple-element.65), channel_id=1, source_target_pairs={{0,1},{1,0},{2,3},{3,2},{4,5},{5,4},{6,7},{7,6},{8,9},{9,8},{10,11... | collective-permute-start | bytes 258056 | tf_op jit(solution)/shard_map/ppermute | solution.py:50
  36.1 10.8 %copy-start.5 = (f32[4,9,9,256]{3,0,2,1:T(4,128)S(1)}, f32[4,9,9,256]{3,0,2,1:T(4,128)}, u32[]{:S(2)}) copy-start(f32[4,9,9,256]{3,0,2,1:T(4,128)} %param.15) | copy-start | bytes 995332
  36.1 10.8 %copy-start.8 = (f32[4,20,10]{1,0,2:T(4,128)S(1)}, f32[4,20,10]{1,0,2:T(4,128)}, u32[]{:S(2)}) copy-start(f32[4,20,10]{1,0,2:T(4,128)} %param.18) | copy-start | bytes 9604
  37.2 11.6 %collective-permute-start.8 = (f32[264,128]{1,0:T(8,128)S(1)}, f32[264,128]{1,0:T(8,128)S(1)}, u32[]{:S(2)}, u32[]{:S(2)}) collective-permute-start(f32[264,128]{1,0:T(8,128)S(1)} %get-tuple-element.70), channel_id=1, source_target_pairs={{4,8},{8,4},{12,16},{16,12},{20,24},{24,20},{5,9},{9,5},{13,17},{1... | collective-permute-start | bytes 405512 | tf_op jit(solution)/shard_map/ppermute | solution.py:50
  37.8 10.9 %collective-permute-start.10 = (f32[264,128]{1,0:T(8,128)S(1)}, f32[264,128]{1,0:T(8,128)S(1)}, u32[]{:S(2)}, u32[]{:S(2)}) collective-permute-start(f32[264,128]{1,0:T(8,128)S(1)} %get-tuple-element.67.refs_10_), channel_id=1, source_target_pairs={{0,4},{4,0},{8,12},{12,8},{16,20},{20,16},{24,28},{28,24},{1,5},{5... | collective-permute-start | bytes 405512 | tf_op jit(solution)/shard_map/ppermute | solution.py:50
  41.9 6.8 %collective-permute-start.9 = (f32[4,8,4,128]{3,2,1,0:T(4,128)S(1)}, f32[4,8,4,128]{3,2,1,0:T(4,128)S(1)}, u32[]{:S(2)}, u32[]{:S(2)}) collective-permute-start(f32[4,8,4,128]{3,2,1,0:T(4,128)S(1)} %get-tuple-element.71), channel_id=1, source_target_pairs={{1,2},{2,1},{5,6},{6,5},{9,10},{10,9},{13,14},{14,13},{17,18},{18,... | collective-permute-start | bytes 196616 | tf_op jit(solution)/shard_map/ppermute | solution.py:50
  42.6 4.4 %copy-start.11 = (s32[4,256]{1,0:T(4,128)S(1)}, s32[4,256]{1,0:T(4,128)}, u32[]{:S(2)}) copy-start(s32[4,256]{1,0:T(4,128)} %refs_3_.3) | copy-start | bytes 12292
  42.6 6.1 %collective-permute-start.11 = (f32[4,8,4,128]{3,2,1,0:T(4,128)S(1)}, f32[4,8,4,128]{3,2,1,0:T(4,128)S(1)}, u32[]{:S(2)}, u32[]{:S(2)}) collective-permute-start(f32[4,8,4,128]{3,2,1,0:T(4,128)S(1)} %get-tuple-element.72), channel_id=1, source_target_pairs={{0,1},{1,0},{2,3},{3,2},{4,5},{5,4},{6,7},{7,6},{8,9},{9,8},{10,11... | collective-permute-start | bytes 196616 | tf_op jit(solution)/shard_map/ppermute | solution.py:50
  49.2 8.7 %collective-permute-start.12 = (f32[72,128]{1,0:T(8,128)S(1)}, f32[72,128]{1,0:T(8,128)S(1)}, u32[]{:S(2)}, u32[]{:S(2)}) collective-permute-start(f32[72,128]{1,0:T(8,128)S(1)} %get-tuple-element.77), channel_id=1, source_target_pairs={{4,8},{8,4},{12,16},{16,12},{20,24},{24,20},{5,9},{9,5},{13,17},{1... | collective-permute-start | bytes 110600 | tf_op jit(solution)/shard_map/ppermute | solution.py:50
  49.8 8.1 %collective-permute-start.13 = (f32[72,128]{1,0:T(8,128)S(1)}, f32[72,128]{1,0:T(8,128)S(1)}, u32[]{:S(2)}, u32[]{:S(2)}) collective-permute-start(f32[72,128]{1,0:T(8,128)S(1)} %get-tuple-element.78), channel_id=1, source_target_pairs={{1,2},{2,1},{5,6},{6,5},{9,10},{10,9},{13,14},{14,13},{17,18},{18,... | collective-permute-start | bytes 110600 | tf_op jit(solution)/shard_map/ppermute | solution.py:50
  50.5 7.4 %collective-permute-start.15 = (f32[72,128]{1,0:T(8,128)S(1)}, f32[72,128]{1,0:T(8,128)S(1)}, u32[]{:S(2)}, u32[]{:S(2)}) collective-permute-start(f32[72,128]{1,0:T(8,128)S(1)} %get-tuple-element.79), channel_id=1, source_target_pairs={{0,1},{1,0},{2,3},{3,2},{4,5},{5,4},{6,7},{7,6},{8,9},{9,8},{10,11... | collective-permute-start | bytes 110600 | tf_op jit(solution)/shard_map/ppermute | solution.py:50
  53.6 5.8 %collective-permute-start.14 = (f32[72,128]{1,0:T(8,128)S(1)}, f32[72,128]{1,0:T(8,128)S(1)}, u32[]{:S(2)}, u32[]{:S(2)}) collective-permute-start(f32[72,128]{1,0:T(8,128)S(1)} %get-tuple-element.76.refs_6_), channel_id=1, source_target_pairs={{0,4},{4,0},{8,12},{12,8},{16,20},{20,16},{24,28},{28,24},{1,5},{5... | collective-permute-start | bytes 110600 | tf_op jit(solution)/shard_map/ppermute | solution.py:50
  59.6 9.5 %collective-permute-start.16 = (f32[264,128]{1,0:T(8,128)S(1)}, f32[264,128]{1,0:T(8,128)S(1)}, u32[]{:S(2)}, u32[]{:S(2)}) collective-permute-start(f32[264,128]{1,0:T(8,128)S(1)} %get-tuple-element.83), channel_id=1, source_target_pairs={{4,8},{8,4},{12,16},{16,12},{20,24},{24,20},{5,9},{9,5},{13,17},{1... | collective-permute-start | bytes 405512 | tf_op jit(solution)/shard_map/ppermute | solution.py:50
  60.3 9.0 %collective-permute-start.18 = (f32[264,128]{1,0:T(8,128)S(1)}, f32[264,128]{1,0:T(8,128)S(1)}, u32[]{:S(2)}, u32[]{:S(2)}) collective-permute-start(f32[264,128]{1,0:T(8,128)S(1)} %get-tuple-element.80.refs_10_), channel_id=1, source_target_pairs={{0,4},{4,0},{8,12},{12,8},{16,20},{20,16},{24,28},{28,24},{1,5},{5... | collective-permute-start | bytes 405512 | tf_op jit(solution)/shard_map/ppermute | solution.py:50
  64.5 4.6 %collective-permute-start.17 = (f32[4,8,4,128]{3,2,1,0:T(4,128)S(1)}, f32[4,8,4,128]{3,2,1,0:T(4,128)S(1)}, u32[]{:S(2)}, u32[]{:S(2)}) collective-permute-start(f32[4,8,4,128]{3,2,1,0:T(4,128)S(1)} %get-tuple-element.84), channel_id=1, source_target_pairs={{1,2},{2,1},{5,6},{6,5},{9,10},{10,9},{13,14},{14,13},{17,18},{18,... | collective-permute-start | bytes 196616 | tf_op jit(solution)/shard_map/ppermute | solution.py:50
  65.2 3.9 %collective-permute-start.19 = (f32[4,8,4,128]{3,2,1,0:T(4,128)S(1)}, f32[4,8,4,128]{3,2,1,0:T(4,128)S(1)}, u32[]{:S(2)}, u32[]{:S(2)}) collective-permute-start(f32[4,8,4,128]{3,2,1,0:T(4,128)S(1)} %get-tuple-element.85), channel_id=1, source_target_pairs={{0,1},{1,0},{2,3},{3,2},{4,5},{5,4},{6,7},{7,6},{8,9},{9,8},{10,11... | collective-permute-start | bytes 196616 | tf_op jit(solution)/shard_map/ppermute | solution.py:50
  69.7 10.4 %collective-permute-start.20 = (f32[72,128]{1,0:T(8,128)S(1)}, f32[72,128]{1,0:T(8,128)S(1)}, u32[]{:S(2)}, u32[]{:S(2)}) collective-permute-start(f32[72,128]{1,0:T(8,128)S(1)} %get-tuple-element.89), channel_id=1, source_target_pairs={{4,8},{8,4},{12,16},{16,12},{20,24},{24,20},{5,9},{9,5},{13,17},{1... | collective-permute-start | bytes 110600 | tf_op jit(solution)/shard_map/ppermute | solution.py:50
  70.3 9.7 %collective-permute-start.21 = (f32[72,128]{1,0:T(8,128)S(1)}, f32[72,128]{1,0:T(8,128)S(1)}, u32[]{:S(2)}, u32[]{:S(2)}) collective-permute-start(f32[72,128]{1,0:T(8,128)S(1)} %get-tuple-element.90), channel_id=1, source_target_pairs={{1,2},{2,1},{5,6},{6,5},{9,10},{10,9},{13,14},{14,13},{17,18},{18,... | collective-permute-start | bytes 110600 | tf_op jit(solution)/shard_map/ppermute | solution.py:50
  71.0 9.1 %collective-permute-start.23 = (f32[72,128]{1,0:T(8,128)S(1)}, f32[72,128]{1,0:T(8,128)S(1)}, u32[]{:S(2)}, u32[]{:S(2)}) collective-permute-start(f32[72,128]{1,0:T(8,128)S(1)} %get-tuple-element.91), channel_id=1, source_target_pairs={{0,1},{1,0},{2,3},{3,2},{4,5},{5,4},{6,7},{7,6},{8,9},{9,8},{10,11... | collective-permute-start | bytes 110600 | tf_op jit(solution)/shard_map/ppermute | solution.py:50
  74.0 6.6 %collective-permute-start.22 = (f32[72,128]{1,0:T(8,128)S(1)}, f32[72,128]{1,0:T(8,128)S(1)}, u32[]{:S(2)}, u32[]{:S(2)}) collective-permute-start(f32[72,128]{1,0:T(8,128)S(1)} %get-tuple-element.87.refs_6_), channel_id=1, source_target_pairs={{0,4},{4,0},{8,12},{12,8},{16,20},{20,16},{24,28},{28,24},{1,5},{5... | collective-permute-start | bytes 110600 | tf_op jit(solution)/shard_map/ppermute | solution.py:50
  (8 other events, 11.1 us)

commit v2 on v1

--- a/solution.py
+++ b/solution.py
@@ -628,7 +628,7 @@
     )
     own, rows = call(
         own_list_kernel, "own_list", [(quants, 16, LANES), (n_gx * n_gz * 8, LANES)],
-        [traces, surface_map, surface_normals], [(surface_map.shape[0], 8, LANES)], after=[rims[3]],
+        [traces, surface_map, surface_normals], [(surface_map.shape[0], 8, LANES)],
     )
     lists = lax.all_to_all(rows, ("gx", "gz"), split_axis=0, concat_axis=0, tiled=True)
     sent_four = call(
@@ -638,10 +638,6 @@
     (moved,) = call(
         advection_kernel, "advection", [(3, nx, nz, ny)],
         [air_state, wind_field, *rims], [ext], flops=10_000_000, after=[rows],
-    )
-    volume, token = call(
-        volume_kernel, "volume", [solid_state.shape, tile], [state, integral, jacobians, stiffness],
-        [(dims * pad, quants * width), (dims * pad, LANES)], flops=10_000_000, after=[rows],
     )
     pressure_x = (HEAD + RADIUS * nz, ny)
     pressure_z = (HEAD + nx * ZRIM, ny)
@@ -649,7 +645,7 @@
     both_z = (pressure_z[0] + sent[0], LANES)
     raw, xb, zb, xa, za = call(
         raw_pressure_kernel, "raw_pressure", [block, both_x, both_z, both_x, both_z],
-        [air_state, wind_field, air_medium, *rims, *sent_four], [ext], after=[moved, token],
+        [air_state, wind_field, air_medium, *rims, *sent_four], [ext], after=[moved],
     )
     both = exchange(xb, zb, xa, za)
     rim_x = (HEAD + 4 * RADIUS * nz, ny)
@@ -658,10 +654,10 @@
         functools.partial(injected_kernel, n_gx, n_gz), "injected",
         [air_state.shape, rim_x, rim_z, rim_x, rim_z, (1, LANES)],
         [air_state, wind_field, air_medium, raw, moved, *rims, *both, lists, surface_map],
-        [(3 * nx, 3 * nz, ny), wide, (3,) + wide], after=[token],
+        [(3 * nx, 3 * nz, ny), wide, (3,) + wide],
     )
     half = faces // 2
-    solid = volume
+    solid = state
     for substep in range(1, SUBSTEPS):
         rims = exchange(xb, zb, xa, za)
         solid, token = call(
@@ -682,7 +678,12 @@
             [air, wind_field, *rims], [ext], flops=10_000_000, after=[xa],
         )
         last = substep == SUBSTEPS - 1
-        if last:
+        if not last:
+            solid, token = call(
+                volume_kernel, "volume", [solid_state.shape, tile], [solid, integral, jacobians, stiffness],
+                [(dims * pad, quants * width), (dims * pad, LANES)], flops=10_000_000, after=[moved],
+            )
+        else:
             (solid,) = call(
                 replies_kernel, "replies", [solid_state.shape],
                 [solid, flux_solvers, lift_matrix, neighbours, surface_map, *replies],
@@ -690,7 +691,8 @@
             )
         outs = [air_state.shape] + ([] if last else [rim_x, rim_z, rim_x, rim_z])
         done = call(
-            velocity_kernel, "velocity", outs, [air, pressure, air_medium, moved, *rises], [wide]
+            velocity_kernel, "velocity", outs, [air, pressure, air_medium, moved, *rises], [wide],
+            after=[token],
         )
         air = done[0]
         if not last:

time: 82.2 us -> 84.6 us (1.029)
  local copies, waits for them, and re-layouts: 3.2 us -> 4.65 us
    unnamed x30 -> x34, local copies, waits for them, and re-layouts: 3.2 us -> 4.65 us
    ppermute x24, starting transfers between devices: 52.7 us -> 53.6 us  [swap(): return lax.ppermute(values, axis, pairs)]
where the time goes in v2:
time: 84.6 us; the launch traced here: 83.9 us
  starting transfers between devices  58.3 us (69%)
  Pallas kernels  17.7 us (21%)
  local copies, waits for them, and re-layouts  4.65 us (5%)
  waiting for transfers between devices  2.24 us (3%)
  between operations  1.04 us (1%)
    ppermute x24, starting transfers between devices, swap(): return lax.ppermute(values, axis, pairs)  53.6 us
    pallas_call x17, Pallas kernels, call(): pl.pallas_call(body, out_shape=[jax.ShapeDtypeStruct(s, F32) for s in out...  17.7 us
    all_to_all x1, starting transfers between devices, shards(): lax.all_to_all(rows, ('gx', 'gz'), split_axis=0, concat_axis=0, tiled=True)  4.72 us
    unnamed x34, local copies, waits for them, and re-layouts  4.65 us
    ppermute x24, waiting for transfers between devices, swap(): return lax.ppermute(values, axis, pairs)  2.24 us
  transfers between devices with their start and end apart: 25, of which 4 were waited for; matrix products, arithmetic and copies ran while one was open for 0% of the time, Pallas kernels for 16%

profile of v2, /device:TPU:0, one launch (start us, length us, event | category | flops | bytes accessed | tf_op | source)
XLA Modules:
  0.0 83.9 jit_solution(837285186670058095)
XLA Ops:
  0.6 0.9 %copy-done = f32[3,8,16,128]{3,2,1,0:T(8,128)S(1)} copy-done((f32[3,8,16,128]{3,2,1,0:T(8,128)S(1)}, f32[3,8,16,128]{3,2,1,0:T(8,128)}, u32[]{:S(2)}) %copy-start) | copy-done | bytes 196632
  1.6 0.9 %copy-done.3 = f32[4,8,16,128]{3,2,1,0:T(8,128)S(1)} copy-done((f32[4,8,16,128]{3,2,1,0:T(8,128)S(1)}, f32[4,8,16,128]{3,2,1,0:T(8,128)}, u32[]{:S(2)}) %copy-start.3) | copy-done | bytes 262168
  2.5 0.8 raw_rims.1
  4.0 5.8 %collective-permute-start.2 = (f32[7,4,16,128]{3,2,1,0:T(8,128)S(1)}, f32[7,4,16,128]{3,2,1,0:T(8,128)S(1)}, u32[]{:S(2)}, u32[]{:S(2)}) collective-permute-start(f32[7,4,16,128]{3,2,1,0:T(8,128)S(1)} %get-tuple-element.52), channel_id=1, source_target_pairs={{0,4},{4,0},{8,12},{12,8},{16,20},{20,16},{24,28},{28,24},{1,5},{5... | collective-permute-start | bytes 688136 | tf_op jit(solution)/shard_map/ppermute | solution.py:50
  9.8 0.9 %copy-done.7 = f32[9,20,256]{2,1,0:T(8,128)S(1)} copy-done((f32[9,20,256]{2,1,0:T(8,128)S(1)}, f32[9,20,256]{2,1,0:T(8,128)}, u32[]{:S(2)}) %copy-start.7) | copy-done | bytes 184344
  10.7 2.5 %predict.1 = (f32[32,2304]{1,0:T(8,128)S(1)}, f32[9,16,1024]{2,1,0:T(8,128)S(1)}, f32[9,20,256]{2,1,0:T(8,128)S(1)}) custom-call(f32[9,20,256]{2,1,0:T(8,128)S(1)} %copy-done.7, f32[9,9,3,256]{3,2,1,0:T(4,128)S(1)} %bitcast.11, f32[3,20,20]{2,1,0:T(8,128)S(1)} %copy-done.9, f32[10,4,20]{2,1,0:T(4,128)S(1)} %bitcast.20), custom_call_target="tpu_custom_call" | custom-call | flops 40000000 | bytes 1510208 | tf_op jit(solution)/shard_map/predict/pallas_call | solution.py:31
  13.3 1.6 %own_list.1 = (f32[9,16,128]{2,1,0:T(8,128)S(1)}, f32[256,128]{1,0:T(8,128)}) custom-call(f32[9,16,1024]{2,1,0:T(8,128)S(1)} %get-tuple-element.48.refs_0_.refs_1_, s32[5,3,8]{2,1,0:T(4,128)S(1)} %bitcast.17, f32[5,3,8]{2,1,0:T(4,128)S(1)} %bitcast.21), custom_call_target="tpu_custom_call" | custom-call | flops 1000000 | bytes 795584 | tf_op jit(solution)/shard_map/own_list/pallas_call | solution.py:31
  14.9 4.7 %all-to-all-start = ((f32[32,8,128]{2,1,0:T(8,128)}), f32[32,8,128]{2,1,0:T(8,128)S(1)}, u32[]{:S(2)}, u32[]{:S(2)}) async-start(f32[32,8,128]{2,1,0:T(8,128)} %bitcast.6), calls=%async_computation | async-start | bytes 262144 | tf_op jit(solution)/shard_map/all_to_all | solution.py:633
  19.6 0.7 collective-permute-start.1
  20.3 3.2 %collective-permute-start.3 = (f32[7,8,4,128]{3,2,1,0:T(4,128)S(1)}, f32[7,8,4,128]{3,2,1,0:T(4,128)S(1)}, u32[]{:S(2)}, u32[]{:S(2)}) collective-permute-start(f32[7,8,4,128]{3,2,1,0:T(4,128)S(1)} %get-tuple-element.53), channel_id=1, source_target_pairs={{0,1},{1,0},{2,3},{3,2},{4,5},{5,4},{6,7},{7,6},{8,9},{9,8},{10,11... | collective-permute-start | bytes 344072 | tf_op jit(solution)/shard_map/ppermute | solution.py:50
  23.5 1.4 %outgoing.1 = (f32[96,128]{1,0:T(8,128)S(1)}, f32[96,128]{1,0:T(8,128)S(1)}, f32[96,128]{1,0:T(8,128)S(1)}, f32[96,128]{1,0:T(8,128)S(1)}) custom-call(f32[9,16,1024]{2,1,0:T(8,128)S(1)} %get-tuple-element.48.refs_0_.refs_1_, s32[4,128]{1,0:T(4,128)S(1)} %copy-done.16, f32[256,128]{1,0:T(8,128)} %get-tuple-element.54.refs_2_.refs_6_), custom_call_target="tpu_custom_call" | custom-call | flops 10000000 | bytes 788480 | tf_op jit(solution)/shard_map/outgoing/pallas_call | solution.py:31
  25.9 1.1 %raw_pressure.1 = (f32[1,8,16,128]{3,2,1,0:T(8,128)S(1)}, f32[168,128]{1,0:T(8,128)}, f32[168,128]{1,0:T(8,128)}, f32[168,128]{1,0:T(8,128)}, f32[168,128]{1,0:T(8,128)}) custom-call(f32[4,8,16,128]{3,2,1,0:T(8,128)S(1)} %copy-done.4, f32[3,8,16,128]{3,2,1,0:T(8,128)S(1)} %copy-done.1, f32[2,8,16,128]{3,2,1,0:T(8,128)S(1)} %copy-done.2, ...), custom_call_target="tpu_custom_call" | custom-call | flops 1000000 | bytes 1884160 | tf_op jit(solution)/shard_map/raw_pressure/pallas_call | solution.py:31
  28.9 4.2 %collective-permute-start.6 = (f32[168,128]{1,0:T(8,128)}, f32[168,128]{1,0:T(8,128)S(1)}, u32[]{:S(2)}, u32[]{:S(2)}) collective-permute-start(f32[168,128]{1,0:T(8,128)} %get-tuple-element.61), channel_id=1, source_target_pairs={{0,4},{4,0},{8,12},{12,8},{16,20},{20,16},{24,28},{28,24},{1,5},{5... | collective-permute-start | bytes 258056 | tf_op jit(solution)/shard_map/ppermute | solution.py:50
  33.2 3.6 %collective-permute-start.7 = (f32[168,128]{1,0:T(8,128)}, f32[168,128]{1,0:T(8,128)S(1)}, u32[]{:S(2)}, u32[]{:S(2)}) collective-permute-start(f32[168,128]{1,0:T(8,128)} %get-tuple-element.62), channel_id=1, source_target_pairs={{0,1},{1,0},{2,3},{3,2},{4,5},{5,4},{6,7},{7,6},{8,9},{9,8},{10,11... | collective-permute-start | bytes 258056 | tf_op jit(solution)/shard_map/ppermute | solution.py:50
  36.7 1.1 %collective-permute-done.7.refs_12_.refs_9_ = f32[168,128]{1,0:T(8,128)S(1)} collective-permute-done((f32[168,128]{1,0:T(8,128)}, f32[168,128]{1,0:T(8,128)S(1)}, u32[]{:S(2)}, u32[]{:S(2)}) %collective-permute-start.7) | collective-permute-done | bytes 86048 | tf_op jit(solution)/shard_map/ppermute | solution.py:50
  37.9 0.8 copy-done.12
  38.7 1.1 %injected.1 = (f32[4,8,16,128]{3,2,1,0:T(8,128)S(1)}, f32[264,128]{1,0:T(8,128)S(1)}, f32[4,8,4,128]{3,2,1,0:T(4,128)S(1)}, f32[264,128]{1,0:T(8,128)S(1)}, f32[...) custom-call(f32[4,8,16,128]{3,2,1,0:T(8,128)S(1)} %copy-done.4, f32[3,8,16,128]{3,2,1,0:T(8,128)S(1)} %copy-done.1, ...), custom_call_target="tpu_custom_call" | custom-call | flops 1000000 | bytes 2679776 | tf_op jit(solution)/shard_map/injected/pallas_call | solution.py:31
  39.8 0.7 collective-permute-start.8
  40.4 4.1 %collective-permute-start.10 = (f32[264,128]{1,0:T(8,128)S(1)}, f32[264,128]{1,0:T(8,128)S(1)}, u32[]{:S(2)}, u32[]{:S(2)}) collective-permute-start(f32[264,128]{1,0:T(8,128)S(1)} %get-tuple-element.64.refs_10_), channel_id=1, source_target_pairs={{0,4},{4,0},{8,12},{12,8},{16,20},{20,16},{24,28},{28,24},{1,5},{5... | collective-permute-start | bytes 405512 | tf_op jit(solution)/shard_map/ppermute | solution.py:50
  45.3 4.4 %collective-permute-start.11 = (f32[4,8,4,128]{3,2,1,0:T(4,128)S(1)}, f32[4,8,4,128]{3,2,1,0:T(4,128)S(1)}, u32[]{:S(2)}, u32[]{:S(2)}) collective-permute-start(f32[4,8,4,128]{3,2,1,0:T(4,128)S(1)} %get-tuple-element.70), channel_id=1, source_target_pairs={{0,1},{1,0},{2,3},{3,2},{4,5},{5,4},{6,7},{7,6},{8,9},{9,8},{10,11... | collective-permute-start | bytes 196616 | tf_op jit(solution)/shard_map/ppermute | solution.py:50
  49.7 1.8 %flux.2 = (f32[9,20,256]{2,1,0:T(8,128)S(1)}, f32[8,128]{1,0:T(8,128)S(1)}) custom-call(f32[9,20,256]{2,1,0:T(8,128)S(1)} %get-tuple-element.47.refs_0_, f32[9,16,1024]{2,1,0:T(8,128)S(1)} %get-tuple-element.48.refs_0_.refs_1_, f32[9,16,128]{2,1,0:T(8,128)S(1)} %get-tuple-element.49.refs_2_, f32[9,9,4,256]{3,2,1,0:T(4,128)S(1)} %bitcast.8, ...), custom_call_target="tpu_custom_call" | custom-call | flops 20000000 | bytes 1719424 | tf_op jit(solution)/shard_map/flux/pallas_call | solution.py:31
  53.2 3.1 %collective-permute-start.15 = (f32[72,128]{1,0:T(8,128)S(1)}, f32[72,128]{1,0:T(8,128)S(1)}, u32[]{:S(2)}, u32[]{:S(2)}) collective-permute-start(f32[72,128]{1,0:T(8,128)S(1)} %get-tuple-element.78), channel_id=1, source_target_pairs={{0,1},{1,0},{2,3},{3,2},{4,5},{5,4},{6,7},{7,6},{8,9},{9,8},{10,11... | collective-permute-start | bytes 110600 | tf_op jit(solution)/shard_map/ppermute | solution.py:50
  56.3 3.6 %collective-permute-start.14 = (f32[72,128]{1,0:T(8,128)S(1)}, f32[72,128]{1,0:T(8,128)S(1)}, u32[]{:S(2)}, u32[]{:S(2)}) collective-permute-start(f32[72,128]{1,0:T(8,128)S(1)} %get-tuple-element.73.refs_6_), channel_id=1, source_target_pairs={{0,4},{4,0},{8,12},{12,8},{16,20},{20,16},{24,28},{28,24},{1,5},{5... | collective-permute-start | bytes 110600 | tf_op jit(solution)/shard_map/ppermute | solution.py:50
  60.4 1.1 %volume.1 = (f32[9,20,256]{2,1,0:T(8,128)S(1)}, f32[8,128]{1,0:T(8,128)S(1)}) custom-call(f32[9,20,256]{2,1,0:T(8,128)S(1)} %get-tuple-element.65.refs_0_, f32[32,2304]{1,0:T(8,128)S(1)} %get-tuple-element.66.refs_1_, f32[9,9,3,256]{3,2,1,0:T(4,128)S(1)} %bitcast.12, f32[3,20,20]{2,1,0:T(8,128)S(1)} %copy-done.9, f32[3,8,16,128]{3,2,1,0:T(8,128)S(1)} %advection.4.refs_4_.refs_3_), custom_call_target="tpu_custom_call" | custom-call | flops 10000000 | bytes 921280 | tf_op jit(solution)/shard_map/volume/pallas_call | solution.py:31
  62.2 0.7 collective-permute-start.16
  62.9 4.1 %collective-permute-start.18 = (f32[264,128]{1,0:T(8,128)S(1)}, f32[264,128]{1,0:T(8,128)S(1)}, u32[]{:S(2)}, u32[]{:S(2)}) collective-permute-start(f32[264,128]{1,0:T(8,128)S(1)} %get-tuple-element.80.refs_10_), channel_id=1, source_target_pairs={{0,4},{4,0},{8,12},{12,8},{16,20},{20,16},{24,28},{28,24},{1,5},{5... | collective-permute-start | bytes 405512 | tf_op jit(solution)/shard_map/ppermute | solution.py:50
  67.6 2.1 %collective-permute-start.19 = (f32[4,8,4,128]{3,2,1,0:T(4,128)S(1)}, f32[4,8,4,128]{3,2,1,0:T(4,128)S(1)}, u32[]{:S(2)}, u32[]{:S(2)}) collective-permute-start(f32[4,8,4,128]{3,2,1,0:T(4,128)S(1)} %get-tuple-element.85), channel_id=1, source_target_pairs={{0,1},{1,0},{2,3},{3,2},{4,5},{5,4},{6,7},{7,6},{8,9},{9,8},{10,11... | collective-permute-start | bytes 196616 | tf_op jit(solution)/shard_map/ppermute | solution.py:50
  69.7 1.8 %flux.3 = (f32[9,20,256]{2,1,0:T(8,128)S(1)}, f32[8,128]{1,0:T(8,128)S(1)}) custom-call(f32[9,20,256]{2,1,0:T(8,128)S(1)} %get-tuple-element.74.refs_0_, f32[9,16,1024]{2,1,0:T(8,128)S(1)} %get-tuple-element.48.refs_0_.refs_1_, f32[9,16,128]{2,1,0:T(8,128)S(1)} %get-tuple-element.49.refs_2_, f32[9,9,4,256]{3,2,1,0:T(4,128)S(1)} %bitcast.9, ...), custom_call_target="tpu_custom_call" | custom-call | flops 20000000 | bytes 1719424 | tf_op jit(solution)/shard_map/flux/pallas_call | solution.py:31
  73.5 2.8 %collective-permute-start.23 = (f32[72,128]{1,0:T(8,128)S(1)}, f32[72,128]{1,0:T(8,128)S(1)}, u32[]{:S(2)}, u32[]{:S(2)}) collective-permute-start(f32[72,128]{1,0:T(8,128)S(1)} %get-tuple-element.91), channel_id=1, source_target_pairs={{0,1},{1,0},{2,3},{3,2},{4,5},{5,4},{6,7},{7,6},{8,9},{9,8},{10,11... | collective-permute-start | bytes 110600 | tf_op jit(solution)/shard_map/ppermute | solution.py:50
  76.3 4.7 %collective-permute-start.22 = (f32[72,128]{1,0:T(8,128)S(1)}, f32[72,128]{1,0:T(8,128)S(1)}, u32[]{:S(2)}, u32[]{:S(2)}) collective-permute-start(f32[72,128]{1,0:T(8,128)S(1)} %get-tuple-element.87.refs_6_), channel_id=1, source_target_pairs={{0,4},{4,0},{8,12},{12,8},{16,20},{20,16},{24,28},{28,24},{1,5},{5... | collective-permute-start | bytes 110600 | tf_op jit(solution)/shard_map/ppermute | solution.py:50
  81.6 0.9 %replies.1 = f32[9,20,256]{2,1,0:T(8,128)} custom-call(f32[9,20,256]{2,1,0:T(8,128)S(1)} %get-tuple-element.81.refs_0_, f32[9,9,4,256]{3,2,1,0:T(4,128)S(1)} %bitcast.10, f32[10,4,20]{2,1,0:T(4,128)S(1)} %bitcast.16, s32[4,256]{1,0:T(4,128)S(1)} %copy-done.13, s32[5,3,8]{2,1,0:T(4,128)S(1)} %bitcast.19, f32[1,128]{1,0:T(1,128)S(1)} %get-tuple-element.71.refs_7_.refs_5_, ...), custom_call_target="tpu_custom_call" | custom-call | flops 1000000 | bytes 782432 | tf_op jit(solution)/shard_map/replies/pallas_call | solution.py:31
  83.0 1.0 %velocity.3 = f32[4,8,16,128]{3,2,1,0:T(8,128)} custom-call(f32[4,8,16,128]{3,2,1,0:T(8,128)S(1)} %get-tuple-element.82.refs_0_, f32[1,8,16,128]{3,2,1,0:T(8,128)S(1)} %get-tuple-element.88.refs_1_, f32[2,8,16,128]{3,2,1,0:T(8,128)S(1)} %copy-done.2, f32[3,8,16,128]{3,2,1,0:T(8,128)S(1)} %advection.5.refs_8_.refs_3_, ...), custom_call_target="tpu_custom_call" | custom-call | flops 1000000 | bytes 1064960 | tf_op jit(solution)/shard_map/velocity/pallas_call | solution.py:31
  (69 shorter events, 10.7 us)
Async XLA Ops:
  2.5 7.3 %copy-start.6 = (f32[3,9,9,256]{3,0,2,1:T(4,128)S(1)}, f32[3,9,9,256]{3,0,2,1:T(4,128)}, u32[]{:S(2)}) copy-start(f32[3,9,9,256]{3,0,2,1:T(4,128)} %param.14) | copy-start | bytes 746500
  2.5 7.3 %copy-start.9 = (f32[3,20,20]{2,1,0:T(8,128)S(1)}, f32[3,20,20]{2,1,0:T(8,128)}, u32[]{:S(2)}) copy-start(f32[3,20,20]{2,1,0:T(8,128)} %refs_3_.2) | copy-start | bytes 14404
  2.5 7.3 %copy-start.14 = (f32[4,10,20]{2,0,1:T(4,128)S(1)}, f32[4,10,20]{2,0,1:T(4,128)}, u32[]{:S(2)}) copy-start(f32[4,10,20]{2,0,1:T(4,128)} %param.17) | copy-start | bytes 9604
  3.3 21.7 %collective-permute-start = (f32[7,4,16,128]{3,2,1,0:T(8,128)}, f32[7,4,16,128]{3,2,1,0:T(8,128)S(1)}, u32[]{:S(2)}, u32[]{:S(2)}) collective-permute-start(f32[7,4,16,128]{3,2,1,0:T(8,128)} %get-tuple-element.50), channel_id=1, source_target_pairs={{4,8},{8,4},{12,16},{16,12},{20,24},{24,20},{5,9},{9,5},{13,17},{1... | collective-permute-start | bytes 688136 | tf_op jit(solution)/shard_map/ppermute | solution.py:50
  4.0 21.0 %collective-permute-start.2 = (f32[7,4,16,128]{3,2,1,0:T(8,128)S(1)}, f32[7,4,16,128]{3,2,1,0:T(8,128)S(1)}, u32[]{:S(2)}, u32[]{:S(2)}) collective-permute-start(f32[7,4,16,128]{3,2,1,0:T(8,128)S(1)} %get-tuple-element.52), channel_id=1, source_target_pairs={{0,4},{4,0},{8,12},{12,8},{16,20},{20,16},{24,28},{28,24},{1,5},{5... | collective-permute-start | bytes 688136 | tf_op jit(solution)/shard_map/ppermute | solution.py:50
  14.9 21.8 %all-to-all-start = ((f32[32,8,128]{2,1,0:T(8,128)}), f32[32,8,128]{2,1,0:T(8,128)S(1)}, u32[]{:S(2)}, u32[]{:S(2)}) async-start(f32[32,8,128]{2,1,0:T(8,128)} %bitcast.6), calls=%async_computation | async-start | bytes 262144 | tf_op jit(solution)/shard_map/all_to_all | solution.py:633
  19.6 5.4 %collective-permute-start.1 = (f32[7,8,4,128]{3,2,1,0:T(4,128)}, f32[7,8,4,128]{3,2,1,0:T(4,128)S(1)}, u32[]{:S(2)}, u32[]{:S(2)}) collective-permute-start(f32[7,8,4,128]{3,2,1,0:T(4,128)} %get-tuple-element.51), channel_id=1, source_target_pairs={{1,2},{2,1},{5,6},{6,5},{9,10},{10,9},{13,14},{14,13},{17,18},{18,... | collective-permute-start | bytes 344072 | tf_op jit(solution)/shard_map/ppermute | solution.py:50
  20.3 4.7 %copy-start.1 = (f32[3,8,16,128]{3,2,1,0:T(8,128)S(1)}, f32[3,8,16,128]{3,2,1,0:T(8,128)}, u32[]{:S(2)}) copy-start(f32[3,8,16,128]{3,2,1,0:T(8,128)} %refs_1_.17) | copy-start | bytes 589828
  20.3 4.7 %copy-start.4 = (f32[4,8,16,128]{3,2,1,0:T(8,128)S(1)}, f32[4,8,16,128]{3,2,1,0:T(8,128)}, u32[]{:S(2)}) copy-start(f32[4,8,16,128]{3,2,1,0:T(8,128)} %refs_0_.9) | copy-start | bytes 786436
  20.3 4.7 %collective-permute-start.3 = (f32[7,8,4,128]{3,2,1,0:T(4,128)S(1)}, f32[7,8,4,128]{3,2,1,0:T(4,128)S(1)}, u32[]{:S(2)}, u32[]{:S(2)}) collective-permute-start(f32[7,8,4,128]{3,2,1,0:T(4,128)S(1)} %get-tuple-element.53), channel_id=1, source_target_pairs={{0,1},{1,0},{2,3},{3,2},{4,5},{5,4},{6,7},{7,6},{8,9},{9,8},{10,11... | collective-permute-start | bytes 344072 | tf_op jit(solution)/shard_map/ppermute | solution.py:50
  27.6 9.1 %collective-permute-start.4 = (f32[168,128]{1,0:T(8,128)}, f32[168,128]{1,0:T(8,128)S(1)}, u32[]{:S(2)}, u32[]{:S(2)}) collective-permute-start(f32[168,128]{1,0:T(8,128)} %get-tuple-element.59), channel_id=1, source_target_pairs={{4,8},{8,4},{12,16},{16,12},{20,24},{24,20},{5,9},{9,5},{13,17},{1... | collective-permute-start | bytes 258056 | tf_op jit(solution)/shard_map/ppermute | solution.py:50
  28.3 8.5 %collective-permute-start.5 = (f32[168,128]{1,0:T(8,128)}, f32[168,128]{1,0:T(8,128)S(1)}, u32[]{:S(2)}, u32[]{:S(2)}) collective-permute-start(f32[168,128]{1,0:T(8,128)} %get-tuple-element.60), channel_id=1, source_target_pairs={{1,2},{2,1},{5,6},{6,5},{9,10},{10,9},{13,14},{14,13},{17,18},{18,... | collective-permute-start | bytes 258056 | tf_op jit(solution)/shard_map/ppermute | solution.py:50
  28.9 7.8 %collective-permute-start.6 = (f32[168,128]{1,0:T(8,128)}, f32[168,128]{1,0:T(8,128)S(1)}, u32[]{:S(2)}, u32[]{:S(2)}) collective-permute-start(f32[168,128]{1,0:T(8,128)} %get-tuple-element.61), channel_id=1, source_target_pairs={{0,4},{4,0},{8,12},{12,8},{16,20},{20,16},{24,28},{28,24},{1,5},{5... | collective-permute-start | bytes 258056 | tf_op jit(solution)/shard_map/ppermute | solution.py:50
  33.2 4.7 %collective-permute-start.7 = (f32[168,128]{1,0:T(8,128)}, f32[168,128]{1,0:T(8,128)S(1)}, u32[]{:S(2)}, u32[]{:S(2)}) collective-permute-start(f32[168,128]{1,0:T(8,128)} %get-tuple-element.62), channel_id=1, source_target_pairs={{0,1},{1,0},{2,3},{3,2},{4,5},{5,4},{6,7},{7,6},{8,9},{9,8},{10,11... | collective-permute-start | bytes 258056 | tf_op jit(solution)/shard_map/ppermute | solution.py:50
  38.7 11.0 %copy-start.5 = (f32[4,9,9,256]{3,0,2,1:T(4,128)S(1)}, f32[4,9,9,256]{3,0,2,1:T(4,128)}, u32[]{:S(2)}) copy-start(f32[4,9,9,256]{3,0,2,1:T(4,128)} %param.15) | copy-start | bytes 995332
  38.7 11.0 %copy-start.8 = (f32[4,20,10]{1,0,2:T(4,128)S(1)}, f32[4,20,10]{1,0,2:T(4,128)}, u32[]{:S(2)}) copy-start(f32[4,20,10]{1,0,2:T(4,128)} %param.18) | copy-start | bytes 9604
  39.8 11.7 %collective-permute-start.8 = (f32[264,128]{1,0:T(8,128)S(1)}, f32[264,128]{1,0:T(8,128)S(1)}, u32[]{:S(2)}, u32[]{:S(2)}) collective-permute-start(f32[264,128]{1,0:T(8,128)S(1)} %get-tuple-element.68), channel_id=1, source_target_pairs={{4,8},{8,4},{12,16},{16,12},{20,24},{24,20},{5,9},{9,5},{13,17},{1... | collective-permute-start | bytes 405512 | tf_op jit(solution)/shard_map/ppermute | solution.py:50
  40.4 11.1 %collective-permute-start.10 = (f32[264,128]{1,0:T(8,128)S(1)}, f32[264,128]{1,0:T(8,128)S(1)}, u32[]{:S(2)}, u32[]{:S(2)}) collective-permute-start(f32[264,128]{1,0:T(8,128)S(1)} %get-tuple-element.64.refs_10_), channel_id=1, source_target_pairs={{0,4},{4,0},{8,12},{12,8},{16,20},{20,16},{24,28},{28,24},{1,5},{5... | collective-permute-start | bytes 405512 | tf_op jit(solution)/shard_map/ppermute | solution.py:50
  44.6 6.9 %collective-permute-start.9 = (f32[4,8,4,128]{3,2,1,0:T(4,128)S(1)}, f32[4,8,4,128]{3,2,1,0:T(4,128)S(1)}, u32[]{:S(2)}, u32[]{:S(2)}) collective-permute-start(f32[4,8,4,128]{3,2,1,0:T(4,128)S(1)} %get-tuple-element.69), channel_id=1, source_target_pairs={{1,2},{2,1},{5,6},{6,5},{9,10},{10,9},{13,14},{14,13},{17,18},{18,... | collective-permute-start | bytes 196616 | tf_op jit(solution)/shard_map/ppermute | solution.py:50
  45.3 6.2 %collective-permute-start.11 = (f32[4,8,4,128]{3,2,1,0:T(4,128)S(1)}, f32[4,8,4,128]{3,2,1,0:T(4,128)S(1)}, u32[]{:S(2)}, u32[]{:S(2)}) collective-permute-start(f32[4,8,4,128]{3,2,1,0:T(4,128)S(1)} %get-tuple-element.70), channel_id=1, source_target_pairs={{0,1},{1,0},{2,3},{3,2},{4,5},{5,4},{6,7},{7,6},{8,9},{9,8},{10,11... | collective-permute-start | bytes 196616 | tf_op jit(solution)/shard_map/ppermute | solution.py:50
  51.9 9.7 %collective-permute-start.12 = (f32[72,128]{1,0:T(8,128)S(1)}, f32[72,128]{1,0:T(8,128)S(1)}, u32[]{:S(2)}, u32[]{:S(2)}) collective-permute-start(f32[72,128]{1,0:T(8,128)S(1)} %get-tuple-element.76), channel_id=1, source_target_pairs={{4,8},{8,4},{12,16},{16,12},{20,24},{24,20},{5,9},{9,5},{13,17},{1... | collective-permute-start | bytes 110600 | tf_op jit(solution)/shard_map/ppermute | solution.py:50
  52.6 9.0 %collective-permute-start.13 = (f32[72,128]{1,0:T(8,128)S(1)}, f32[72,128]{1,0:T(8,128)S(1)}, u32[]{:S(2)}, u32[]{:S(2)}) collective-permute-start(f32[72,128]{1,0:T(8,128)S(1)} %get-tuple-element.77), channel_id=1, source_target_pairs={{1,2},{2,1},{5,6},{6,5},{9,10},{10,9},{13,14},{14,13},{17,18},{18,... | collective-permute-start | bytes 110600 | tf_op jit(solution)/shard_map/ppermute | solution.py:50
  53.2 8.3 %collective-permute-start.15 = (f32[72,128]{1,0:T(8,128)S(1)}, f32[72,128]{1,0:T(8,128)S(1)}, u32[]{:S(2)}, u32[]{:S(2)}) collective-permute-start(f32[72,128]{1,0:T(8,128)S(1)} %get-tuple-element.78), channel_id=1, source_target_pairs={{0,1},{1,0},{2,3},{3,2},{4,5},{5,4},{6,7},{7,6},{8,9},{9,8},{10,11... | collective-permute-start | bytes 110600 | tf_op jit(solution)/shard_map/ppermute | solution.py:50
  56.3 5.6 %collective-permute-start.14 = (f32[72,128]{1,0:T(8,128)S(1)}, f32[72,128]{1,0:T(8,128)S(1)}, u32[]{:S(2)}, u32[]{:S(2)}) collective-permute-start(f32[72,128]{1,0:T(8,128)S(1)} %get-tuple-element.73.refs_6_), channel_id=1, source_target_pairs={{0,4},{4,0},{8,12},{12,8},{16,20},{20,16},{24,28},{28,24},{1,5},{5... | collective-permute-start | bytes 110600 | tf_op jit(solution)/shard_map/ppermute | solution.py:50
  62.2 9.4 %collective-permute-start.16 = (f32[264,128]{1,0:T(8,128)S(1)}, f32[264,128]{1,0:T(8,128)S(1)}, u32[]{:S(2)}, u32[]{:S(2)}) collective-permute-start(f32[264,128]{1,0:T(8,128)S(1)} %get-tuple-element.83), channel_id=1, source_target_pairs={{4,8},{8,4},{12,16},{16,12},{20,24},{24,20},{5,9},{9,5},{13,17},{1... | collective-permute-start | bytes 405512 | tf_op jit(solution)/shard_map/ppermute | solution.py:50
  62.9 9.0 %collective-permute-start.18 = (f32[264,128]{1,0:T(8,128)S(1)}, f32[264,128]{1,0:T(8,128)S(1)}, u32[]{:S(2)}, u32[]{:S(2)}) collective-permute-start(f32[264,128]{1,0:T(8,128)S(1)} %get-tuple-element.80.refs_10_), channel_id=1, source_target_pairs={{0,4},{4,0},{8,12},{12,8},{16,20},{20,16},{24,28},{28,24},{1,5},{5... | collective-permute-start | bytes 405512 | tf_op jit(solution)/shard_map/ppermute | solution.py:50
  67.0 4.5 %collective-permute-start.17 = (f32[4,8,4,128]{3,2,1,0:T(4,128)S(1)}, f32[4,8,4,128]{3,2,1,0:T(4,128)S(1)}, u32[]{:S(2)}, u32[]{:S(2)}) collective-permute-start(f32[4,8,4,128]{3,2,1,0:T(4,128)S(1)} %get-tuple-element.84), channel_id=1, source_target_pairs={{1,2},{2,1},{5,6},{6,5},{9,10},{10,9},{13,14},{14,13},{17,18},{18,... | collective-permute-start | bytes 196616 | tf_op jit(solution)/shard_map/ppermute | solution.py:50
  67.6 3.9 %collective-permute-start.19 = (f32[4,8,4,128]{3,2,1,0:T(4,128)S(1)}, f32[4,8,4,128]{3,2,1,0:T(4,128)S(1)}, u32[]{:S(2)}, u32[]{:S(2)}) collective-permute-start(f32[4,8,4,128]{3,2,1,0:T(4,128)S(1)} %get-tuple-element.85), channel_id=1, source_target_pairs={{0,1},{1,0},{2,3},{3,2},{4,5},{5,4},{6,7},{7,6},{8,9},{9,8},{10,11... | collective-permute-start | bytes 196616 | tf_op jit(solution)/shard_map/ppermute | solution.py:50
  72.2 10.3 %collective-permute-start.20 = (f32[72,128]{1,0:T(8,128)S(1)}, f32[72,128]{1,0:T(8,128)S(1)}, u32[]{:S(2)}, u32[]{:S(2)}) collective-permute-start(f32[72,128]{1,0:T(8,128)S(1)} %get-tuple-element.89), channel_id=1, source_target_pairs={{4,8},{8,4},{12,16},{16,12},{20,24},{24,20},{5,9},{9,5},{13,17},{1... | collective-permute-start | bytes 110600 | tf_op jit(solution)/shard_map/ppermute | solution.py:50
  72.9 9.6 %collective-permute-start.21 = (f32[72,128]{1,0:T(8,128)S(1)}, f32[72,128]{1,0:T(8,128)S(1)}, u32[]{:S(2)}, u32[]{:S(2)}) collective-permute-start(f32[72,128]{1,0:T(8,128)S(1)} %get-tuple-element.90), channel_id=1, source_target_pairs={{1,2},{2,1},{5,6},{6,5},{9,10},{10,9},{13,14},{14,13},{17,18},{18,... | collective-permute-start | bytes 110600 | tf_op jit(solution)/shard_map/ppermute | solution.py:50
  73.5 8.9 %collective-permute-start.23 = (f32[72,128]{1,0:T(8,128)S(1)}, f32[72,128]{1,0:T(8,128)S(1)}, u32[]{:S(2)}, u32[]{:S(2)}) collective-permute-start(f32[72,128]{1,0:T(8,128)S(1)} %get-tuple-element.91), channel_id=1, source_target_pairs={{0,1},{1,0},{2,3},{3,2},{4,5},{5,4},{6,7},{7,6},{8,9},{9,8},{10,11... | collective-permute-start | bytes 110600 | tf_op jit(solution)/shard_map/ppermute | solution.py:50
  76.3 6.6 %collective-permute-start.22 = (f32[72,128]{1,0:T(8,128)S(1)}, f32[72,128]{1,0:T(8,128)S(1)}, u32[]{:S(2)}, u32[]{:S(2)}) collective-permute-start(f32[72,128]{1,0:T(8,128)S(1)} %get-tuple-element.87.refs_6_), channel_id=1, source_target_pairs={{0,4},{4,0},{8,12},{12,8},{16,20},{20,16},{24,28},{28,24},{1,5},{5... | collective-permute-start | bytes 110600 | tf_op jit(solution)/shard_map/ppermute | solution.py:50
  (10 other events, 18.6 us)

commit v3 on v2

--- a/solution.py
+++ b/solution.py
@@ -629,6 +629,7 @@
     own, rows = call(
         own_list_kernel, "own_list", [(quants, 16, LANES), (n_gx * n_gz * 8, LANES)],
         [traces, surface_map, surface_normals], [(surface_map.shape[0], 8, LANES)],
+        after=[rims[1], rims[3]],
     )
     lists = lax.all_to_all(rows, ("gx", "gz"), split_axis=0, concat_axis=0, tiled=True)
     sent_four = call(

time: 84.6 us -> 82.1 us (0.970)
  starting transfers between devices: 58.3 us -> 57 us
    all_to_all x1, starting transfers between devices: 4.72 us -> 3.8 us  [shards(): lax.all_to_all(rows, ('gx', 'gz'), split_axis=0, concat_axis=0, tiled=True)]
  transfers between devices with their start and end apart: 25 -> 25, of which waited for: 4 -> 3; matrix products, arithmetic and copies ran while one was open for 0% -> 0% of each run, Pallas kernels for 16% -> 16%
where the time goes in v3:
time: 82.1 us; the launch traced here: 81.5 us
  starting transfers between devices  57 us (69%)
  Pallas kernels  17 us (21%)
  local copies, waits for them, and re-layouts  4.68 us (6%)
  waiting for transfers between devices  1.77 us (2%)
  between operations  1.04 us (1%)
    ppermute x24, starting transfers between devices, swap(): return lax.ppermute(values, axis, pairs)  53.2 us
    pallas_call x17, Pallas kernels, call(): pl.pallas_call(body, out_shape=[jax.ShapeDtypeStruct(s, F32) for s in out...  17 us
    unnamed x34, local copies, waits for them, and re-layouts  4.68 us
    all_to_all x1, starting transfers between devices, shards(): lax.all_to_all(rows, ('gx', 'gz'), split_axis=0, concat_axis=0, tiled=True)  3.8 us
    ppermute x24, waiting for transfers between devices, swap(): return lax.ppermute(values, axis, pairs)  1.77 us
  transfers between devices with their start and end apart: 25, of which 3 were waited for; matrix products, arithmetic and copies ran while one was open for 0% of the time, Pallas kernels for 16%

profile of v3, /device:TPU:0, one launch (start us, length us, event | category | flops | bytes accessed | tf_op | source)
XLA Modules:
  0.0 81.5 jit_solution(14755281115742764633)
XLA Ops:
  0.6 0.9 %copy-done = f32[3,8,16,128]{3,2,1,0:T(8,128)S(1)} copy-done((f32[3,8,16,128]{3,2,1,0:T(8,128)S(1)}, f32[3,8,16,128]{3,2,1,0:T(8,128)}, u32[]{:S(2)}) %copy-start) | copy-done | bytes 196632
  1.6 0.9 %copy-done.3 = f32[4,8,16,128]{3,2,1,0:T(8,128)S(1)} copy-done((f32[4,8,16,128]{3,2,1,0:T(8,128)S(1)}, f32[4,8,16,128]{3,2,1,0:T(8,128)}, u32[]{:S(2)}) %copy-start.3) | copy-done | bytes 262168
  2.5 0.8 %raw_rims.1 = (f32[7,4,16,128]{3,2,1,0:T(8,128)}, f32[7,8,4,128]{3,2,1,0:T(4,128)S(1)}, f32[7,4,16,128]{3,2,1,0:T(8,128)}, f32[7,8,4,128]{3,2,1,0:T(4,128)S(1)}) custom-call(f32[4,8,16,128]{3,2,1,0:T(8,128)S(1)} %copy-done.3, f32[3,8,16,128]{3,2,1,0:T(8,128)S(1)} %copy-done), custom_call_target="tpu_custom_call" | custom-call | flops 1000000 | bytes 1146880 | tf_op jit(solution)/shard_map/raw_rims/pallas_call | solution.py:31
  4.0 4.4 %collective-permute-start.1 = (f32[7,8,4,128]{3,2,1,0:T(4,128)S(1)}, f32[7,8,4,128]{3,2,1,0:T(4,128)S(1)}, u32[]{:S(2)}, u32[]{:S(2)}) collective-permute-start(f32[7,8,4,128]{3,2,1,0:T(4,128)S(1)} %get-tuple-element.50), channel_id=1, source_target_pairs={{0,1},{1,0},{2,3},{3,2},{4,5},{5,4},{6,7},{7,6},{8,9},{9,8},{10,11... | collective-permute-start | bytes 344072 | tf_op jit(solution)/shard_map/ppermute | solution.py:50
  9.0 4.3 %collective-permute-start.3 = (f32[7,4,16,128]{3,2,1,0:T(8,128)}, f32[7,4,16,128]{3,2,1,0:T(8,128)S(1)}, u32[]{:S(2)}, u32[]{:S(2)}) collective-permute-start(f32[7,4,16,128]{3,2,1,0:T(8,128)} %get-tuple-element.53), channel_id=1, source_target_pairs={{0,4},{4,0},{8,12},{12,8},{16,20},{20,16},{24,28},{28,24},{1,5},{5... | collective-permute-start | bytes 688136 | tf_op jit(solution)/shard_map/ppermute | solution.py:50
  13.4 0.9 %copy-done.7 = f32[9,20,256]{2,1,0:T(8,128)S(1)} copy-done((f32[9,20,256]{2,1,0:T(8,128)S(1)}, f32[9,20,256]{2,1,0:T(8,128)}, u32[]{:S(2)}) %copy-start.7) | copy-done | bytes 184344
  14.3 2.5 %predict.1 = (f32[32,2304]{1,0:T(8,128)S(1)}, f32[9,16,1024]{2,1,0:T(8,128)S(1)}, f32[9,20,256]{2,1,0:T(8,128)S(1)}) custom-call(f32[9,20,256]{2,1,0:T(8,128)S(1)} %copy-done.7, f32[9,9,3,256]{3,2,1,0:T(4,128)S(1)} %bitcast.11, f32[3,20,20]{2,1,0:T(8,128)S(1)} %copy-done.9, f32[10,4,20]{2,1,0:T(4,128)S(1)} %bitcast.20), custom_call_target="tpu_custom_call" | custom-call | flops 40000000 | bytes 1510208 | tf_op jit(solution)/shard_map/predict/pallas_call | solution.py:31
  16.9 1.6 %own_list.1 = (f32[9,16,128]{2,1,0:T(8,128)S(1)}, f32[256,128]{1,0:T(8,128)}) custom-call(f32[9,16,1024]{2,1,0:T(8,128)S(1)} %get-tuple-element.48.refs_0_.refs_1_, s32[5,3,8]{2,1,0:T(4,128)S(1)} %bitcast.17, f32[5,3,8]{2,1,0:T(4,128)S(1)} %bitcast.21, f32[7,8,4,128]{3,2,1,0:T(4,128)S(1)} %collective-permute-done.refs_3_.refs_4_.refs_6_, ...), custom_call_target="tpu_custom_call" | custom-call | flops 1000000 | bytes 795584 | tf_op jit(solution)/shard_map/own_list/pallas_call | solution.py:31
  18.5 3.8 %all-to-all-start = ((f32[32,8,128]{2,1,0:T(8,128)}), f32[32,8,128]{2,1,0:T(8,128)S(1)}, u32[]{:S(2)}, u32[]{:S(2)}) async-start(f32[32,8,128]{2,1,0:T(8,128)} %bitcast.6), calls=%async_computation | async-start | bytes 262144 | tf_op jit(solution)/shard_map/all_to_all | solution.py:634
  22.4 1.5 %outgoing.1 = (f32[96,128]{1,0:T(8,128)S(1)}, f32[96,128]{1,0:T(8,128)S(1)}, f32[96,128]{1,0:T(8,128)S(1)}, f32[96,128]{1,0:T(8,128)S(1)}) custom-call(f32[9,16,1024]{2,1,0:T(8,128)S(1)} %get-tuple-element.48.refs_0_.refs_1_, s32[4,128]{1,0:T(4,128)S(1)} %copy-done.16, f32[256,128]{1,0:T(8,128)} %get-tuple-element.54.refs_2_.refs_6_), custom_call_target="tpu_custom_call" | custom-call | flops 10000000 | bytes 788480 | tf_op jit(solution)/shard_map/outgoing/pallas_call | solution.py:31
  26.4 0.7 collective-permute-start.5
  27.1 4.5 %collective-permute-start.6 = (f32[168,128]{1,0:T(8,128)S(1)}, f32[168,128]{1,0:T(8,128)S(1)}, u32[]{:S(2)}, u32[]{:S(2)}) collective-permute-start(f32[168,128]{1,0:T(8,128)S(1)} %get-tuple-element.61), channel_id=1, source_target_pairs={{0,4},{4,0},{8,12},{12,8},{16,20},{20,16},{24,28},{28,24},{1,5},{5... | collective-permute-start | bytes 258056 | tf_op jit(solution)/shard_map/ppermute | solution.py:50
  31.6 2.5 %collective-permute-start.7 = (f32[168,128]{1,0:T(8,128)S(1)}, f32[168,128]{1,0:T(8,128)S(1)}, u32[]{:S(2)}, u32[]{:S(2)}) collective-permute-start(f32[168,128]{1,0:T(8,128)S(1)} %get-tuple-element.62), channel_id=1, source_target_pairs={{0,1},{1,0},{2,3},{3,2},{4,5},{5,4},{6,7},{7,6},{8,9},{9,8},{10,11... | collective-permute-start | bytes 258056 | tf_op jit(solution)/shard_map/ppermute | solution.py:50
  34.2 0.9 %collective-permute-done.7.refs_12_.refs_9_ = f32[168,128]{1,0:T(8,128)S(1)} collective-permute-done((f32[168,128]{1,0:T(8,128)S(1)}, f32[168,128]{1,0:T(8,128)S(1)}, u32[]{:S(2)}, u32[]{:S(2)}) %collective-permute-start.7) | collective-permute-done | bytes 86048 | tf_op jit(solution)/shard_map/ppermute | solution.py:50
  35.1 0.8 %copy-done.12 = f32[1,8,16,128]{3,2,1,0:T(8,128)S(1)} copy-done((f32[1,8,16,128]{3,2,1,0:T(8,128)S(1)}, f32[1,8,16,128]{3,2,1,0:T(8,128)}, u32[]{:S(2)}) %copy-start.12) | copy-done | bytes 65560
  35.9 1.1 %injected.1 = (f32[4,8,16,128]{3,2,1,0:T(8,128)S(1)}, f32[264,128]{1,0:T(8,128)S(1)}, f32[4,8,4,128]{3,2,1,0:T(4,128)S(1)}, f32[264,128]{1,0:T(8,128)S(1)}, f32[...) custom-call(f32[4,8,16,128]{3,2,1,0:T(8,128)S(1)} %copy-done.4, f32[3,8,16,128]{3,2,1,0:T(8,128)S(1)} %copy-done.1, ...), custom_call_target="tpu_custom_call" | custom-call | flops 1000000 | bytes 2679776 | tf_op jit(solution)/shard_map/injected/pallas_call | solution.py:31
  37.0 0.7 collective-permute-start.8
  37.7 4.2 %collective-permute-start.10 = (f32[264,128]{1,0:T(8,128)S(1)}, f32[264,128]{1,0:T(8,128)S(1)}, u32[]{:S(2)}, u32[]{:S(2)}) collective-permute-start(f32[264,128]{1,0:T(8,128)S(1)} %get-tuple-element.64.refs_10_), channel_id=1, source_target_pairs={{0,4},{4,0},{8,12},{12,8},{16,20},{20,16},{24,28},{28,24},{1,5},{5... | collective-permute-start | bytes 405512 | tf_op jit(solution)/shard_map/ppermute | solution.py:50
  42.6 3.7 %collective-permute-start.11 = (f32[4,8,4,128]{3,2,1,0:T(4,128)S(1)}, f32[4,8,4,128]{3,2,1,0:T(4,128)S(1)}, u32[]{:S(2)}, u32[]{:S(2)}) collective-permute-start(f32[4,8,4,128]{3,2,1,0:T(4,128)S(1)} %get-tuple-element.70), channel_id=1, source_target_pairs={{0,1},{1,0},{2,3},{3,2},{4,5},{5,4},{6,7},{7,6},{8,9},{9,8},{10,11... | collective-permute-start | bytes 196616 | tf_op jit(solution)/shard_map/ppermute | solution.py:50
  46.3 1.8 %flux.2 = (f32[9,20,256]{2,1,0:T(8,128)S(1)}, f32[8,128]{1,0:T(8,128)S(1)}) custom-call(f32[9,20,256]{2,1,0:T(8,128)S(1)} %get-tuple-element.47.refs_0_, f32[9,16,1024]{2,1,0:T(8,128)S(1)} %get-tuple-element.48.refs_0_.refs_1_, f32[9,16,128]{2,1,0:T(8,128)S(1)} %get-tuple-element.51.refs_2_, f32[9,9,4,256]{3,2,1,0:T(4,128)S(1)} %bitcast.8, ...), custom_call_target="tpu_custom_call" | custom-call | flops 20000000 | bytes 1719424 | tf_op jit(solution)/shard_map/flux/pallas_call | solution.py:31
  48.5 0.7 collective-permute-start.12
  49.9 3.1 %collective-permute-start.15 = (f32[72,128]{1,0:T(8,128)S(1)}, f32[72,128]{1,0:T(8,128)S(1)}, u32[]{:S(2)}, u32[]{:S(2)}) collective-permute-start(f32[72,128]{1,0:T(8,128)S(1)} %get-tuple-element.78), channel_id=1, source_target_pairs={{0,1},{1,0},{2,3},{3,2},{4,5},{5,4},{6,7},{7,6},{8,9},{9,8},{10,11... | collective-permute-start | bytes 110600 | tf_op jit(solution)/shard_map/ppermute | solution.py:50
  52.9 4.2 %collective-permute-start.14 = (f32[72,128]{1,0:T(8,128)S(1)}, f32[72,128]{1,0:T(8,128)S(1)}, u32[]{:S(2)}, u32[]{:S(2)}) collective-permute-start(f32[72,128]{1,0:T(8,128)S(1)} %get-tuple-element.73.refs_6_), channel_id=1, source_target_pairs={{0,4},{4,0},{8,12},{12,8},{16,20},{20,16},{24,28},{28,24},{1,5},{5... | collective-permute-start | bytes 110600 | tf_op jit(solution)/shard_map/ppermute | solution.py:50
  57.6 1.1 %volume.1 = (f32[9,20,256]{2,1,0:T(8,128)S(1)}, f32[8,128]{1,0:T(8,128)S(1)}) custom-call(f32[9,20,256]{2,1,0:T(8,128)S(1)} %get-tuple-element.65.refs_0_, f32[32,2304]{1,0:T(8,128)S(1)} %get-tuple-element.66.refs_1_, f32[9,9,3,256]{3,2,1,0:T(4,128)S(1)} %bitcast.12, f32[3,20,20]{2,1,0:T(8,128)S(1)} %copy-done.9, f32[3,8,16,128]{3,2,1,0:T(8,128)S(1)} %advection.4.refs_4_.refs_3_), custom_call_target="tpu_custom_call" | custom-call | flops 10000000 | bytes 921280 | tf_op jit(solution)/shard_map/volume/pallas_call | solution.py:31
  59.4 0.7 collective-permute-start.16
  60.0 4.2 %collective-permute-start.18 = (f32[264,128]{1,0:T(8,128)S(1)}, f32[264,128]{1,0:T(8,128)S(1)}, u32[]{:S(2)}, u32[]{:S(2)}) collective-permute-start(f32[264,128]{1,0:T(8,128)S(1)} %get-tuple-element.80.refs_10_), channel_id=1, source_target_pairs={{0,4},{4,0},{8,12},{12,8},{16,20},{20,16},{24,28},{28,24},{1,5},{5... | collective-permute-start | bytes 405512 | tf_op jit(solution)/shard_map/ppermute | solution.py:50
  64.9 2.4 %collective-permute-start.19 = (f32[4,8,4,128]{3,2,1,0:T(4,128)S(1)}, f32[4,8,4,128]{3,2,1,0:T(4,128)S(1)}, u32[]{:S(2)}, u32[]{:S(2)}) collective-permute-start(f32[4,8,4,128]{3,2,1,0:T(4,128)S(1)} %get-tuple-element.85), channel_id=1, source_target_pairs={{0,1},{1,0},{2,3},{3,2},{4,5},{5,4},{6,7},{7,6},{8,9},{9,8},{10,11... | collective-permute-start | bytes 196616 | tf_op jit(solution)/shard_map/ppermute | solution.py:50
  67.3 1.8 %flux.3 = (f32[9,20,256]{2,1,0:T(8,128)S(1)}, f32[8,128]{1,0:T(8,128)S(1)}) custom-call(f32[9,20,256]{2,1,0:T(8,128)S(1)} %get-tuple-element.74.refs_0_, f32[9,16,1024]{2,1,0:T(8,128)S(1)} %get-tuple-element.48.refs_0_.refs_1_, f32[9,16,128]{2,1,0:T(8,128)S(1)} %get-tuple-element.51.refs_2_, f32[9,9,4,256]{3,2,1,0:T(4,128)S(1)} %bitcast.9, ...), custom_call_target="tpu_custom_call" | custom-call | flops 20000000 | bytes 1719424 | tf_op jit(solution)/shard_map/flux/pallas_call | solution.py:31
  70.9 3.1 %collective-permute-start.23 = (f32[72,128]{1,0:T(8,128)S(1)}, f32[72,128]{1,0:T(8,128)S(1)}, u32[]{:S(2)}, u32[]{:S(2)}) collective-permute-start(f32[72,128]{1,0:T(8,128)S(1)} %get-tuple-element.91), channel_id=1, source_target_pairs={{0,1},{1,0},{2,3},{3,2},{4,5},{5,4},{6,7},{7,6},{8,9},{9,8},{10,11... | collective-permute-start | bytes 110600 | tf_op jit(solution)/shard_map/ppermute | solution.py:50
  74.0 4.6 %collective-permute-start.22 = (f32[72,128]{1,0:T(8,128)S(1)}, f32[72,128]{1,0:T(8,128)S(1)}, u32[]{:S(2)}, u32[]{:S(2)}) collective-permute-start(f32[72,128]{1,0:T(8,128)S(1)} %get-tuple-element.87.refs_6_), channel_id=1, source_target_pairs={{0,4},{4,0},{8,12},{12,8},{16,20},{20,16},{24,28},{28,24},{1,5},{5... | collective-permute-start | bytes 110600 | tf_op jit(solution)/shard_map/ppermute | solution.py:50
  79.1 0.9 %replies.1 = f32[9,20,256]{2,1,0:T(8,128)} custom-call(f32[9,20,256]{2,1,0:T(8,128)S(1)} %get-tuple-element.81.refs_0_, f32[9,9,4,256]{3,2,1,0:T(4,128)S(1)} %bitcast.10, f32[10,4,20]{2,1,0:T(4,128)S(1)} %bitcast.16, s32[4,256]{1,0:T(4,128)S(1)} %copy-done.13, s32[5,3,8]{2,1,0:T(4,128)S(1)} %bitcast.19, f32[1,128]{1,0:T(1,128)S(1)} %get-tuple-element.71.refs_7_.refs_5_, ...), custom_call_target="tpu_custom_call" | custom-call | flops 1000000 | bytes 782432 | tf_op jit(solution)/shard_map/replies/pallas_call | solution.py:31
  80.5 1.0 %velocity.3 = f32[4,8,16,128]{3,2,1,0:T(8,128)} custom-call(f32[4,8,16,128]{3,2,1,0:T(8,128)S(1)} %get-tuple-element.82.refs_0_, f32[1,8,16,128]{3,2,1,0:T(8,128)S(1)} %get-tuple-element.88.refs_1_, f32[2,8,16,128]{3,2,1,0:T(8,128)S(1)} %copy-done.2, f32[3,8,16,128]{3,2,1,0:T(8,128)S(1)} %advection.5.refs_8_.refs_3_, ...), custom_call_target="tpu_custom_call" | custom-call | flops 1000000 | bytes 1064960 | tf_op jit(solution)/shard_map/velocity/pallas_call | solution.py:31
  (69 shorter events, 10.1 us)
Async XLA Ops:
  2.5 10.9 %copy-start.6 = (f32[3,9,9,256]{3,0,2,1:T(4,128)S(1)}, f32[3,9,9,256]{3,0,2,1:T(4,128)}, u32[]{:S(2)}) copy-start(f32[3,9,9,256]{3,0,2,1:T(4,128)} %param.14) | copy-start | bytes 746500
  2.5 10.9 %copy-start.9 = (f32[3,20,20]{2,1,0:T(8,128)S(1)}, f32[3,20,20]{2,1,0:T(8,128)}, u32[]{:S(2)}) copy-start(f32[3,20,20]{2,1,0:T(8,128)} %refs_3_.2) | copy-start | bytes 14404
  2.5 10.9 %copy-start.14 = (f32[4,10,20]{2,0,1:T(4,128)S(1)}, f32[4,10,20]{2,0,1:T(4,128)}, u32[]{:S(2)}) copy-start(f32[4,10,20]{2,0,1:T(4,128)} %param.17) | copy-start | bytes 9604
  3.4 13.5 %collective-permute-start = (f32[7,8,4,128]{3,2,1,0:T(4,128)S(1)}, f32[7,8,4,128]{3,2,1,0:T(4,128)S(1)}, u32[]{:S(2)}, u32[]{:S(2)}) collective-permute-start(f32[7,8,4,128]{3,2,1,0:T(4,128)S(1)} %get-tuple-element.49), channel_id=1, source_target_pairs={{1,2},{2,1},{5,6},{6,5},{9,10},{10,9},{13,14},{14,13},{17,18},{18,... | collective-permute-start | bytes 344072 | tf_op jit(solution)/shard_map/ppermute | solution.py:50
  4.0 12.9 %collective-permute-start.1 = (f32[7,8,4,128]{3,2,1,0:T(4,128)S(1)}, f32[7,8,4,128]{3,2,1,0:T(4,128)S(1)}, u32[]{:S(2)}, u32[]{:S(2)}) collective-permute-start(f32[7,8,4,128]{3,2,1,0:T(4,128)S(1)} %get-tuple-element.50), channel_id=1, source_target_pairs={{0,1},{1,0},{2,3},{3,2},{4,5},{5,4},{6,7},{7,6},{8,9},{9,8},{10,11... | collective-permute-start | bytes 344072 | tf_op jit(solution)/shard_map/ppermute | solution.py:50
  8.4 15.5 %collective-permute-start.2 = (f32[7,4,16,128]{3,2,1,0:T(8,128)}, f32[7,4,16,128]{3,2,1,0:T(8,128)S(1)}, u32[]{:S(2)}, u32[]{:S(2)}) collective-permute-start(f32[7,4,16,128]{3,2,1,0:T(8,128)} %get-tuple-element.52), channel_id=1, source_target_pairs={{4,8},{8,4},{12,16},{16,12},{20,24},{24,20},{5,9},{9,5},{13,17},{1... | collective-permute-start | bytes 688136 | tf_op jit(solution)/shard_map/ppermute | solution.py:50
  9.0 14.8 %collective-permute-start.3 = (f32[7,4,16,128]{3,2,1,0:T(8,128)}, f32[7,4,16,128]{3,2,1,0:T(8,128)S(1)}, u32[]{:S(2)}, u32[]{:S(2)}) collective-permute-start(f32[7,4,16,128]{3,2,1,0:T(8,128)} %get-tuple-element.53), channel_id=1, source_target_pairs={{0,4},{4,0},{8,12},{12,8},{16,20},{20,16},{24,28},{28,24},{1,5},{5... | collective-permute-start | bytes 688136 | tf_op jit(solution)/shard_map/ppermute | solution.py:50
  18.5 3.8 %copy-start.16 = (s32[4,128]{1,0:T(4,128)S(1)}, s32[4,128]{1,0:T(4,128)}, u32[]{:S(2)}) copy-start(s32[4,128]{1,0:T(4,128)} %refs_1_.10) | copy-start | bytes 6148
  18.5 16.6 %all-to-all-start = ((f32[32,8,128]{2,1,0:T(8,128)}), f32[32,8,128]{2,1,0:T(8,128)S(1)}, u32[]{:S(2)}, u32[]{:S(2)}) async-start(f32[32,8,128]{2,1,0:T(8,128)} %bitcast.6), calls=%async_computation | async-start | bytes 262144 | tf_op jit(solution)/shard_map/all_to_all | solution.py:634
  25.7 8.4 %collective-permute-start.4 = (f32[168,128]{1,0:T(8,128)S(1)}, f32[168,128]{1,0:T(8,128)S(1)}, u32[]{:S(2)}, u32[]{:S(2)}) collective-permute-start(f32[168,128]{1,0:T(8,128)S(1)} %get-tuple-element.59), channel_id=1, source_target_pairs={{4,8},{8,4},{12,16},{16,12},{20,24},{24,20},{5,9},{9,5},{13,17},{1... | collective-permute-start | bytes 258056 | tf_op jit(solution)/shard_map/ppermute | solution.py:50
  26.4 7.8 %collective-permute-start.5 = (f32[168,128]{1,0:T(8,128)S(1)}, f32[168,128]{1,0:T(8,128)S(1)}, u32[]{:S(2)}, u32[]{:S(2)}) collective-permute-start(f32[168,128]{1,0:T(8,128)S(1)} %get-tuple-element.60), channel_id=1, source_target_pairs={{1,2},{2,1},{5,6},{6,5},{9,10},{10,9},{13,14},{14,13},{17,18},{18,... | collective-permute-start | bytes 258056 | tf_op jit(solution)/shard_map/ppermute | solution.py:50
  27.1 7.1 %collective-permute-start.6 = (f32[168,128]{1,0:T(8,128)S(1)}, f32[168,128]{1,0:T(8,128)S(1)}, u32[]{:S(2)}, u32[]{:S(2)}) collective-permute-start(f32[168,128]{1,0:T(8,128)S(1)} %get-tuple-element.61), channel_id=1, source_target_pairs={{0,4},{4,0},{8,12},{12,8},{16,20},{20,16},{24,28},{28,24},{1,5},{5... | collective-permute-start | bytes 258056 | tf_op jit(solution)/shard_map/ppermute | solution.py:50
  31.6 3.5 %collective-permute-start.7 = (f32[168,128]{1,0:T(8,128)S(1)}, f32[168,128]{1,0:T(8,128)S(1)}, u32[]{:S(2)}, u32[]{:S(2)}) collective-permute-start(f32[168,128]{1,0:T(8,128)S(1)} %get-tuple-element.62), channel_id=1, source_target_pairs={{0,1},{1,0},{2,3},{3,2},{4,5},{5,4},{6,7},{7,6},{8,9},{9,8},{10,11... | collective-permute-start | bytes 258056 | tf_op jit(solution)/shard_map/ppermute | solution.py:50
  35.9 10.4 %copy-start.5 = (f32[4,9,9,256]{3,0,2,1:T(4,128)S(1)}, f32[4,9,9,256]{3,0,2,1:T(4,128)}, u32[]{:S(2)}) copy-start(f32[4,9,9,256]{3,0,2,1:T(4,128)} %param.15) | copy-start | bytes 995332
  35.9 10.4 %copy-start.8 = (f32[4,20,10]{1,0,2:T(4,128)S(1)}, f32[4,20,10]{1,0,2:T(4,128)}, u32[]{:S(2)}) copy-start(f32[4,20,10]{1,0,2:T(4,128)} %param.18) | copy-start | bytes 9604
  37.0 11.1 %collective-permute-start.8 = (f32[264,128]{1,0:T(8,128)S(1)}, f32[264,128]{1,0:T(8,128)S(1)}, u32[]{:S(2)}, u32[]{:S(2)}) collective-permute-start(f32[264,128]{1,0:T(8,128)S(1)} %get-tuple-element.68), channel_id=1, source_target_pairs={{4,8},{8,4},{12,16},{16,12},{20,24},{24,20},{5,9},{9,5},{13,17},{1... | collective-permute-start | bytes 405512 | tf_op jit(solution)/shard_map/ppermute | solution.py:50
  37.7 10.5 %collective-permute-start.10 = (f32[264,128]{1,0:T(8,128)S(1)}, f32[264,128]{1,0:T(8,128)S(1)}, u32[]{:S(2)}, u32[]{:S(2)}) collective-permute-start(f32[264,128]{1,0:T(8,128)S(1)} %get-tuple-element.64.refs_10_), channel_id=1, source_target_pairs={{0,4},{4,0},{8,12},{12,8},{16,20},{20,16},{24,28},{28,24},{1,5},{5... | collective-permute-start | bytes 405512 | tf_op jit(solution)/shard_map/ppermute | solution.py:50
  41.9 6.2 %collective-permute-start.9 = (f32[4,8,4,128]{3,2,1,0:T(4,128)S(1)}, f32[4,8,4,128]{3,2,1,0:T(4,128)S(1)}, u32[]{:S(2)}, u32[]{:S(2)}) collective-permute-start(f32[4,8,4,128]{3,2,1,0:T(4,128)S(1)} %get-tuple-element.69), channel_id=1, source_target_pairs={{1,2},{2,1},{5,6},{6,5},{9,10},{10,9},{13,14},{14,13},{17,18},{18,... | collective-permute-start | bytes 196616 | tf_op jit(solution)/shard_map/ppermute | solution.py:50
  42.6 3.7 %copy-start.13 = (s32[4,256]{1,0:T(4,128)S(1)}, s32[4,256]{1,0:T(4,128)}, u32[]{:S(2)}) copy-start(s32[4,256]{1,0:T(4,128)} %refs_3_.3) | copy-start | bytes 12292
  42.6 5.5 %collective-permute-start.11 = (f32[4,8,4,128]{3,2,1,0:T(4,128)S(1)}, f32[4,8,4,128]{3,2,1,0:T(4,128)S(1)}, u32[]{:S(2)}, u32[]{:S(2)}) collective-permute-start(f32[4,8,4,128]{3,2,1,0:T(4,128)S(1)} %get-tuple-element.70), channel_id=1, source_target_pairs={{0,1},{1,0},{2,3},{3,2},{4,5},{5,4},{6,7},{7,6},{8,9},{9,8},{10,11... | collective-permute-start | bytes 196616 | tf_op jit(solution)/shard_map/ppermute | solution.py:50
  48.5 10.2 %collective-permute-start.12 = (f32[72,128]{1,0:T(8,128)S(1)}, f32[72,128]{1,0:T(8,128)S(1)}, u32[]{:S(2)}, u32[]{:S(2)}) collective-permute-start(f32[72,128]{1,0:T(8,128)S(1)} %get-tuple-element.76), channel_id=1, source_target_pairs={{4,8},{8,4},{12,16},{16,12},{20,24},{24,20},{5,9},{9,5},{13,17},{1... | collective-permute-start | bytes 110600 | tf_op jit(solution)/shard_map/ppermute | solution.py:50
  49.2 9.5 %collective-permute-start.13 = (f32[72,128]{1,0:T(8,128)S(1)}, f32[72,128]{1,0:T(8,128)S(1)}, u32[]{:S(2)}, u32[]{:S(2)}) collective-permute-start(f32[72,128]{1,0:T(8,128)S(1)} %get-tuple-element.77), channel_id=1, source_target_pairs={{1,2},{2,1},{5,6},{6,5},{9,10},{10,9},{13,14},{14,13},{17,18},{18,... | collective-permute-start | bytes 110600 | tf_op jit(solution)/shard_map/ppermute | solution.py:50
  49.9 8.9 %collective-permute-start.15 = (f32[72,128]{1,0:T(8,128)S(1)}, f32[72,128]{1,0:T(8,128)S(1)}, u32[]{:S(2)}, u32[]{:S(2)}) collective-permute-start(f32[72,128]{1,0:T(8,128)S(1)} %get-tuple-element.78), channel_id=1, source_target_pairs={{0,1},{1,0},{2,3},{3,2},{4,5},{5,4},{6,7},{7,6},{8,9},{9,8},{10,11... | collective-permute-start | bytes 110600 | tf_op jit(solution)/shard_map/ppermute | solution.py:50
  52.9 6.1 %collective-permute-start.14 = (f32[72,128]{1,0:T(8,128)S(1)}, f32[72,128]{1,0:T(8,128)S(1)}, u32[]{:S(2)}, u32[]{:S(2)}) collective-permute-start(f32[72,128]{1,0:T(8,128)S(1)} %get-tuple-element.73.refs_6_), channel_id=1, source_target_pairs={{0,4},{4,0},{8,12},{12,8},{16,20},{20,16},{24,28},{28,24},{1,5},{5... | collective-permute-start | bytes 110600 | tf_op jit(solution)/shard_map/ppermute | solution.py:50
  59.4 9.8 %collective-permute-start.16 = (f32[264,128]{1,0:T(8,128)S(1)}, f32[264,128]{1,0:T(8,128)S(1)}, u32[]{:S(2)}, u32[]{:S(2)}) collective-permute-start(f32[264,128]{1,0:T(8,128)S(1)} %get-tuple-element.83), channel_id=1, source_target_pairs={{4,8},{8,4},{12,16},{16,12},{20,24},{24,20},{5,9},{9,5},{13,17},{1... | collective-permute-start | bytes 405512 | tf_op jit(solution)/shard_map/ppermute | solution.py:50
  60.0 9.1 %collective-permute-start.18 = (f32[264,128]{1,0:T(8,128)S(1)}, f32[264,128]{1,0:T(8,128)S(1)}, u32[]{:S(2)}, u32[]{:S(2)}) collective-permute-start(f32[264,128]{1,0:T(8,128)S(1)} %get-tuple-element.80.refs_10_), channel_id=1, source_target_pairs={{0,4},{4,0},{8,12},{12,8},{16,20},{20,16},{24,28},{28,24},{1,5},{5... | collective-permute-start | bytes 405512 | tf_op jit(solution)/shard_map/ppermute | solution.py:50
  64.3 4.8 %collective-permute-start.17 = (f32[4,8,4,128]{3,2,1,0:T(4,128)S(1)}, f32[4,8,4,128]{3,2,1,0:T(4,128)S(1)}, u32[]{:S(2)}, u32[]{:S(2)}) collective-permute-start(f32[4,8,4,128]{3,2,1,0:T(4,128)S(1)} %get-tuple-element.84), channel_id=1, source_target_pairs={{1,2},{2,1},{5,6},{6,5},{9,10},{10,9},{13,14},{14,13},{17,18},{18,... | collective-permute-start | bytes 196616 | tf_op jit(solution)/shard_map/ppermute | solution.py:50
  64.9 4.2 %collective-permute-start.19 = (f32[4,8,4,128]{3,2,1,0:T(4,128)S(1)}, f32[4,8,4,128]{3,2,1,0:T(4,128)S(1)}, u32[]{:S(2)}, u32[]{:S(2)}) collective-permute-start(f32[4,8,4,128]{3,2,1,0:T(4,128)S(1)} %get-tuple-element.85), channel_id=1, source_target_pairs={{0,1},{1,0},{2,3},{3,2},{4,5},{5,4},{6,7},{7,6},{8,9},{9,8},{10,11... | collective-permute-start | bytes 196616 | tf_op jit(solution)/shard_map/ppermute | solution.py:50
  69.6 10.5 %collective-permute-start.20 = (f32[72,128]{1,0:T(8,128)S(1)}, f32[72,128]{1,0:T(8,128)S(1)}, u32[]{:S(2)}, u32[]{:S(2)}) collective-permute-start(f32[72,128]{1,0:T(8,128)S(1)} %get-tuple-element.89), channel_id=1, source_target_pairs={{4,8},{8,4},{12,16},{16,12},{20,24},{24,20},{5,9},{9,5},{13,17},{1... | collective-permute-start | bytes 110600 | tf_op jit(solution)/shard_map/ppermute | solution.py:50
  70.2 9.8 %collective-permute-start.21 = (f32[72,128]{1,0:T(8,128)S(1)}, f32[72,128]{1,0:T(8,128)S(1)}, u32[]{:S(2)}, u32[]{:S(2)}) collective-permute-start(f32[72,128]{1,0:T(8,128)S(1)} %get-tuple-element.90), channel_id=1, source_target_pairs={{1,2},{2,1},{5,6},{6,5},{9,10},{10,9},{13,14},{14,13},{17,18},{18,... | collective-permute-start | bytes 110600 | tf_op jit(solution)/shard_map/ppermute | solution.py:50
  70.9 9.1 %collective-permute-start.23 = (f32[72,128]{1,0:T(8,128)S(1)}, f32[72,128]{1,0:T(8,128)S(1)}, u32[]{:S(2)}, u32[]{:S(2)}) collective-permute-start(f32[72,128]{1,0:T(8,128)S(1)} %get-tuple-element.91), channel_id=1, source_target_pairs={{0,1},{1,0},{2,3},{3,2},{4,5},{5,4},{6,7},{7,6},{8,9},{9,8},{10,11... | collective-permute-start | bytes 110600 | tf_op jit(solution)/shard_map/ppermute | solution.py:50
  74.0 6.6 %collective-permute-start.22 = (f32[72,128]{1,0:T(8,128)S(1)}, f32[72,128]{1,0:T(8,128)S(1)}, u32[]{:S(2)}, u32[]{:S(2)}) collective-permute-start(f32[72,128]{1,0:T(8,128)S(1)} %get-tuple-element.87.refs_6_), channel_id=1, source_target_pairs={{0,4},{4,0},{8,12},{12,8},{16,20},{20,16},{24,28},{28,24},{1,5},{5... | collective-permute-start | bytes 110600 | tf_op jit(solution)/shard_map/ppermute | solution.py:50
  (10 other events, 13.3 us)

commit v4 on v3

--- a/solution.py
+++ b/solution.py
@@ -348,8 +348,9 @@
 
 
 def widen_pressure(ext, center, xb, zb, xa, za):
-    nx, nz, ny = center.shape
-    ext[RADIUS:RADIUS + nx, ZRIM:ZRIM + nz] = center[...]
+    nx, nz, ny = ext.shape[0] - 2 * RADIUS, ext.shape[1] - 2 * ZRIM, ext.shape[2]
+    if center is not None:
+        ext[RADIUS:RADIUS + nx, ZRIM:ZRIM + nz] = center[...]
     for got, side in zip((xa, xb), sides("gx")):
         ext[pl.ds(side * (nx + RADIUS), RADIUS), ZRIM:ZRIM + nz] = got[HEAD:HEAD + RADIUS * nz, :].reshape(RADIUS, nz, ny)
     for got, side in zip((za, zb), sides("gz")):
@@ -358,7 +359,7 @@
 
 
 def raw_pressure_kernel(
-    air, wind, medium, xb, zb, xa, za, txa, txb, tza, tzb, pressure, oxb, ozb, oxa, oza, ext
+    air, wind, medium, xb, zb, xa, za, txa, txb, tza, tzb, oxb, ozb, oxa, oza, ext, pressure
 ):
     nx, nz, ny = air.shape[1:]
     widen(ext, air, xb, zb, xa, za)
@@ -412,7 +413,7 @@
 
 
 def injected_kernel(
-    n_gx, n_gz, air, wind, medium, raw, moved, wxb, wzb, wxa, wza, pxb, pzb, pxa, pza, table, smap,
+    n_gx, n_gz, air, wind, medium, rxb, rxa, moved, wxb, wzb, wxa, wza, pxb, pzb, pxa, pza, table, smap,
     out, oxb, ozb, oxa, oza, answer, spread, wide, wide_wind,
 ):
     nx, nz, ny = air.shape[1:]
@@ -434,7 +435,10 @@
             block = mul(jnp.where(row_mask, speed, 0.0).astype(BF16), columns)
             spread[da * nx:(da + 1) * nx, db * nz:(db + 1) * nz] = block.reshape(nx, nz, ny)
     widen(wide_wind, wind, wxb, wzb, wxa, wza, first=air.shape[0])
-    widen_pressure(wide, raw.at[0], pxb, pzb, pxa, pza)
+    widen_pressure(wide, None, pxb, pzb, pxa, pza)
+    for got, side in zip((rxa, rxb), sides("gx")):
+        rows = got[HEAD:HEAD + RADIUS * nz, :].reshape(RADIUS, nz, ny)
+        wide[pl.ds(RADIUS + side * (nx - RADIUS), RADIUS), ZRIM:ZRIM + nz] = rows
     load = plane(spread)
     for x in range(nx + 2 * RADIUS):
         xs = x + nx - RADIUS
@@ -644,17 +648,17 @@
     pressure_z = (HEAD + nx * ZRIM, ny)
     both_x = (pressure_x[0] + sent[0], LANES)
     both_z = (pressure_z[0] + sent[0], LANES)
-    raw, xb, zb, xa, za = call(
-        raw_pressure_kernel, "raw_pressure", [block, both_x, both_z, both_x, both_z],
-        [air_state, wind_field, air_medium, *rims, *sent_four], [ext], after=[moved],
-    )
-    both = exchange(xb, zb, xa, za)
+    raw_xb, zb, raw_xa, za = call(
+        raw_pressure_kernel, "raw_pressure", [both_x, both_z, both_x, both_z],
+        [air_state, wind_field, air_medium, *rims, *sent_four], [ext, block], after=[moved],
+    )
+    both = exchange(raw_xb, zb, raw_xa, za)
     rim_x = (HEAD + 4 * RADIUS * nz, ny)
     rim_z = (4, nx, RADIUS, ny)
     air, xb, zb, xa, za, answer = call(
         functools.partial(injected_kernel, n_gx, n_gz), "injected",
         [air_state.shape, rim_x, rim_z, rim_x, rim_z, (1, LANES)],
-        [air_state, wind_field, air_medium, raw, moved, *rims, *both, lists, surface_map],
+        [air_state, wind_field, air_medium, raw_xb, raw_xa, moved, *rims, *both, lists, surface_map],
         [(3 * nx, 3 * nz, ny), wide, (3,) + wide],
     )
     half = faces // 2

time: 82.1 us -> 84.8 us (1.033)
  local copies, waits for them, and re-layouts: 4.68 us -> 6.26 us
  waiting for transfers between devices: 1.77 us -> 3.28 us
    unnamed x34 -> x38, local copies, waits for them, and re-layouts: 4.68 us -> 6.26 us
    ppermute x24, waiting for transfers between devices: 1.77 us -> 3.28 us  [swap(): return lax.ppermute(values, axis, pairs)]
  transfers between devices with their start and end apart: 25 -> 25, of which waited for: 3 -> 4; matrix products, arithmetic and copies ran while one was open for 0% -> 0% of each run, Pallas kernels for 16% -> 15%
where the time goes in v4:
time: 84.8 us; the launch traced here: 84.1 us
  starting transfers between devices  56.6 us (67%)
  Pallas kernels  17 us (20%)
  local copies, waits for them, and re-layouts  6.26 us (7%)
  waiting for transfers between devices  3.28 us (4%)
  between operations  1.04 us (1%)
    ppermute x24, starting transfers between devices, swap(): return lax.ppermute(values, axis, pairs)  52.8 us
    pallas_call x17, Pallas kernels, call(): pl.pallas_call(body, out_shape=[jax.ShapeDtypeStruct(s, F32) for s in out...  17 us
    unnamed x38, local copies, waits for them, and re-layouts  6.26 us
    all_to_all x1, starting transfers between devices, shards(): lax.all_to_all(rows, ('gx', 'gz'), split_axis=0, concat_axis=0, tiled=True)  3.8 us
    ppermute x24, waiting for transfers between devices, swap(): return lax.ppermute(values, axis, pairs)  3.28 us
  transfers between devices with their start and end apart: 25, of which 4 were waited for; matrix products, arithmetic and copies ran while one was open for 0% of the time, Pallas kernels for 15%

profile of v4, /device:TPU:0, one launch (start us, length us, event | category | flops | bytes accessed | tf_op | source)
XLA Modules:
  0.0 84.1 jit_solution(3151189290515939145)
XLA Ops:
  0.6 0.9 %copy-done = f32[3,8,16,128]{3,2,1,0:T(8,128)S(1)} copy-done((f32[3,8,16,128]{3,2,1,0:T(8,128)S(1)}, f32[3,8,16,128]{3,2,1,0:T(8,128)}, u32[]{:S(2)}) %copy-start) | copy-done | bytes 196632
  1.6 0.9 %copy-done.3 = f32[4,8,16,128]{3,2,1,0:T(8,128)S(1)} copy-done((f32[4,8,16,128]{3,2,1,0:T(8,128)S(1)}, f32[4,8,16,128]{3,2,1,0:T(8,128)}, u32[]{:S(2)}) %copy-start.3) | copy-done | bytes 262168
  2.5 0.8 raw_rims.1
  4.0 4.4 %collective-permute-start.1 = (f32[7,8,4,128]{3,2,1,0:T(4,128)S(1)}, f32[7,8,4,128]{3,2,1,0:T(4,128)S(1)}, u32[]{:S(2)}, u32[]{:S(2)}) collective-permute-start(f32[7,8,4,128]{3,2,1,0:T(4,128)S(1)} %get-tuple-element.49), channel_id=1, source_target_pairs={{0,1},{1,0},{2,3},{3,2},{4,5},{5,4},{6,7},{7,6},{8,9},{9,8},{10,11... | collective-permute-start | bytes 344072 | tf_op jit(solution)/shard_map/ppermute | solution.py:50
  9.0 4.3 %collective-permute-start.3 = (f32[7,4,16,128]{3,2,1,0:T(8,128)}, f32[7,4,16,128]{3,2,1,0:T(8,128)S(1)}, u32[]{:S(2)}, u32[]{:S(2)}) collective-permute-start(f32[7,4,16,128]{3,2,1,0:T(8,128)} %get-tuple-element.52), channel_id=1, source_target_pairs={{0,4},{4,0},{8,12},{12,8},{16,20},{20,16},{24,28},{28,24},{1,5},{5... | collective-permute-start | bytes 688136 | tf_op jit(solution)/shard_map/ppermute | solution.py:50
  13.4 0.9 %copy-done.7 = f32[9,20,256]{2,1,0:T(8,128)S(1)} copy-done((f32[9,20,256]{2,1,0:T(8,128)S(1)}, f32[9,20,256]{2,1,0:T(8,128)}, u32[]{:S(2)}) %copy-start.7) | copy-done | bytes 184344
  14.3 2.5 %predict.1 = (f32[32,2304]{1,0:T(8,128)S(1)}, f32[9,16,1024]{2,1,0:T(8,128)S(1)}, f32[9,20,256]{2,1,0:T(8,128)S(1)}) custom-call(f32[9,20,256]{2,1,0:T(8,128)S(1)} %copy-done.7, f32[9,9,3,256]{3,2,1,0:T(4,128)S(1)} %bitcast.11, f32[3,20,20]{2,1,0:T(8,128)S(1)} %copy-done.9, f32[10,4,20]{2,1,0:T(4,128)S(1)} %bitcast.20), custom_call_target="tpu_custom_call" | custom-call | flops 40000000 | bytes 1510208 | tf_op jit(solution)/shard_map/predict/pallas_call | solution.py:31
  16.9 1.6 %own_list.1 = (f32[9,16,128]{2,1,0:T(8,128)S(1)}, f32[256,128]{1,0:T(8,128)}) custom-call(f32[9,16,1024]{2,1,0:T(8,128)S(1)} %get-tuple-element.47.refs_0_.refs_1_, s32[5,3,8]{2,1,0:T(4,128)S(1)} %bitcast.17, f32[5,3,8]{2,1,0:T(4,128)S(1)} %bitcast.21, f32[7,8,4,128]{3,2,1,0:T(4,128)S(1)} %collective-permute-done.refs_3_.refs_4_.refs_7_, ...), custom_call_target="tpu_custom_call" | custom-call | flops 1000000 | bytes 795584 | tf_op jit(solution)/shard_map/own_list/pallas_call | solution.py:31
  18.5 3.8 %all-to-all-start = ((f32[32,8,128]{2,1,0:T(8,128)}), f32[32,8,128]{2,1,0:T(8,128)S(1)}, u32[]{:S(2)}, u32[]{:S(2)}) async-start(f32[32,8,128]{2,1,0:T(8,128)} %bitcast.6), calls=%async_computation | async-start | bytes 262144 | tf_op jit(solution)/shard_map/all_to_all | solution.py:638
  22.4 1.5 %outgoing.1 = (f32[96,128]{1,0:T(8,128)S(1)}, f32[96,128]{1,0:T(8,128)S(1)}, f32[96,128]{1,0:T(8,128)S(1)}, f32[96,128]{1,0:T(8,128)S(1)}) custom-call(f32[9,16,1024]{2,1,0:T(8,128)S(1)} %get-tuple-element.47.refs_0_.refs_1_, s32[4,128]{1,0:T(4,128)S(1)} %copy-done.18, f32[256,128]{1,0:T(8,128)} %get-tuple-element.53.refs_2_.refs_6_), custom_call_target="tpu_custom_call" | custom-call | flops 10000000 | bytes 788480 | tf_op jit(solution)/shard_map/outgoing/pallas_call | solution.py:31
  25.1 0.7 collective-permute-start.5
  25.8 3.2 %collective-permute-start.7 = (f32[168,128]{1,0:T(8,128)S(1)}, f32[168,128]{1,0:T(8,128)S(1)}, u32[]{:S(2)}, u32[]{:S(2)}) collective-permute-start(f32[168,128]{1,0:T(8,128)S(1)} %get-tuple-element.61), channel_id=1, source_target_pairs={{0,1},{1,0},{2,3},{3,2},{4,5},{5,4},{6,7},{7,6},{8,9},{9,8},{10,11... | collective-permute-start | bytes 258056 | tf_op jit(solution)/shard_map/ppermute | solution.py:50
  30.3 4.2 %collective-permute-start.6 = (f32[168,128]{1,0:T(8,128)S(1)}, f32[168,128]{1,0:T(8,128)S(1)}, u32[]{:S(2)}, u32[]{:S(2)}) collective-permute-start(f32[168,128]{1,0:T(8,128)S(1)} %get-tuple-element.60.refs_4_), channel_id=1, source_target_pairs={{0,4},{4,0},{8,12},{12,8},{16,20},{20,16},{24,28},{28,24},{1,5},{5... | collective-permute-start | bytes 258056 | tf_op jit(solution)/shard_map/ppermute | solution.py:50
  35.1 2.0 %collective-permute-done.6.refs_12_.refs_8_ = f32[168,128]{1,0:T(8,128)S(1)} collective-permute-done((f32[168,128]{1,0:T(8,128)S(1)}, f32[168,128]{1,0:T(8,128)S(1)}, u32[]{:S(2)}, u32[]{:S(2)}) %collective-permute-start.6) | collective-permute-done | bytes 86048 | tf_op jit(solution)/shard_map/ppermute | solution.py:50
  37.1 0.9 %copy-done.12 = f32[168,128]{1,0:T(8,128)S(1)} copy-done((f32[168,128]{1,0:T(8,128)S(1)}, f32[168,128]{1,0:T(8,128)}, u32[]{:S(2)}) %copy-start.12) | copy-done | bytes 86040
  38.0 0.9 %copy-done.14 = f32[168,128]{1,0:T(8,128)S(1)} copy-done((f32[168,128]{1,0:T(8,128)S(1)}, f32[168,128]{1,0:T(8,128)}, u32[]{:S(2)}) %copy-start.14) | copy-done | bytes 86040
  38.8 1.1 %injected.1 = (f32[4,8,16,128]{3,2,1,0:T(8,128)S(1)}, f32[264,128]{1,0:T(8,128)S(1)}, f32[4,8,4,128]{3,2,1,0:T(4,128)S(1)}, f32[264,128]{1,0:T(8,128)S(1)}, f32[...) custom-call(f32[4,8,16,128]{3,2,1,0:T(8,128)S(1)} %copy-done.4, f32[3,8,16,128]{3,2,1,0:T(8,128)S(1)} %copy-done.1, ...), custom_call_target="tpu_custom_call" | custom-call | flops 1000000 | bytes 2786272 | tf_op jit(solution)/shard_map/injected/pallas_call | solution.py:31
  39.9 0.7 collective-permute-start.8
  40.6 5.2 %collective-permute-start.10 = (f32[264,128]{1,0:T(8,128)S(1)}, f32[264,128]{1,0:T(8,128)S(1)}, u32[]{:S(2)}, u32[]{:S(2)}) collective-permute-start(f32[264,128]{1,0:T(8,128)S(1)} %get-tuple-element.62.refs_10_), channel_id=1, source_target_pairs={{0,4},{4,0},{8,12},{12,8},{16,20},{20,16},{24,28},{28,24},{1,5},{5... | collective-permute-start | bytes 405512 | tf_op jit(solution)/shard_map/ppermute | solution.py:50
  46.5 2.1 %collective-permute-start.11 = (f32[4,8,4,128]{3,2,1,0:T(4,128)S(1)}, f32[4,8,4,128]{3,2,1,0:T(4,128)S(1)}, u32[]{:S(2)}, u32[]{:S(2)}) collective-permute-start(f32[4,8,4,128]{3,2,1,0:T(4,128)S(1)} %get-tuple-element.68), channel_id=1, source_target_pairs={{0,1},{1,0},{2,3},{3,2},{4,5},{5,4},{6,7},{7,6},{8,9},{9,8},{10,11... | collective-permute-start | bytes 196616 | tf_op jit(solution)/shard_map/ppermute | solution.py:50
  48.6 1.8 %flux.2 = (f32[9,20,256]{2,1,0:T(8,128)S(1)}, f32[8,128]{1,0:T(8,128)S(1)}) custom-call(f32[9,20,256]{2,1,0:T(8,128)S(1)} %get-tuple-element.46.refs_0_, f32[9,16,1024]{2,1,0:T(8,128)S(1)} %get-tuple-element.47.refs_0_.refs_1_, f32[9,16,128]{2,1,0:T(8,128)S(1)} %get-tuple-element.50.refs_2_, f32[9,9,4,256]{3,2,1,0:T(4,128)S(1)} %bitcast.8, ...), custom_call_target="tpu_custom_call" | custom-call | flops 20000000 | bytes 1719424 | tf_op jit(solution)/shard_map/flux/pallas_call | solution.py:31
  52.6 2.6 %collective-permute-start.15 = (f32[72,128]{1,0:T(8,128)S(1)}, f32[72,128]{1,0:T(8,128)S(1)}, u32[]{:S(2)}, u32[]{:S(2)}) collective-permute-start(f32[72,128]{1,0:T(8,128)S(1)} %get-tuple-element.76), channel_id=1, source_target_pairs={{0,1},{1,0},{2,3},{3,2},{4,5},{5,4},{6,7},{7,6},{8,9},{9,8},{10,11... | collective-permute-start | bytes 110600 | tf_op jit(solution)/shard_map/ppermute | solution.py:50
  55.2 4.9 %collective-permute-start.14 = (f32[72,128]{1,0:T(8,128)S(1)}, f32[72,128]{1,0:T(8,128)S(1)}, u32[]{:S(2)}, u32[]{:S(2)}) collective-permute-start(f32[72,128]{1,0:T(8,128)S(1)} %get-tuple-element.71.refs_6_), channel_id=1, source_target_pairs={{0,4},{4,0},{8,12},{12,8},{16,20},{20,16},{24,28},{28,24},{1,5},{5... | collective-permute-start | bytes 110600 | tf_op jit(solution)/shard_map/ppermute | solution.py:50
  60.6 1.1 %volume.1 = (f32[9,20,256]{2,1,0:T(8,128)S(1)}, f32[8,128]{1,0:T(8,128)S(1)}) custom-call(f32[9,20,256]{2,1,0:T(8,128)S(1)} %get-tuple-element.63.refs_0_, f32[32,2304]{1,0:T(8,128)S(1)} %get-tuple-element.64.refs_1_, f32[9,9,3,256]{3,2,1,0:T(4,128)S(1)} %bitcast.12, f32[3,20,20]{2,1,0:T(8,128)S(1)} %copy-done.9, f32[3,8,16,128]{3,2,1,0:T(8,128)S(1)} %advection.4.refs_4_.refs_3_), custom_call_target="tpu_custom_call" | custom-call | flops 10000000 | bytes 921280 | tf_op jit(solution)/shard_map/volume/pallas_call | solution.py:31
  62.4 0.7 collective-permute-start.16
  63.1 4.8 %collective-permute-start.18 = (f32[264,128]{1,0:T(8,128)S(1)}, f32[264,128]{1,0:T(8,128)S(1)}, u32[]{:S(2)}, u32[]{:S(2)}) collective-permute-start(f32[264,128]{1,0:T(8,128)S(1)} %get-tuple-element.78.refs_10_), channel_id=1, source_target_pairs={{0,4},{4,0},{8,12},{12,8},{16,20},{20,16},{24,28},{28,24},{1,5},{5... | collective-permute-start | bytes 405512 | tf_op jit(solution)/shard_map/ppermute | solution.py:50
  68.5 1.9 %collective-permute-start.19 = (f32[4,8,4,128]{3,2,1,0:T(4,128)S(1)}, f32[4,8,4,128]{3,2,1,0:T(4,128)S(1)}, u32[]{:S(2)}, u32[]{:S(2)}) collective-permute-start(f32[4,8,4,128]{3,2,1,0:T(4,128)S(1)} %get-tuple-element.83), channel_id=1, source_target_pairs={{0,1},{1,0},{2,3},{3,2},{4,5},{5,4},{6,7},{7,6},{8,9},{9,8},{10,11... | collective-permute-start | bytes 196616 | tf_op jit(solution)/shard_map/ppermute | solution.py:50
  70.4 1.8 %flux.3 = (f32[9,20,256]{2,1,0:T(8,128)S(1)}, f32[8,128]{1,0:T(8,128)S(1)}) custom-call(f32[9,20,256]{2,1,0:T(8,128)S(1)} %get-tuple-element.72.refs_0_, f32[9,16,1024]{2,1,0:T(8,128)S(1)} %get-tuple-element.47.refs_0_.refs_1_, f32[9,16,128]{2,1,0:T(8,128)S(1)} %get-tuple-element.50.refs_2_, f32[9,9,4,256]{3,2,1,0:T(4,128)S(1)} %bitcast.9, ...), custom_call_target="tpu_custom_call" | custom-call | flops 20000000 | bytes 1719424 | tf_op jit(solution)/shard_map/flux/pallas_call | solution.py:31
  73.9 3.1 %collective-permute-start.23 = (f32[72,128]{1,0:T(8,128)S(1)}, f32[72,128]{1,0:T(8,128)S(1)}, u32[]{:S(2)}, u32[]{:S(2)}) collective-permute-start(f32[72,128]{1,0:T(8,128)S(1)} %get-tuple-element.89), channel_id=1, source_target_pairs={{0,1},{1,0},{2,3},{3,2},{4,5},{5,4},{6,7},{7,6},{8,9},{9,8},{10,11... | collective-permute-start | bytes 110600 | tf_op jit(solution)/shard_map/ppermute | solution.py:50
  77.0 4.2 %collective-permute-start.22 = (f32[72,128]{1,0:T(8,128)S(1)}, f32[72,128]{1,0:T(8,128)S(1)}, u32[]{:S(2)}, u32[]{:S(2)}) collective-permute-start(f32[72,128]{1,0:T(8,128)S(1)} %get-tuple-element.85.refs_6_), channel_id=1, source_target_pairs={{0,4},{4,0},{8,12},{12,8},{16,20},{20,16},{24,28},{28,24},{1,5},{5... | collective-permute-start | bytes 110600 | tf_op jit(solution)/shard_map/ppermute | solution.py:50
  81.7 0.9 %replies.1 = f32[9,20,256]{2,1,0:T(8,128)} custom-call(f32[9,20,256]{2,1,0:T(8,128)S(1)} %get-tuple-element.79.refs_0_, f32[9,9,4,256]{3,2,1,0:T(4,128)S(1)} %bitcast.10, f32[10,4,20]{2,1,0:T(4,128)S(1)} %bitcast.16, s32[4,256]{1,0:T(4,128)S(1)} %copy-done.15, s32[5,3,8]{2,1,0:T(4,128)S(1)} %bitcast.19, f32[1,128]{1,0:T(1,128)S(1)} %get-tuple-element.69.refs_7_.refs_5_, ...), custom_call_target="tpu_custom_call" | custom-call | flops 1000000 | bytes 782432 | tf_op jit(solution)/shard_map/replies/pallas_call | solution.py:31
  83.1 1.0 %velocity.3 = f32[4,8,16,128]{3,2,1,0:T(8,128)} custom-call(f32[4,8,16,128]{3,2,1,0:T(8,128)S(1)} %get-tuple-element.80.refs_0_, f32[1,8,16,128]{3,2,1,0:T(8,128)S(1)} %get-tuple-element.86.refs_1_, f32[2,8,16,128]{3,2,1,0:T(8,128)S(1)} %copy-done.2, f32[3,8,16,128]{3,2,1,0:T(8,128)S(1)} %advection.5.refs_8_.refs_3_, ...), custom_call_target="tpu_custom_call" | custom-call | flops 1000000 | bytes 1064960 | tf_op jit(solution)/shard_map/velocity/pallas_call | solution.py:31
  (73 shorter events, 11.9 us)
Async XLA Ops:
  2.5 10.9 %copy-start.6 = (f32[3,9,9,256]{3,0,2,1:T(4,128)S(1)}, f32[3,9,9,256]{3,0,2,1:T(4,128)}, u32[]{:S(2)}) copy-start(f32[3,9,9,256]{3,0,2,1:T(4,128)} %param.14) | copy-start | bytes 746500
  2.5 10.9 %copy-start.9 = (f32[3,20,20]{2,1,0:T(8,128)S(1)}, f32[3,20,20]{2,1,0:T(8,128)}, u32[]{:S(2)}) copy-start(f32[3,20,20]{2,1,0:T(8,128)} %refs_3_.2) | copy-start | bytes 14404
  2.5 10.9 %copy-start.16 = (f32[4,10,20]{2,0,1:T(4,128)S(1)}, f32[4,10,20]{2,0,1:T(4,128)}, u32[]{:S(2)}) copy-start(f32[4,10,20]{2,0,1:T(4,128)} %param.17) | copy-start | bytes 9604
  3.4 13.5 %collective-permute-start = (f32[7,8,4,128]{3,2,1,0:T(4,128)S(1)}, f32[7,8,4,128]{3,2,1,0:T(4,128)S(1)}, u32[]{:S(2)}, u32[]{:S(2)}) collective-permute-start(f32[7,8,4,128]{3,2,1,0:T(4,128)S(1)} %get-tuple-element.48), channel_id=1, source_target_pairs={{1,2},{2,1},{5,6},{6,5},{9,10},{10,9},{13,14},{14,13},{17,18},{18,... | collective-permute-start | bytes 344072 | tf_op jit(solution)/shard_map/ppermute | solution.py:50
  4.0 12.8 %collective-permute-start.1 = (f32[7,8,4,128]{3,2,1,0:T(4,128)S(1)}, f32[7,8,4,128]{3,2,1,0:T(4,128)S(1)}, u32[]{:S(2)}, u32[]{:S(2)}) collective-permute-start(f32[7,8,4,128]{3,2,1,0:T(4,128)S(1)} %get-tuple-element.49), channel_id=1, source_target_pairs={{0,1},{1,0},{2,3},{3,2},{4,5},{5,4},{6,7},{7,6},{8,9},{9,8},{10,11... | collective-permute-start | bytes 344072 | tf_op jit(solution)/shard_map/ppermute | solution.py:50
  8.4 15.5 %collective-permute-start.2 = (f32[7,4,16,128]{3,2,1,0:T(8,128)}, f32[7,4,16,128]{3,2,1,0:T(8,128)S(1)}, u32[]{:S(2)}, u32[]{:S(2)}) collective-permute-start(f32[7,4,16,128]{3,2,1,0:T(8,128)} %get-tuple-element.51), channel_id=1, source_target_pairs={{4,8},{8,4},{12,16},{16,12},{20,24},{24,20},{5,9},{9,5},{13,17},{1... | collective-permute-start | bytes 688136 | tf_op jit(solution)/shard_map/ppermute | solution.py:50
  9.0 14.8 %collective-permute-start.3 = (f32[7,4,16,128]{3,2,1,0:T(8,128)}, f32[7,4,16,128]{3,2,1,0:T(8,128)S(1)}, u32[]{:S(2)}, u32[]{:S(2)}) collective-permute-start(f32[7,4,16,128]{3,2,1,0:T(8,128)} %get-tuple-element.52), channel_id=1, source_target_pairs={{0,4},{4,0},{8,12},{12,8},{16,20},{20,16},{24,28},{28,24},{1,5},{5... | collective-permute-start | bytes 688136 | tf_op jit(solution)/shard_map/ppermute | solution.py:50
  14.3 2.6 %copy-start.17 = (f32[3,5,8]{2,0,1:T(4,128)S(1)}, f32[3,5,8]{2,0,1:T(4,128)}, u32[]{:S(2)}) copy-start(f32[3,5,8]{2,0,1:T(4,128)} %param.22) | copy-start | bytes 1444
  18.5 3.8 %copy-start.18 = (s32[4,128]{1,0:T(4,128)S(1)}, s32[4,128]{1,0:T(4,128)}, u32[]{:S(2)}) copy-start(s32[4,128]{1,0:T(4,128)} %refs_1_.10) | copy-start | bytes 6148
  18.5 18.5 %all-to-all-start = ((f32[32,8,128]{2,1,0:T(8,128)}), f32[32,8,128]{2,1,0:T(8,128)S(1)}, u32[]{:S(2)}, u32[]{:S(2)}) async-start(f32[32,8,128]{2,1,0:T(8,128)} %bitcast.6), calls=%async_computation | async-start | bytes 262144 | tf_op jit(solution)/shard_map/all_to_all | solution.py:638
  25.1 10.0 %collective-permute-start.5 = (f32[168,128]{1,0:T(8,128)S(1)}, f32[168,128]{1,0:T(8,128)S(1)}, u32[]{:S(2)}, u32[]{:S(2)}) collective-permute-start(f32[168,128]{1,0:T(8,128)S(1)} %get-tuple-element.59), channel_id=1, source_target_pairs={{1,2},{2,1},{5,6},{6,5},{9,10},{10,9},{13,14},{14,13},{17,18},{18,... | collective-permute-start | bytes 258056 | tf_op jit(solution)/shard_map/ppermute | solution.py:50
  25.8 9.3 %collective-permute-start.7 = (f32[168,128]{1,0:T(8,128)S(1)}, f32[168,128]{1,0:T(8,128)S(1)}, u32[]{:S(2)}, u32[]{:S(2)}) collective-permute-start(f32[168,128]{1,0:T(8,128)S(1)} %get-tuple-element.61), channel_id=1, source_target_pairs={{0,1},{1,0},{2,3},{3,2},{4,5},{5,4},{6,7},{7,6},{8,9},{9,8},{10,11... | collective-permute-start | bytes 258056 | tf_op jit(solution)/shard_map/ppermute | solution.py:50
  29.0 6.1 %collective-permute-start.4 = (f32[168,128]{1,0:T(8,128)S(1)}, f32[168,128]{1,0:T(8,128)S(1)}, u32[]{:S(2)}, u32[]{:S(2)}) collective-permute-start(f32[168,128]{1,0:T(8,128)S(1)} %get-tuple-element.58.refs_3_), channel_id=1, source_target_pairs={{4,8},{8,4},{12,16},{16,12},{20,24},{24,20},{5,9},{9,5},{13,17},{1... | collective-permute-start | bytes 258056 | tf_op jit(solution)/shard_map/ppermute | solution.py:50
  30.3 6.8 %collective-permute-start.6 = (f32[168,128]{1,0:T(8,128)S(1)}, f32[168,128]{1,0:T(8,128)S(1)}, u32[]{:S(2)}, u32[]{:S(2)}) collective-permute-start(f32[168,128]{1,0:T(8,128)S(1)} %get-tuple-element.60.refs_4_), channel_id=1, source_target_pairs={{0,4},{4,0},{8,12},{12,8},{16,20},{20,16},{24,28},{28,24},{1,5},{5... | collective-permute-start | bytes 258056 | tf_op jit(solution)/shard_map/ppermute | solution.py:50
  38.8 9.8 %copy-start.5 = (f32[4,9,9,256]{3,0,2,1:T(4,128)S(1)}, f32[4,9,9,256]{3,0,2,1:T(4,128)}, u32[]{:S(2)}) copy-start(f32[4,9,9,256]{3,0,2,1:T(4,128)} %param.15) | copy-start | bytes 995332
  38.8 9.8 %copy-start.8 = (f32[4,20,10]{1,0,2:T(4,128)S(1)}, f32[4,20,10]{1,0,2:T(4,128)}, u32[]{:S(2)}) copy-start(f32[4,20,10]{1,0,2:T(4,128)} %param.18) | copy-start | bytes 9604
  39.9 10.5 %collective-permute-start.8 = (f32[264,128]{1,0:T(8,128)S(1)}, f32[264,128]{1,0:T(8,128)S(1)}, u32[]{:S(2)}, u32[]{:S(2)}) collective-permute-start(f32[264,128]{1,0:T(8,128)S(1)} %get-tuple-element.66), channel_id=1, source_target_pairs={{4,8},{8,4},{12,16},{16,12},{20,24},{24,20},{5,9},{9,5},{13,17},{1... | collective-permute-start | bytes 405512 | tf_op jit(solution)/shard_map/ppermute | solution.py:50
  40.6 10.3 %collective-permute-start.10 = (f32[264,128]{1,0:T(8,128)S(1)}, f32[264,128]{1,0:T(8,128)S(1)}, u32[]{:S(2)}, u32[]{:S(2)}) collective-permute-start(f32[264,128]{1,0:T(8,128)S(1)} %get-tuple-element.62.refs_10_), channel_id=1, source_target_pairs={{0,4},{4,0},{8,12},{12,8},{16,20},{20,16},{24,28},{28,24},{1,5},{5... | collective-permute-start | bytes 405512 | tf_op jit(solution)/shard_map/ppermute | solution.py:50
  45.8 4.6 %collective-permute-start.9 = (f32[4,8,4,128]{3,2,1,0:T(4,128)S(1)}, f32[4,8,4,128]{3,2,1,0:T(4,128)S(1)}, u32[]{:S(2)}, u32[]{:S(2)}) collective-permute-start(f32[4,8,4,128]{3,2,1,0:T(4,128)S(1)} %get-tuple-element.67), channel_id=1, source_target_pairs={{1,2},{2,1},{5,6},{6,5},{9,10},{10,9},{13,14},{14,13},{17,18},{18,... | collective-permute-start | bytes 196616 | tf_op jit(solution)/shard_map/ppermute | solution.py:50
  46.5 3.9 %collective-permute-start.11 = (f32[4,8,4,128]{3,2,1,0:T(4,128)S(1)}, f32[4,8,4,128]{3,2,1,0:T(4,128)S(1)}, u32[]{:S(2)}, u32[]{:S(2)}) collective-permute-start(f32[4,8,4,128]{3,2,1,0:T(4,128)S(1)} %get-tuple-element.68), channel_id=1, source_target_pairs={{0,1},{1,0},{2,3},{3,2},{4,5},{5,4},{6,7},{7,6},{8,9},{9,8},{10,11... | collective-permute-start | bytes 196616 | tf_op jit(solution)/shard_map/ppermute | solution.py:50
  51.3 10.5 %collective-permute-start.12 = (f32[72,128]{1,0:T(8,128)S(1)}, f32[72,128]{1,0:T(8,128)S(1)}, u32[]{:S(2)}, u32[]{:S(2)}) collective-permute-start(f32[72,128]{1,0:T(8,128)S(1)} %get-tuple-element.74), channel_id=1, source_target_pairs={{4,8},{8,4},{12,16},{16,12},{20,24},{24,20},{5,9},{9,5},{13,17},{1... | collective-permute-start | bytes 110600 | tf_op jit(solution)/shard_map/ppermute | solution.py:50
  51.9 9.8 %collective-permute-start.13 = (f32[72,128]{1,0:T(8,128)S(1)}, f32[72,128]{1,0:T(8,128)S(1)}, u32[]{:S(2)}, u32[]{:S(2)}) collective-permute-start(f32[72,128]{1,0:T(8,128)S(1)} %get-tuple-element.75), channel_id=1, source_target_pairs={{1,2},{2,1},{5,6},{6,5},{9,10},{10,9},{13,14},{14,13},{17,18},{18,... | collective-permute-start | bytes 110600 | tf_op jit(solution)/shard_map/ppermute | solution.py:50
  52.6 9.2 %collective-permute-start.15 = (f32[72,128]{1,0:T(8,128)S(1)}, f32[72,128]{1,0:T(8,128)S(1)}, u32[]{:S(2)}, u32[]{:S(2)}) collective-permute-start(f32[72,128]{1,0:T(8,128)S(1)} %get-tuple-element.76), channel_id=1, source_target_pairs={{0,1},{1,0},{2,3},{3,2},{4,5},{5,4},{6,7},{7,6},{8,9},{9,8},{10,11... | collective-permute-start | bytes 110600 | tf_op jit(solution)/shard_map/ppermute | solution.py:50
  55.2 6.8 %collective-permute-start.14 = (f32[72,128]{1,0:T(8,128)S(1)}, f32[72,128]{1,0:T(8,128)S(1)}, u32[]{:S(2)}, u32[]{:S(2)}) collective-permute-start(f32[72,128]{1,0:T(8,128)S(1)} %get-tuple-element.71.refs_6_), channel_id=1, source_target_pairs={{0,4},{4,0},{8,12},{12,8},{16,20},{20,16},{24,28},{28,24},{1,5},{5... | collective-permute-start | bytes 110600 | tf_op jit(solution)/shard_map/ppermute | solution.py:50
  62.4 9.8 %collective-permute-start.16 = (f32[264,128]{1,0:T(8,128)S(1)}, f32[264,128]{1,0:T(8,128)S(1)}, u32[]{:S(2)}, u32[]{:S(2)}) collective-permute-start(f32[264,128]{1,0:T(8,128)S(1)} %get-tuple-element.81), channel_id=1, source_target_pairs={{4,8},{8,4},{12,16},{16,12},{20,24},{24,20},{5,9},{9,5},{13,17},{1... | collective-permute-start | bytes 405512 | tf_op jit(solution)/shard_map/ppermute | solution.py:50
  63.1 9.1 %collective-permute-start.18 = (f32[264,128]{1,0:T(8,128)S(1)}, f32[264,128]{1,0:T(8,128)S(1)}, u32[]{:S(2)}, u32[]{:S(2)}) collective-permute-start(f32[264,128]{1,0:T(8,128)S(1)} %get-tuple-element.78.refs_10_), channel_id=1, source_target_pairs={{0,4},{4,0},{8,12},{12,8},{16,20},{20,16},{24,28},{28,24},{1,5},{5... | collective-permute-start | bytes 405512 | tf_op jit(solution)/shard_map/ppermute | solution.py:50
  67.8 4.3 %collective-permute-start.17 = (f32[4,8,4,128]{3,2,1,0:T(4,128)S(1)}, f32[4,8,4,128]{3,2,1,0:T(4,128)S(1)}, u32[]{:S(2)}, u32[]{:S(2)}) collective-permute-start(f32[4,8,4,128]{3,2,1,0:T(4,128)S(1)} %get-tuple-element.82), channel_id=1, source_target_pairs={{1,2},{2,1},{5,6},{6,5},{9,10},{10,9},{13,14},{14,13},{17,18},{18,... | collective-permute-start | bytes 196616 | tf_op jit(solution)/shard_map/ppermute | solution.py:50
  68.5 3.7 %collective-permute-start.19 = (f32[4,8,4,128]{3,2,1,0:T(4,128)S(1)}, f32[4,8,4,128]{3,2,1,0:T(4,128)S(1)}, u32[]{:S(2)}, u32[]{:S(2)}) collective-permute-start(f32[4,8,4,128]{3,2,1,0:T(4,128)S(1)} %get-tuple-element.83), channel_id=1, source_target_pairs={{0,1},{1,0},{2,3},{3,2},{4,5},{5,4},{6,7},{7,6},{8,9},{9,8},{10,11... | collective-permute-start | bytes 196616 | tf_op jit(solution)/shard_map/ppermute | solution.py:50
  72.6 10.0 %collective-permute-start.20 = (f32[72,128]{1,0:T(8,128)S(1)}, f32[72,128]{1,0:T(8,128)S(1)}, u32[]{:S(2)}, u32[]{:S(2)}) collective-permute-start(f32[72,128]{1,0:T(8,128)S(1)} %get-tuple-element.87), channel_id=1, source_target_pairs={{4,8},{8,4},{12,16},{16,12},{20,24},{24,20},{5,9},{9,5},{13,17},{1... | collective-permute-start | bytes 110600 | tf_op jit(solution)/shard_map/ppermute | solution.py:50
  73.3 9.4 %collective-permute-start.21 = (f32[72,128]{1,0:T(8,128)S(1)}, f32[72,128]{1,0:T(8,128)S(1)}, u32[]{:S(2)}, u32[]{:S(2)}) collective-permute-start(f32[72,128]{1,0:T(8,128)S(1)} %get-tuple-element.88), channel_id=1, source_target_pairs={{1,2},{2,1},{5,6},{6,5},{9,10},{10,9},{13,14},{14,13},{17,18},{18,... | collective-permute-start | bytes 110600 | tf_op jit(solution)/shard_map/ppermute | solution.py:50
  73.9 8.7 %collective-permute-start.23 = (f32[72,128]{1,0:T(8,128)S(1)}, f32[72,128]{1,0:T(8,128)S(1)}, u32[]{:S(2)}, u32[]{:S(2)}) collective-permute-start(f32[72,128]{1,0:T(8,128)S(1)} %get-tuple-element.89), channel_id=1, source_target_pairs={{0,1},{1,0},{2,3},{3,2},{4,5},{5,4},{6,7},{7,6},{8,9},{9,8},{10,11... | collective-permute-start | bytes 110600 | tf_op jit(solution)/shard_map/ppermute | solution.py:50
  77.0 6.1 %collective-permute-start.22 = (f32[72,128]{1,0:T(8,128)S(1)}, f32[72,128]{1,0:T(8,128)S(1)}, u32[]{:S(2)}, u32[]{:S(2)}) collective-permute-start(f32[72,128]{1,0:T(8,128)S(1)} %get-tuple-element.85.refs_6_), channel_id=1, source_target_pairs={{0,4},{4,0},{8,12},{12,8},{16,20},{20,16},{24,28},{28,24},{1,5},{5... | collective-permute-start | bytes 110600 | tf_op jit(solution)/shard_map/ppermute | solution.py:50
  (12 other events, 14.5 us)

commit v5 on v4

--- a/solution.py
+++ b/solution.py
@@ -413,8 +413,8 @@
 
 
 def injected_kernel(
-    n_gx, n_gz, air, wind, medium, rxb, rxa, moved, wxb, wzb, wxa, wza, pxb, pzb, pxa, pza, table, smap,
-    out, oxb, ozb, oxa, oza, answer, spread, wide, wide_wind,
+    n_gx, n_gz, air, wind, medium, moved, wxb, wzb, wxa, wza, pxb, pzb, pxa, pza, table, smap,
+    out, oxb, ozb, oxa, oza, answer, spread, wide, wide_wind, ext,
 ):
     nx, nz, ny = air.shape[1:]
     reach, _, slots = smap.shape
@@ -436,9 +436,9 @@
             spread[da * nx:(da + 1) * nx, db * nz:(db + 1) * nz] = block.reshape(nx, nz, ny)
     widen(wide_wind, wind, wxb, wzb, wxa, wza, first=air.shape[0])
     widen_pressure(wide, None, pxb, pzb, pxa, pza)
-    for got, side in zip((rxa, rxb), sides("gx")):
-        rows = got[HEAD:HEAD + RADIUS * nz, :].reshape(RADIUS, nz, ny)
-        wide[pl.ds(RADIUS + side * (nx - RADIUS), RADIUS), ZRIM:ZRIM + nz] = rows
+    widen(ext, air, wxb, wzb, wxa, wza)
+    for x in range(nx):
+        wide[RADIUS + x, ZRIM:ZRIM + nz] = pressure_rows(ext, wind, medium, x, nz)
     load = plane(spread)
     for x in range(nx + 2 * RADIUS):
         xs = x + nx - RADIUS
@@ -648,18 +648,18 @@
     pressure_z = (HEAD + nx * ZRIM, ny)
     both_x = (pressure_x[0] + sent[0], LANES)
     both_z = (pressure_z[0] + sent[0], LANES)
-    raw_xb, zb, raw_xa, za = call(
+    xb, zb, xa, za = call(
         raw_pressure_kernel, "raw_pressure", [both_x, both_z, both_x, both_z],
         [air_state, wind_field, air_medium, *rims, *sent_four], [ext, block], after=[moved],
     )
-    both = exchange(raw_xb, zb, raw_xa, za)
+    both = exchange(xb, zb, xa, za)
     rim_x = (HEAD + 4 * RADIUS * nz, ny)
     rim_z = (4, nx, RADIUS, ny)
     air, xb, zb, xa, za, answer = call(
         functools.partial(injected_kernel, n_gx, n_gz), "injected",
         [air_state.shape, rim_x, rim_z, rim_x, rim_z, (1, LANES)],
-        [air_state, wind_field, air_medium, raw_xb, raw_xa, moved, *rims, *both, lists, surface_map],
-        [(3 * nx, 3 * nz, ny), wide, (3,) + wide],
+        [air_state, wind_field, air_medium, moved, *rims, *both, lists, surface_map],
+        [(3 * nx, 3 * nz, ny), wide, (3,) + wide, ext],
     )
     half = faces // 2
     solid = state

time: 84.8 us -> 80.9 us (0.954)
  local copies, waits for them, and re-layouts: 6.26 us -> 3.21 us
  waiting for transfers between devices: 3.28 us -> 1.77 us
    unnamed x38 -> x30, local copies, waits for them, and re-layouts: 6.26 us -> 3.21 us
    ppermute x24, waiting for transfers between devices: 3.28 us -> 1.77 us  [swap(): return lax.ppermute(values, axis, pairs)]
  transfers between devices with their start and end apart: 25 -> 25, of which waited for: 4 -> 3; matrix products, arithmetic and copies ran while one was open for 0% -> 0% of each run, Pallas kernels for 15% -> 16%
where the time goes in v5:
time: 80.9 us; the launch traced here: 80.3 us
  starting transfers between devices  57.1 us (71%)
  Pallas kernels  17.2 us (21%)
  local copies, waits for them, and re-layouts  3.21 us (4%)
  waiting for transfers between devices  1.77 us (2%)
  between operations  1.03 us (1%)
    ppermute x24, starting transfers between devices, swap(): return lax.ppermute(values, axis, pairs)  53.3 us
    pallas_call x17, Pallas kernels, call(): pl.pallas_call(body, out_shape=[jax.ShapeDtypeStruct(s, F32) for s in out...  17.2 us
    all_to_all x1, starting transfers between devices, shards(): lax.all_to_all(rows, ('gx', 'gz'), split_axis=0, concat_axis=0, tiled=True)  3.79 us
    unnamed x30, local copies, waits for them, and re-layouts  3.21 us
    ppermute x24, waiting for transfers between devices, swap(): return lax.ppermute(values, axis, pairs)  1.77 us
  transfers between devices with their start and end apart: 25, of which 3 were waited for; matrix products, arithmetic and copies ran while one was open for 0% of the time, Pallas kernels for 16%

profile of v5, /device:TPU:0, one launch (start us, length us, event | category | flops | bytes accessed | tf_op | source)
XLA Modules:
  0.0 80.3 jit_solution(2512186121535812825)
XLA Ops:
  0.6 0.9 %copy-done = f32[3,8,16,128]{3,2,1,0:T(8,128)S(1)} copy-done((f32[3,8,16,128]{3,2,1,0:T(8,128)S(1)}, f32[3,8,16,128]{3,2,1,0:T(8,128)}, u32[]{:S(2)}) %copy-start) | copy-done | bytes 196632
  1.6 0.9 %copy-done.3 = f32[4,8,16,128]{3,2,1,0:T(8,128)S(1)} copy-done((f32[4,8,16,128]{3,2,1,0:T(8,128)S(1)}, f32[4,8,16,128]{3,2,1,0:T(8,128)}, u32[]{:S(2)}) %copy-start.3) | copy-done | bytes 262168
  2.5 0.8 %raw_rims.1 = (f32[7,4,16,128]{3,2,1,0:T(8,128)}, f32[7,8,4,128]{3,2,1,0:T(4,128)S(1)}, f32[7,4,16,128]{3,2,1,0:T(8,128)}, f32[7,8,4,128]{3,2,1,0:T(4,128)S(1)}) custom-call(f32[4,8,16,128]{3,2,1,0:T(8,128)S(1)} %copy-done.3, f32[3,8,16,128]{3,2,1,0:T(8,128)S(1)} %copy-done), custom_call_target="tpu_custom_call" | custom-call | flops 1000000 | bytes 1146880 | tf_op jit(solution)/shard_map/raw_rims/pallas_call | solution.py:31
  4.0 4.4 %collective-permute-start.1 = (f32[7,8,4,128]{3,2,1,0:T(4,128)S(1)}, f32[7,8,4,128]{3,2,1,0:T(4,128)S(1)}, u32[]{:S(2)}, u32[]{:S(2)}) collective-permute-start(f32[7,8,4,128]{3,2,1,0:T(4,128)S(1)} %get-tuple-element.49), channel_id=1, source_target_pairs={{0,1},{1,0},{2,3},{3,2},{4,5},{5,4},{6,7},{7,6},{8,9},{9,8},{10,11... | collective-permute-start | bytes 344072 | tf_op jit(solution)/shard_map/ppermute | solution.py:50
  9.0 4.3 %collective-permute-start.3 = (f32[7,4,16,128]{3,2,1,0:T(8,128)}, f32[7,4,16,128]{3,2,1,0:T(8,128)S(1)}, u32[]{:S(2)}, u32[]{:S(2)}) collective-permute-start(f32[7,4,16,128]{3,2,1,0:T(8,128)} %get-tuple-element.52), channel_id=1, source_target_pairs={{0,4},{4,0},{8,12},{12,8},{16,20},{20,16},{24,28},{28,24},{1,5},{5... | collective-permute-start | bytes 688136 | tf_op jit(solution)/shard_map/ppermute | solution.py:50
  13.4 0.9 %copy-done.7 = f32[9,20,256]{2,1,0:T(8,128)S(1)} copy-done((f32[9,20,256]{2,1,0:T(8,128)S(1)}, f32[9,20,256]{2,1,0:T(8,128)}, u32[]{:S(2)}) %copy-start.7) | copy-done | bytes 184344
  14.3 2.5 %predict.1 = (f32[32,2304]{1,0:T(8,128)S(1)}, f32[9,16,1024]{2,1,0:T(8,128)S(1)}, f32[9,20,256]{2,1,0:T(8,128)S(1)}) custom-call(f32[9,20,256]{2,1,0:T(8,128)S(1)} %copy-done.7, f32[9,9,3,256]{3,2,1,0:T(4,128)S(1)} %bitcast.11, f32[3,20,20]{2,1,0:T(8,128)S(1)} %copy-done.9, f32[10,4,20]{2,1,0:T(4,128)S(1)} %bitcast.20), custom_call_target="tpu_custom_call" | custom-call | flops 40000000 | bytes 1510208 | tf_op jit(solution)/shard_map/predict/pallas_call | solution.py:31
  16.9 1.6 %own_list.1 = (f32[9,16,128]{2,1,0:T(8,128)S(1)}, f32[256,128]{1,0:T(8,128)}) custom-call(f32[9,16,1024]{2,1,0:T(8,128)S(1)} %get-tuple-element.47.refs_0_.refs_1_, s32[5,3,8]{2,1,0:T(4,128)S(1)} %bitcast.17, f32[5,3,8]{2,1,0:T(4,128)S(1)} %bitcast.21, f32[7,8,4,128]{3,2,1,0:T(4,128)S(1)} %collective-permute-done.refs_3_.refs_4_.refs_5_, ...), custom_call_target="tpu_custom_call" | custom-call | flops 1000000 | bytes 795584 | tf_op jit(solution)/shard_map/own_list/pallas_call | solution.py:31
  18.5 3.8 %all-to-all-start = ((f32[32,8,128]{2,1,0:T(8,128)}), f32[32,8,128]{2,1,0:T(8,128)S(1)}, u32[]{:S(2)}, u32[]{:S(2)}) async-start(f32[32,8,128]{2,1,0:T(8,128)} %bitcast.6), calls=%async_computation | async-start | bytes 262144 | tf_op jit(solution)/shard_map/all_to_all | solution.py:638
  22.4 1.5 %outgoing.1 = (f32[96,128]{1,0:T(8,128)S(1)}, f32[96,128]{1,0:T(8,128)S(1)}, f32[96,128]{1,0:T(8,128)S(1)}, f32[96,128]{1,0:T(8,128)S(1)}) custom-call(f32[9,16,1024]{2,1,0:T(8,128)S(1)} %get-tuple-element.47.refs_0_.refs_1_, s32[4,128]{1,0:T(4,128)S(1)} %copy-done.14, f32[256,128]{1,0:T(8,128)} %get-tuple-element.53.refs_2_.refs_6_), custom_call_target="tpu_custom_call" | custom-call | flops 10000000 | bytes 788480 | tf_op jit(solution)/shard_map/outgoing/pallas_call | solution.py:31
  25.1 0.7 collective-permute-start.4
  25.8 0.7 collective-permute-start.5
  26.4 4.5 %collective-permute-start.6 = (f32[168,128]{1,0:T(8,128)S(1)}, f32[168,128]{1,0:T(8,128)S(1)}, u32[]{:S(2)}, u32[]{:S(2)}) collective-permute-start(f32[168,128]{1,0:T(8,128)S(1)} %get-tuple-element.60), channel_id=1, source_target_pairs={{0,4},{4,0},{8,12},{12,8},{16,20},{20,16},{24,28},{28,24},{1,5},{5... | collective-permute-start | bytes 258056 | tf_op jit(solution)/shard_map/ppermute | solution.py:50
  31.0 2.5 %collective-permute-start.7 = (f32[168,128]{1,0:T(8,128)S(1)}, f32[168,128]{1,0:T(8,128)S(1)}, u32[]{:S(2)}, u32[]{:S(2)}) collective-permute-start(f32[168,128]{1,0:T(8,128)S(1)} %get-tuple-element.61), channel_id=1, source_target_pairs={{0,1},{1,0},{2,3},{3,2},{4,5},{5,4},{6,7},{7,6},{8,9},{9,8},{10,11... | collective-permute-start | bytes 258056 | tf_op jit(solution)/shard_map/ppermute | solution.py:50
  33.5 0.9 %collective-permute-done.7.refs_11_.refs_9_ = f32[168,128]{1,0:T(8,128)S(1)} collective-permute-done((f32[168,128]{1,0:T(8,128)S(1)}, f32[168,128]{1,0:T(8,128)S(1)}, u32[]{:S(2)}, u32[]{:S(2)}) %collective-permute-start.7) | collective-permute-done | bytes 86048 | tf_op jit(solution)/shard_map/ppermute | solution.py:50
  34.5 1.2 %injected.1 = (f32[4,8,16,128]{3,2,1,0:T(8,128)S(1)}, f32[264,128]{1,0:T(8,128)S(1)}, f32[4,8,4,128]{3,2,1,0:T(4,128)S(1)}, f32[264,128]{1,0:T(8,128)S(1)}, f32[...) custom-call(f32[4,8,16,128]{3,2,1,0:T(8,128)S(1)} %copy-done.4, f32[3,8,16,128]{3,2,1,0:T(8,128)S(1)} %copy-done.1, ...), custom_call_target="tpu_custom_call" | custom-call | flops 1000000 | bytes 2614240 | tf_op jit(solution)/shard_map/injected/pallas_call | solution.py:31
  35.7 0.7 collective-permute-start.8
  36.4 4.2 %collective-permute-start.10 = (f32[264,128]{1,0:T(8,128)S(1)}, f32[264,128]{1,0:T(8,128)S(1)}, u32[]{:S(2)}, u32[]{:S(2)}) collective-permute-start(f32[264,128]{1,0:T(8,128)S(1)} %get-tuple-element.62.refs_10_), channel_id=1, source_target_pairs={{0,4},{4,0},{8,12},{12,8},{16,20},{20,16},{24,28},{28,24},{1,5},{5... | collective-permute-start | bytes 405512 | tf_op jit(solution)/shard_map/ppermute | solution.py:50
  41.3 3.7 %collective-permute-start.11 = (f32[4,8,4,128]{3,2,1,0:T(4,128)S(1)}, f32[4,8,4,128]{3,2,1,0:T(4,128)S(1)}, u32[]{:S(2)}, u32[]{:S(2)}) collective-permute-start(f32[4,8,4,128]{3,2,1,0:T(4,128)S(1)} %get-tuple-element.68), channel_id=1, source_target_pairs={{0,1},{1,0},{2,3},{3,2},{4,5},{5,4},{6,7},{7,6},{8,9},{9,8},{10,11... | collective-permute-start | bytes 196616 | tf_op jit(solution)/shard_map/ppermute | solution.py:50
  45.0 1.8 %flux.2 = (f32[9,20,256]{2,1,0:T(8,128)S(1)}, f32[8,128]{1,0:T(8,128)S(1)}) custom-call(f32[9,20,256]{2,1,0:T(8,128)S(1)} %get-tuple-element.46.refs_0_, f32[9,16,1024]{2,1,0:T(8,128)S(1)} %get-tuple-element.47.refs_0_.refs_1_, f32[9,16,128]{2,1,0:T(8,128)S(1)} %get-tuple-element.50.refs_2_, f32[9,9,4,256]{3,2,1,0:T(4,128)S(1)} %bitcast.8, ...), custom_call_target="tpu_custom_call" | custom-call | flops 20000000 | bytes 1719424 | tf_op jit(solution)/shard_map/flux/pallas_call | solution.py:31
  47.2 0.7 collective-permute-start.12
  48.6 3.1 %collective-permute-start.15 = (f32[72,128]{1,0:T(8,128)S(1)}, f32[72,128]{1,0:T(8,128)S(1)}, u32[]{:S(2)}, u32[]{:S(2)}) collective-permute-start(f32[72,128]{1,0:T(8,128)S(1)} %get-tuple-element.76), channel_id=1, source_target_pairs={{0,1},{1,0},{2,3},{3,2},{4,5},{5,4},{6,7},{7,6},{8,9},{9,8},{10,11... | collective-permute-start | bytes 110600 | tf_op jit(solution)/shard_map/ppermute | solution.py:50
  51.6 4.2 %collective-permute-start.14 = (f32[72,128]{1,0:T(8,128)S(1)}, f32[72,128]{1,0:T(8,128)S(1)}, u32[]{:S(2)}, u32[]{:S(2)}) collective-permute-start(f32[72,128]{1,0:T(8,128)S(1)} %get-tuple-element.71.refs_6_), channel_id=1, source_target_pairs={{0,4},{4,0},{8,12},{12,8},{16,20},{20,16},{24,28},{28,24},{1,5},{5... | collective-permute-start | bytes 110600 | tf_op jit(solution)/shard_map/ppermute | solution.py:50
  56.3 1.1 %volume.1 = (f32[9,20,256]{2,1,0:T(8,128)S(1)}, f32[8,128]{1,0:T(8,128)S(1)}) custom-call(f32[9,20,256]{2,1,0:T(8,128)S(1)} %get-tuple-element.63.refs_0_, f32[32,2304]{1,0:T(8,128)S(1)} %get-tuple-element.64.refs_1_, f32[9,9,3,256]{3,2,1,0:T(4,128)S(1)} %bitcast.12, f32[3,20,20]{2,1,0:T(8,128)S(1)} %copy-done.9, f32[3,8,16,128]{3,2,1,0:T(8,128)S(1)} %advection.4.refs_4_.refs_3_), custom_call_target="tpu_custom_call" | custom-call | flops 10000000 | bytes 921280 | tf_op jit(solution)/shard_map/volume/pallas_call | solution.py:31
  58.1 0.7 collective-permute-start.16
  58.7 4.2 %collective-permute-start.18 = (f32[264,128]{1,0:T(8,128)S(1)}, f32[264,128]{1,0:T(8,128)S(1)}, u32[]{:S(2)}, u32[]{:S(2)}) collective-permute-start(f32[264,128]{1,0:T(8,128)S(1)} %get-tuple-element.78.refs_10_), channel_id=1, source_target_pairs={{0,4},{4,0},{8,12},{12,8},{16,20},{20,16},{24,28},{28,24},{1,5},{5... | collective-permute-start | bytes 405512 | tf_op jit(solution)/shard_map/ppermute | solution.py:50
  63.7 2.3 %collective-permute-start.19 = (f32[4,8,4,128]{3,2,1,0:T(4,128)S(1)}, f32[4,8,4,128]{3,2,1,0:T(4,128)S(1)}, u32[]{:S(2)}, u32[]{:S(2)}) collective-permute-start(f32[4,8,4,128]{3,2,1,0:T(4,128)S(1)} %get-tuple-element.83), channel_id=1, source_target_pairs={{0,1},{1,0},{2,3},{3,2},{4,5},{5,4},{6,7},{7,6},{8,9},{9,8},{10,11... | collective-permute-start | bytes 196616 | tf_op jit(solution)/shard_map/ppermute | solution.py:50
  66.0 1.8 %flux.3 = (f32[9,20,256]{2,1,0:T(8,128)S(1)}, f32[8,128]{1,0:T(8,128)S(1)}) custom-call(f32[9,20,256]{2,1,0:T(8,128)S(1)} %get-tuple-element.72.refs_0_, f32[9,16,1024]{2,1,0:T(8,128)S(1)} %get-tuple-element.47.refs_0_.refs_1_, f32[9,16,128]{2,1,0:T(8,128)S(1)} %get-tuple-element.50.refs_2_, f32[9,9,4,256]{3,2,1,0:T(4,128)S(1)} %bitcast.9, ...), custom_call_target="tpu_custom_call" | custom-call | flops 20000000 | bytes 1719424 | tf_op jit(solution)/shard_map/flux/pallas_call | solution.py:31
  69.6 3.1 %collective-permute-start.23 = (f32[72,128]{1,0:T(8,128)S(1)}, f32[72,128]{1,0:T(8,128)S(1)}, u32[]{:S(2)}, u32[]{:S(2)}) collective-permute-start(f32[72,128]{1,0:T(8,128)S(1)} %get-tuple-element.89), channel_id=1, source_target_pairs={{0,1},{1,0},{2,3},{3,2},{4,5},{5,4},{6,7},{7,6},{8,9},{9,8},{10,11... | collective-permute-start | bytes 110600 | tf_op jit(solution)/shard_map/ppermute | solution.py:50
  72.7 4.7 %collective-permute-start.22 = (f32[72,128]{1,0:T(8,128)S(1)}, f32[72,128]{1,0:T(8,128)S(1)}, u32[]{:S(2)}, u32[]{:S(2)}) collective-permute-start(f32[72,128]{1,0:T(8,128)S(1)} %get-tuple-element.85.refs_6_), channel_id=1, source_target_pairs={{0,4},{4,0},{8,12},{12,8},{16,20},{20,16},{24,28},{28,24},{1,5},{5... | collective-permute-start | bytes 110600 | tf_op jit(solution)/shard_map/ppermute | solution.py:50
  77.9 0.9 %replies.1 = f32[9,20,256]{2,1,0:T(8,128)} custom-call(f32[9,20,256]{2,1,0:T(8,128)S(1)} %get-tuple-element.79.refs_0_, f32[9,9,4,256]{3,2,1,0:T(4,128)S(1)} %bitcast.10, f32[10,4,20]{2,1,0:T(4,128)S(1)} %bitcast.16, s32[4,256]{1,0:T(4,128)S(1)} %copy-done.11, s32[5,3,8]{2,1,0:T(4,128)S(1)} %bitcast.19, f32[1,128]{1,0:T(1,128)S(1)} %get-tuple-element.69.refs_7_.refs_5_, ...), custom_call_target="tpu_custom_call" | custom-call | flops 1000000 | bytes 782432 | tf_op jit(solution)/shard_map/replies/pallas_call | solution.py:31
  79.3 1.0 %velocity.3 = f32[4,8,16,128]{3,2,1,0:T(8,128)} custom-call(f32[4,8,16,128]{3,2,1,0:T(8,128)S(1)} %get-tuple-element.80.refs_0_, f32[1,8,16,128]{3,2,1,0:T(8,128)S(1)} %get-tuple-element.86.refs_1_, f32[2,8,16,128]{3,2,1,0:T(8,128)S(1)} %copy-done.2, f32[3,8,16,128]{3,2,1,0:T(8,128)S(1)} %advection.5.refs_8_.refs_3_, ...), custom_call_target="tpu_custom_call" | custom-call | flops 1000000 | bytes 1064960 | tf_op jit(solution)/shard_map/velocity/pallas_call | solution.py:31
  (65 shorter events, 8.8 us)
Async XLA Ops:
  2.5 10.9 %copy-start.6 = (f32[3,9,9,256]{3,0,2,1:T(4,128)S(1)}, f32[3,9,9,256]{3,0,2,1:T(4,128)}, u32[]{:S(2)}) copy-start(f32[3,9,9,256]{3,0,2,1:T(4,128)} %param.14) | copy-start | bytes 746500
  2.5 10.9 %copy-start.9 = (f32[3,20,20]{2,1,0:T(8,128)S(1)}, f32[3,20,20]{2,1,0:T(8,128)}, u32[]{:S(2)}) copy-start(f32[3,20,20]{2,1,0:T(8,128)} %refs_3_.2) | copy-start | bytes 14404
  2.5 10.9 %copy-start.12 = (f32[4,10,20]{2,0,1:T(4,128)S(1)}, f32[4,10,20]{2,0,1:T(4,128)}, u32[]{:S(2)}) copy-start(f32[4,10,20]{2,0,1:T(4,128)} %param.17) | copy-start | bytes 9604
  3.4 13.5 %collective-permute-start = (f32[7,8,4,128]{3,2,1,0:T(4,128)S(1)}, f32[7,8,4,128]{3,2,1,0:T(4,128)S(1)}, u32[]{:S(2)}, u32[]{:S(2)}) collective-permute-start(f32[7,8,4,128]{3,2,1,0:T(4,128)S(1)} %get-tuple-element.48), channel_id=1, source_target_pairs={{1,2},{2,1},{5,6},{6,5},{9,10},{10,9},{13,14},{14,13},{17,18},{18,... | collective-permute-start | bytes 344072 | tf_op jit(solution)/shard_map/ppermute | solution.py:50
  4.0 12.9 %collective-permute-start.1 = (f32[7,8,4,128]{3,2,1,0:T(4,128)S(1)}, f32[7,8,4,128]{3,2,1,0:T(4,128)S(1)}, u32[]{:S(2)}, u32[]{:S(2)}) collective-permute-start(f32[7,8,4,128]{3,2,1,0:T(4,128)S(1)} %get-tuple-element.49), channel_id=1, source_target_pairs={{0,1},{1,0},{2,3},{3,2},{4,5},{5,4},{6,7},{7,6},{8,9},{9,8},{10,11... | collective-permute-start | bytes 344072 | tf_op jit(solution)/shard_map/ppermute | solution.py:50
  8.4 15.4 %collective-permute-start.2 = (f32[7,4,16,128]{3,2,1,0:T(8,128)}, f32[7,4,16,128]{3,2,1,0:T(8,128)S(1)}, u32[]{:S(2)}, u32[]{:S(2)}) collective-permute-start(f32[7,4,16,128]{3,2,1,0:T(8,128)} %get-tuple-element.51), channel_id=1, source_target_pairs={{4,8},{8,4},{12,16},{16,12},{20,24},{24,20},{5,9},{9,5},{13,17},{1... | collective-permute-start | bytes 688136 | tf_op jit(solution)/shard_map/ppermute | solution.py:50
  9.0 14.8 %collective-permute-start.3 = (f32[7,4,16,128]{3,2,1,0:T(8,128)}, f32[7,4,16,128]{3,2,1,0:T(8,128)S(1)}, u32[]{:S(2)}, u32[]{:S(2)}) collective-permute-start(f32[7,4,16,128]{3,2,1,0:T(8,128)} %get-tuple-element.52), channel_id=1, source_target_pairs={{0,4},{4,0},{8,12},{12,8},{16,20},{20,16},{24,28},{28,24},{1,5},{5... | collective-permute-start | bytes 688136 | tf_op jit(solution)/shard_map/ppermute | solution.py:50
  18.5 3.8 %copy-start.14 = (s32[4,128]{1,0:T(4,128)S(1)}, s32[4,128]{1,0:T(4,128)}, u32[]{:S(2)}) copy-start(s32[4,128]{1,0:T(4,128)} %refs_1_.10) | copy-start | bytes 6148
  18.5 15.9 %all-to-all-start = ((f32[32,8,128]{2,1,0:T(8,128)}), f32[32,8,128]{2,1,0:T(8,128)S(1)}, u32[]{:S(2)}, u32[]{:S(2)}) async-start(f32[32,8,128]{2,1,0:T(8,128)} %bitcast.6), calls=%async_computation | async-start | bytes 262144 | tf_op jit(solution)/shard_map/all_to_all | solution.py:638
  25.1 8.4 %collective-permute-start.4 = (f32[168,128]{1,0:T(8,128)S(1)}, f32[168,128]{1,0:T(8,128)S(1)}, u32[]{:S(2)}, u32[]{:S(2)}) collective-permute-start(f32[168,128]{1,0:T(8,128)S(1)} %get-tuple-element.58), channel_id=1, source_target_pairs={{4,8},{8,4},{12,16},{16,12},{20,24},{24,20},{5,9},{9,5},{13,17},{1... | collective-permute-start | bytes 258056 | tf_op jit(solution)/shard_map/ppermute | solution.py:50
  25.8 7.8 %collective-permute-start.5 = (f32[168,128]{1,0:T(8,128)S(1)}, f32[168,128]{1,0:T(8,128)S(1)}, u32[]{:S(2)}, u32[]{:S(2)}) collective-permute-start(f32[168,128]{1,0:T(8,128)S(1)} %get-tuple-element.59), channel_id=1, source_target_pairs={{1,2},{2,1},{5,6},{6,5},{9,10},{10,9},{13,14},{14,13},{17,18},{18,... | collective-permute-start | bytes 258056 | tf_op jit(solution)/shard_map/ppermute | solution.py:50
  26.4 7.1 %collective-permute-start.6 = (f32[168,128]{1,0:T(8,128)S(1)}, f32[168,128]{1,0:T(8,128)S(1)}, u32[]{:S(2)}, u32[]{:S(2)}) collective-permute-start(f32[168,128]{1,0:T(8,128)S(1)} %get-tuple-element.60), channel_id=1, source_target_pairs={{0,4},{4,0},{8,12},{12,8},{16,20},{20,16},{24,28},{28,24},{1,5},{5... | collective-permute-start | bytes 258056 | tf_op jit(solution)/shard_map/ppermute | solution.py:50
  31.0 3.5 %collective-permute-start.7 = (f32[168,128]{1,0:T(8,128)S(1)}, f32[168,128]{1,0:T(8,128)S(1)}, u32[]{:S(2)}, u32[]{:S(2)}) collective-permute-start(f32[168,128]{1,0:T(8,128)S(1)} %get-tuple-element.61), channel_id=1, source_target_pairs={{0,1},{1,0},{2,3},{3,2},{4,5},{5,4},{6,7},{7,6},{8,9},{9,8},{10,11... | collective-permute-start | bytes 258056 | tf_op jit(solution)/shard_map/ppermute | solution.py:50
  34.5 10.6 %copy-start.5 = (f32[4,9,9,256]{3,0,2,1:T(4,128)S(1)}, f32[4,9,9,256]{3,0,2,1:T(4,128)}, u32[]{:S(2)}) copy-start(f32[4,9,9,256]{3,0,2,1:T(4,128)} %param.15) | copy-start | bytes 995332
  34.5 10.6 %copy-start.8 = (f32[4,20,10]{1,0,2:T(4,128)S(1)}, f32[4,20,10]{1,0,2:T(4,128)}, u32[]{:S(2)}) copy-start(f32[4,20,10]{1,0,2:T(4,128)} %param.18) | copy-start | bytes 9604
  35.7 11.1 %collective-permute-start.8 = (f32[264,128]{1,0:T(8,128)S(1)}, f32[264,128]{1,0:T(8,128)S(1)}, u32[]{:S(2)}, u32[]{:S(2)}) collective-permute-start(f32[264,128]{1,0:T(8,128)S(1)} %get-tuple-element.66), channel_id=1, source_target_pairs={{4,8},{8,4},{12,16},{16,12},{20,24},{24,20},{5,9},{9,5},{13,17},{1... | collective-permute-start | bytes 405512 | tf_op jit(solution)/shard_map/ppermute | solution.py:50
  36.4 10.5 %collective-permute-start.10 = (f32[264,128]{1,0:T(8,128)S(1)}, f32[264,128]{1,0:T(8,128)S(1)}, u32[]{:S(2)}, u32[]{:S(2)}) collective-permute-start(f32[264,128]{1,0:T(8,128)S(1)} %get-tuple-element.62.refs_10_), channel_id=1, source_target_pairs={{0,4},{4,0},{8,12},{12,8},{16,20},{20,16},{24,28},{28,24},{1,5},{5... | collective-permute-start | bytes 405512 | tf_op jit(solution)/shard_map/ppermute | solution.py:50
  40.6 6.2 %collective-permute-start.9 = (f32[4,8,4,128]{3,2,1,0:T(4,128)S(1)}, f32[4,8,4,128]{3,2,1,0:T(4,128)S(1)}, u32[]{:S(2)}, u32[]{:S(2)}) collective-permute-start(f32[4,8,4,128]{3,2,1,0:T(4,128)S(1)} %get-tuple-element.67), channel_id=1, source_target_pairs={{1,2},{2,1},{5,6},{6,5},{9,10},{10,9},{13,14},{14,13},{17,18},{18,... | collective-permute-start | bytes 196616 | tf_op jit(solution)/shard_map/ppermute | solution.py:50
  41.3 3.8 %copy-start.11 = (s32[4,256]{1,0:T(4,128)S(1)}, s32[4,256]{1,0:T(4,128)}, u32[]{:S(2)}) copy-start(s32[4,256]{1,0:T(4,128)} %refs_3_.3) | copy-start | bytes 12292
  41.3 5.5 %collective-permute-start.11 = (f32[4,8,4,128]{3,2,1,0:T(4,128)S(1)}, f32[4,8,4,128]{3,2,1,0:T(4,128)S(1)}, u32[]{:S(2)}, u32[]{:S(2)}) collective-permute-start(f32[4,8,4,128]{3,2,1,0:T(4,128)S(1)} %get-tuple-element.68), channel_id=1, source_target_pairs={{0,1},{1,0},{2,3},{3,2},{4,5},{5,4},{6,7},{7,6},{8,9},{9,8},{10,11... | collective-permute-start | bytes 196616 | tf_op jit(solution)/shard_map/ppermute | solution.py:50
  47.2 10.2 %collective-permute-start.12 = (f32[72,128]{1,0:T(8,128)S(1)}, f32[72,128]{1,0:T(8,128)S(1)}, u32[]{:S(2)}, u32[]{:S(2)}) collective-permute-start(f32[72,128]{1,0:T(8,128)S(1)} %get-tuple-element.74), channel_id=1, source_target_pairs={{4,8},{8,4},{12,16},{16,12},{20,24},{24,20},{5,9},{9,5},{13,17},{1... | collective-permute-start | bytes 110600 | tf_op jit(solution)/shard_map/ppermute | solution.py:50
  47.9 9.5 %collective-permute-start.13 = (f32[72,128]{1,0:T(8,128)S(1)}, f32[72,128]{1,0:T(8,128)S(1)}, u32[]{:S(2)}, u32[]{:S(2)}) collective-permute-start(f32[72,128]{1,0:T(8,128)S(1)} %get-tuple-element.75), channel_id=1, source_target_pairs={{1,2},{2,1},{5,6},{6,5},{9,10},{10,9},{13,14},{14,13},{17,18},{18,... | collective-permute-start | bytes 110600 | tf_op jit(solution)/shard_map/ppermute | solution.py:50
  48.6 8.9 %collective-permute-start.15 = (f32[72,128]{1,0:T(8,128)S(1)}, f32[72,128]{1,0:T(8,128)S(1)}, u32[]{:S(2)}, u32[]{:S(2)}) collective-permute-start(f32[72,128]{1,0:T(8,128)S(1)} %get-tuple-element.76), channel_id=1, source_target_pairs={{0,1},{1,0},{2,3},{3,2},{4,5},{5,4},{6,7},{7,6},{8,9},{9,8},{10,11... | collective-permute-start | bytes 110600 | tf_op jit(solution)/shard_map/ppermute | solution.py:50
  51.6 6.1 %collective-permute-start.14 = (f32[72,128]{1,0:T(8,128)S(1)}, f32[72,128]{1,0:T(8,128)S(1)}, u32[]{:S(2)}, u32[]{:S(2)}) collective-permute-start(f32[72,128]{1,0:T(8,128)S(1)} %get-tuple-element.71.refs_6_), channel_id=1, source_target_pairs={{0,4},{4,0},{8,12},{12,8},{16,20},{20,16},{24,28},{28,24},{1,5},{5... | collective-permute-start | bytes 110600 | tf_op jit(solution)/shard_map/ppermute | solution.py:50
  58.1 9.8 %collective-permute-start.16 = (f32[264,128]{1,0:T(8,128)S(1)}, f32[264,128]{1,0:T(8,128)S(1)}, u32[]{:S(2)}, u32[]{:S(2)}) collective-permute-start(f32[264,128]{1,0:T(8,128)S(1)} %get-tuple-element.81), channel_id=1, source_target_pairs={{4,8},{8,4},{12,16},{16,12},{20,24},{24,20},{5,9},{9,5},{13,17},{1... | collective-permute-start | bytes 405512 | tf_op jit(solution)/shard_map/ppermute | solution.py:50
  58.7 9.1 %collective-permute-start.18 = (f32[264,128]{1,0:T(8,128)S(1)}, f32[264,128]{1,0:T(8,128)S(1)}, u32[]{:S(2)}, u32[]{:S(2)}) collective-permute-start(f32[264,128]{1,0:T(8,128)S(1)} %get-tuple-element.78.refs_10_), channel_id=1, source_target_pairs={{0,4},{4,0},{8,12},{12,8},{16,20},{20,16},{24,28},{28,24},{1,5},{5... | collective-permute-start | bytes 405512 | tf_op jit(solution)/shard_map/ppermute | solution.py:50
  63.0 4.8 %collective-permute-start.17 = (f32[4,8,4,128]{3,2,1,0:T(4,128)S(1)}, f32[4,8,4,128]{3,2,1,0:T(4,128)S(1)}, u32[]{:S(2)}, u32[]{:S(2)}) collective-permute-start(f32[4,8,4,128]{3,2,1,0:T(4,128)S(1)} %get-tuple-element.82), channel_id=1, source_target_pairs={{1,2},{2,1},{5,6},{6,5},{9,10},{10,9},{13,14},{14,13},{17,18},{18,... | collective-permute-start | bytes 196616 | tf_op jit(solution)/shard_map/ppermute | solution.py:50
  63.7 4.2 %collective-permute-start.19 = (f32[4,8,4,128]{3,2,1,0:T(4,128)S(1)}, f32[4,8,4,128]{3,2,1,0:T(4,128)S(1)}, u32[]{:S(2)}, u32[]{:S(2)}) collective-permute-start(f32[4,8,4,128]{3,2,1,0:T(4,128)S(1)} %get-tuple-element.83), channel_id=1, source_target_pairs={{0,1},{1,0},{2,3},{3,2},{4,5},{5,4},{6,7},{7,6},{8,9},{9,8},{10,11... | collective-permute-start | bytes 196616 | tf_op jit(solution)/shard_map/ppermute | solution.py:50
  68.2 10.5 %collective-permute-start.20 = (f32[72,128]{1,0:T(8,128)S(1)}, f32[72,128]{1,0:T(8,128)S(1)}, u32[]{:S(2)}, u32[]{:S(2)}) collective-permute-start(f32[72,128]{1,0:T(8,128)S(1)} %get-tuple-element.87), channel_id=1, source_target_pairs={{4,8},{8,4},{12,16},{16,12},{20,24},{24,20},{5,9},{9,5},{13,17},{1... | collective-permute-start | bytes 110600 | tf_op jit(solution)/shard_map/ppermute | solution.py:50
  68.9 9.9 %collective-permute-start.21 = (f32[72,128]{1,0:T(8,128)S(1)}, f32[72,128]{1,0:T(8,128)S(1)}, u32[]{:S(2)}, u32[]{:S(2)}) collective-permute-start(f32[72,128]{1,0:T(8,128)S(1)} %get-tuple-element.88), channel_id=1, source_target_pairs={{1,2},{2,1},{5,6},{6,5},{9,10},{10,9},{13,14},{14,13},{17,18},{18,... | collective-permute-start | bytes 110600 | tf_op jit(solution)/shard_map/ppermute | solution.py:50
  69.6 9.2 %collective-permute-start.23 = (f32[72,128]{1,0:T(8,128)S(1)}, f32[72,128]{1,0:T(8,128)S(1)}, u32[]{:S(2)}, u32[]{:S(2)}) collective-permute-start(f32[72,128]{1,0:T(8,128)S(1)} %get-tuple-element.89), channel_id=1, source_target_pairs={{0,1},{1,0},{2,3},{3,2},{4,5},{5,4},{6,7},{7,6},{8,9},{9,8},{10,11... | collective-permute-start | bytes 110600 | tf_op jit(solution)/shard_map/ppermute | solution.py:50
  72.7 6.6 %collective-permute-start.22 = (f32[72,128]{1,0:T(8,128)S(1)}, f32[72,128]{1,0:T(8,128)S(1)}, u32[]{:S(2)}, u32[]{:S(2)}) collective-permute-start(f32[72,128]{1,0:T(8,128)S(1)} %get-tuple-element.85.refs_6_), channel_id=1, source_target_pairs={{0,4},{4,0},{8,12},{12,8},{16,20},{20,16},{24,28},{28,24},{1,5},{5... | collective-permute-start | bytes 110600 | tf_op jit(solution)/shard_map/ppermute | solution.py:50
  (8 other events, 11.9 us)

commit v6 on v5

--- a/solution.py
+++ b/solution.py
@@ -281,24 +281,35 @@
             traces[q, :, f * width:(f + 1) * width] = done[f * 16:(f + 1) * 16]
 
 
-def own_list_kernel(traces, smap, normals, own, rows, spread):
-    quants, _, all_slots = traces.shape
+def own_list_kernel(traces, smap, normals, rows, spread, own):
+    all_slots = traces.shape[2]
     slots = flat_slots(smap, spread)
     wanted = jnp.broadcast_to(slots[0:1].astype(jnp.int32), (16, LANES))
 
     def gather(q, carry):
-        own[q] = take_slots([traces[q, :, s * LANES:(s + 1) * LANES] for s in range(all_slots // LANES)], wanted)
+        own[q] = take_slots([traces[6 + q, :, s * LANES:(s + 1) * LANES] for s in range(all_slots // LANES)], wanted)
         return carry
 
-    lax.fori_loop(0, quants, gather, 0)
+    lax.fori_loop(0, 3, gather, 0)
     normal = flat_slots(normals, spread)
     speed = jnp.zeros((1, LANES), F32)
     for c in range(3):
-        mean = jnp.sum(own[6 + c, 0:FACE_ROWS, :], axis=0, keepdims=True) * (1.0 / FACE_ROWS)
+        mean = jnp.sum(own[c, 0:FACE_ROWS, :], axis=0, keepdims=True) * (1.0 / FACE_ROWS)
         speed = speed + normal[c:c + 1] * mean
     lane = lax.broadcasted_iota(jnp.int32, (1, LANES), 1)
     cells = pltpu.roll(slots[1:2], LANES // 2, 1)
     rows[...] = jnp.broadcast_to(jnp.where(lane < LANES // 2, slots[2:3] * speed, cells), rows.shape)
+
+
+def own_traces_kernel(traces, smap, own, spread):
+    quants, _, all_slots = traces.shape
+    wanted = jnp.broadcast_to(flat_slots(smap, spread)[0:1].astype(jnp.int32), (16, LANES))
+
+    def gather(q, carry):
+        own[q] = take_slots([traces[q, :, s * LANES:(s + 1) * LANES] for s in range(all_slots // LANES)], wanted)
+        return carry
+
+    lax.fori_loop(0, quants, gather, 0)
 
 
 def outgoing_kernel(traces, sends, xa, xb, za, zb, picked):
@@ -630,19 +641,15 @@
         [(K, quants * width), (dims * pad, quants * width), (dims * pad, LANES), (faces * 16, LANES)],
         flops=40_000_000,
     )
-    own, rows = call(
-        own_list_kernel, "own_list", [(quants, 16, LANES), (n_gx * n_gz * 8, LANES)],
-        [traces, surface_map, surface_normals], [(surface_map.shape[0], 8, LANES)],
+    (rows,) = call(
+        own_list_kernel, "own_list", [(n_gx * n_gz * 8, LANES)],
+        [traces, surface_map, surface_normals], [(surface_map.shape[0], 8, LANES), (3, 16, LANES)],
         after=[rims[1], rims[3]],
     )
     lists = lax.all_to_all(rows, ("gx", "gz"), split_axis=0, concat_axis=0, tiled=True)
     sent_four = call(
         outgoing_kernel, "outgoing", [sent, sent, sent, sent], [traces, send_faces],
         [(4, quants, 16, LANES)], flops=10_000_000, after=[rows],
-    )
-    (moved,) = call(
-        advection_kernel, "advection", [(3, nx, nz, ny)],
-        [air_state, wind_field, *rims], [ext], flops=10_000_000, after=[rows],
     )
     pressure_x = (HEAD + RADIUS * nz, ny)
     pressure_z = (HEAD + nx * ZRIM, ny)
@@ -650,16 +657,25 @@
     both_z = (pressure_z[0] + sent[0], LANES)
     xb, zb, xa, za = call(
         raw_pressure_kernel, "raw_pressure", [both_x, both_z, both_x, both_z],
-        [air_state, wind_field, air_medium, *rims, *sent_four], [ext, block], after=[moved],
+        [air_state, wind_field, air_medium, *rims, *sent_four], [ext, block],
     )
     both = exchange(xb, zb, xa, za)
+    (moved,) = call(
+        advection_kernel, "advection", [(3, nx, nz, ny)],
+        [air_state, wind_field, *rims], [ext], flops=10_000_000, after=[xa],
+    )
+    (own,) = call(
+        own_traces_kernel, "own_traces", [(quants, 16, LANES)], [traces, surface_map],
+        [(surface_map.shape[0], 8, LANES)], after=[xa],
+    )
+
     rim_x = (HEAD + 4 * RADIUS * nz, ny)
     rim_z = (4, nx, RADIUS, ny)
     air, xb, zb, xa, za, answer = call(
         functools.partial(injected_kernel, n_gx, n_gz), "injected",
         [air_state.shape, rim_x, rim_z, rim_x, rim_z, (1, LANES)],
         [air_state, wind_field, air_medium, moved, *rims, *both, lists, surface_map],
-        [(3 * nx, 3 * nz, ny), wide, (3,) + wide, ext],
+        [(3 * nx, 3 * nz, ny), wide, (3,) + wide, ext], after=[own],
     )
     half = faces // 2
     solid = state

time: 80.9 us -> 79 us (0.977)
  starting transfers between devices: 57.1 us -> 55.6 us
    ppermute x24, starting transfers between devices: 53.3 us -> 51.8 us  [swap(): return lax.ppermute(values, axis, pairs)]
    pallas_call x17 -> x18, Pallas kernels: 17.2 us -> 16.7 us  [call(): pl.pallas_call(body, out_shape=[jax.ShapeDtypeStruct(s, F32) for s in out...]
  transfers between devices with their start and end apart: 25 -> 25, of which waited for: 3 -> 4; matrix products, arithmetic and copies ran while one was open for 0% -> 0% of each run, Pallas kernels for 16% -> 17%
where the time goes in v6:
time: 79 us; the launch traced here: 78.5 us
  starting transfers between devices  55.6 us (70%)
  Pallas kernels  16.7 us (21%)
  local copies, waits for them, and re-layouts  2.86 us (4%)
  waiting for transfers between devices  2.25 us (3%)
  between operations  1.05 us (1%)
    ppermute x24, starting transfers between devices, swap(): return lax.ppermute(values, axis, pairs)  51.8 us
    pallas_call x18, Pallas kernels, call(): pl.pallas_call(body, out_shape=[jax.ShapeDtypeStruct(s, F32) for s in out...  16.7 us
    all_to_all x1, starting transfers between devices, shards(): lax.all_to_all(rows, ('gx', 'gz'), split_axis=0, concat_axis=0, tiled=True)  3.8 us
    unnamed x30, local copies, waits for them, and re-layouts  2.86 us
    ppermute x24, waiting for transfers between devices, swap(): return lax.ppermute(values, axis, pairs)  2.25 us
  transfers between devices with their start and end apart: 25, of which 4 were waited for; matrix products, arithmetic and copies ran while one was open for 0% of the time, Pallas kernels for 17%

profile of v6, /device:TPU:0, one launch (start us, length us, event | category | flops | bytes accessed | tf_op | source)
XLA Modules:
  0.0 78.5 jit_solution(4652933559832828113)
XLA Ops:
  0.6 0.9 %copy-done = f32[3,8,16,128]{3,2,1,0:T(8,128)S(1)} copy-done((f32[3,8,16,128]{3,2,1,0:T(8,128)S(1)}, f32[3,8,16,128]{3,2,1,0:T(8,128)}, u32[]{:S(2)}) %copy-start) | copy-done | bytes 196632
  1.6 0.9 %copy-done.3 = f32[4,8,16,128]{3,2,1,0:T(8,128)S(1)} copy-done((f32[4,8,16,128]{3,2,1,0:T(8,128)S(1)}, f32[4,8,16,128]{3,2,1,0:T(8,128)}, u32[]{:S(2)}) %copy-start.3) | copy-done | bytes 262168
  2.6 0.8 %collective-permute-start.1 = (f32[7,8,4,128]{3,2,1,0:T(4,128)S(1)}, f32[7,8,4,128]{3,2,1,0:T(4,128)S(1)}, u32[]{:S(2)}, u32[]{:S(2)}) collective-permute-start(f32[7,8,4,128]{3,2,1,0:T(4,128)S(1)} %get-tuple-element.47), channel_id=1, source_target_pairs={{1,2},{2,1},{5,6},{6,5},{9,10},{10,9},{13,14},{14,13},{17,18},{18,... | collective-permute-start | bytes 344072 | tf_op jit(solution)/shard_map/ppermute | solution.py:50
  3.4 4.4 %collective-permute-start.3 = (f32[7,8,4,128]{3,2,1,0:T(4,128)S(1)}, f32[7,8,4,128]{3,2,1,0:T(4,128)S(1)}, u32[]{:S(2)}, u32[]{:S(2)}) collective-permute-start(f32[7,8,4,128]{3,2,1,0:T(4,128)S(1)} %get-tuple-element.49), channel_id=1, source_target_pairs={{0,1},{1,0},{2,3},{3,2},{4,5},{5,4},{6,7},{7,6},{8,9},{9,8},{10,11... | collective-permute-start | bytes 344072 | tf_op jit(solution)/shard_map/ppermute | solution.py:50
  8.4 4.3 %collective-permute-start.2 = (f32[7,4,16,128]{3,2,1,0:T(8,128)S(1)}, f32[7,4,16,128]{3,2,1,0:T(8,128)S(1)}, u32[]{:S(2)}, u32[]{:S(2)}) collective-permute-start(f32[7,4,16,128]{3,2,1,0:T(8,128)S(1)} %get-tuple-element.48), channel_id=1, source_target_pairs={{0,4},{4,0},{8,12},{12,8},{16,20},{20,16},{24,28},{28,24},{1,5},{5... | collective-permute-start | bytes 688136 | tf_op jit(solution)/shard_map/ppermute | solution.py:50
  12.8 0.9 %copy-done.7 = f32[9,20,256]{2,1,0:T(8,128)S(1)} copy-done((f32[9,20,256]{2,1,0:T(8,128)S(1)}, f32[9,20,256]{2,1,0:T(8,128)}, u32[]{:S(2)}) %copy-start.7) | copy-done | bytes 184344
  13.7 2.5 %predict.1 = (f32[32,2304]{1,0:T(8,128)S(1)}, f32[9,16,1024]{2,1,0:T(8,128)S(1)}, f32[9,20,256]{2,1,0:T(8,128)S(1)}) custom-call(f32[9,20,256]{2,1,0:T(8,128)S(1)} %copy-done.7, f32[9,9,3,256]{3,2,1,0:T(4,128)S(1)} %bitcast.11, f32[3,20,20]{2,1,0:T(8,128)S(1)} %copy-done.10, f32[10,4,20]{2,1,0:T(4,128)S(1)} %bitcast.21), custom_call_target="tpu_custom_call" | custom-call | flops 40000000 | bytes 1510208 | tf_op jit(solution)/shard_map/predict/pallas_call | solution.py:31
  16.3 1.1 %own_list.1.refs_2_ = f32[256,128]{1,0:T(8,128)} custom-call(f32[9,16,1024]{2,1,0:T(8,128)S(1)} %get-tuple-element.45.refs_0_.refs_1_, s32[5,3,8]{2,1,0:T(4,128)S(1)} %bitcast.17, f32[5,3,8]{2,1,0:T(4,128)S(1)} %bitcast.22, f32[7,8,4,128]{3,2,1,0:T(4,128)S(1)} %collective-permute-done.1.refs_3_.refs_4_.refs_5_, ...), custom_call_target="tpu_custom_call" | custom-call | flops 1000000 | bytes 721856 | tf_op jit(solution)/shard_map/own_list/pallas_call | solution.py:31
  17.3 3.8 %all-to-all-start = ((f32[32,8,128]{2,1,0:T(8,128)}), f32[32,8,128]{2,1,0:T(8,128)S(1)}, u32[]{:S(2)}, u32[]{:S(2)}) async-start(f32[32,8,128]{2,1,0:T(8,128)} %bitcast.6), calls=%async_computation | async-start | bytes 262144 | tf_op jit(solution)/shard_map/all_to_all | solution.py:649
  21.2 1.5 %outgoing.1 = (f32[96,128]{1,0:T(8,128)S(1)}, f32[96,128]{1,0:T(8,128)S(1)}, f32[96,128]{1,0:T(8,128)S(1)}, f32[96,128]{1,0:T(8,128)S(1)}) custom-call(f32[9,16,1024]{2,1,0:T(8,128)S(1)} %get-tuple-element.45.refs_0_.refs_1_, s32[4,128]{1,0:T(4,128)S(1)} %copy-done.14, f32[256,128]{1,0:T(8,128)} %own_list.1.refs_2_), custom_call_target="tpu_custom_call" | custom-call | flops 10000000 | bytes 788480 | tf_op jit(solution)/shard_map/outgoing/pallas_call | solution.py:31
  23.7 0.7 collective-permute-start.5
  24.4 3.2 %collective-permute-start.7 = (f32[168,128]{1,0:T(8,128)S(1)}, f32[168,128]{1,0:T(8,128)S(1)}, u32[]{:S(2)}, u32[]{:S(2)}) collective-permute-start(f32[168,128]{1,0:T(8,128)S(1)} %get-tuple-element.57), channel_id=1, source_target_pairs={{0,1},{1,0},{2,3},{3,2},{4,5},{5,4},{6,7},{7,6},{8,9},{9,8},{10,11... | collective-permute-start | bytes 258056 | tf_op jit(solution)/shard_map/ppermute | solution.py:50
  27.6 4.2 %collective-permute-start.6 = (f32[168,128]{1,0:T(8,128)S(1)}, f32[168,128]{1,0:T(8,128)S(1)}, u32[]{:S(2)}, u32[]{:S(2)}) collective-permute-start(f32[168,128]{1,0:T(8,128)S(1)} %get-tuple-element.54.refs_2_.refs_6_), channel_id=1, source_target_pairs={{0,4},{4,0},{8,12},{12,8},{16,20},{20,16},{24,28},{28,24},{1,5},{5... | collective-permute-start | bytes 258056 | tf_op jit(solution)/shard_map/ppermute | solution.py:50
  31.8 0.9 %own_traces.1.refs_14_.refs_2_ = f32[9,16,128]{2,1,0:T(8,128)S(1)} custom-call(f32[9,16,1024]{2,1,0:T(8,128)S(1)} %get-tuple-element.45.refs_0_.refs_1_, s32[5,3,8]{2,1,0:T(4,128)S(1)} %bitcast.18, f32[168,128]{1,0:T(8,128)S(1)} %get-tuple-element.54.refs_2_.refs_6_), custom_call_target="tpu_custom_call" | custom-call | flops 1000000 | bytes 664032 | tf_op jit(solution)/shard_map/own_traces/pallas_call | solution.py:31
  33.2 1.3 %collective-permute-done.6.refs_10_.refs_8_ = f32[168,128]{1,0:T(8,128)S(1)} collective-permute-done((f32[168,128]{1,0:T(8,128)S(1)}, f32[168,128]{1,0:T(8,128)S(1)}, u32[]{:S(2)}, u32[]{:S(2)}) %collective-permute-start.6) | collective-permute-done | bytes 86048 | tf_op jit(solution)/shard_map/ppermute | solution.py:50
  34.6 1.2 %injected.1 = (f32[4,8,16,128]{3,2,1,0:T(8,128)S(1)}, f32[264,128]{1,0:T(8,128)S(1)}, f32[4,8,4,128]{3,2,1,0:T(4,128)S(1)}, f32[264,128]{1,0:T(8,128)S(1)}, f32[...) custom-call(f32[4,8,16,128]{3,2,1,0:T(8,128)S(1)} %copy-done.4, f32[3,8,16,128]{3,2,1,0:T(8,128)S(1)} %copy-done.1, ...), custom_call_target="tpu_custom_call" | custom-call | flops 1000000 | bytes 2614240 | tf_op jit(solution)/shard_map/injected/pallas_call | solution.py:31
  35.8 0.7 collective-permute-start.8
  36.5 4.5 %collective-permute-start.10 = (f32[264,128]{1,0:T(8,128)S(1)}, f32[264,128]{1,0:T(8,128)S(1)}, u32[]{:S(2)}, u32[]{:S(2)}) collective-permute-start(f32[264,128]{1,0:T(8,128)S(1)} %get-tuple-element.58.refs_10_), channel_id=1, source_target_pairs={{0,4},{4,0},{8,12},{12,8},{16,20},{20,16},{24,28},{28,24},{1,5},{5... | collective-permute-start | bytes 405512 | tf_op jit(solution)/shard_map/ppermute | solution.py:50
  41.0 0.8 collective-permute-start.9
  41.8 1.8 %collective-permute-start.11 = (f32[4,8,4,128]{3,2,1,0:T(4,128)S(1)}, f32[4,8,4,128]{3,2,1,0:T(4,128)S(1)}, u32[]{:S(2)}, u32[]{:S(2)}) collective-permute-start(f32[4,8,4,128]{3,2,1,0:T(4,128)S(1)} %get-tuple-element.64), channel_id=1, source_target_pairs={{0,1},{1,0},{2,3},{3,2},{4,5},{5,4},{6,7},{7,6},{8,9},{9,8},{10,11... | collective-permute-start | bytes 196616 | tf_op jit(solution)/shard_map/ppermute | solution.py:50
  43.6 1.8 %flux.2 = (f32[9,20,256]{2,1,0:T(8,128)S(1)}, f32[8,128]{1,0:T(8,128)S(1)}) custom-call(f32[9,20,256]{2,1,0:T(8,128)S(1)} %get-tuple-element.44.refs_0_, f32[9,16,1024]{2,1,0:T(8,128)S(1)} %get-tuple-element.45.refs_0_.refs_1_, f32[9,16,128]{2,1,0:T(8,128)S(1)} %own_traces.1.refs_14_.refs_2_, f32[9,9,4,256]{3,2,1,0:T(4,128)S(1)} %bitcast.8, ...), custom_call_target="tpu_custom_call" | custom-call | flops 20000000 | bytes 1719424 | tf_op jit(solution)/shard_map/flux/pallas_call | solution.py:31
  47.2 3.0 %collective-permute-start.15 = (f32[72,128]{1,0:T(8,128)S(1)}, f32[72,128]{1,0:T(8,128)S(1)}, u32[]{:S(2)}, u32[]{:S(2)}) collective-permute-start(f32[72,128]{1,0:T(8,128)S(1)} %get-tuple-element.72), channel_id=1, source_target_pairs={{0,1},{1,0},{2,3},{3,2},{4,5},{5,4},{6,7},{7,6},{8,9},{9,8},{10,11... | collective-permute-start | bytes 110600 | tf_op jit(solution)/shard_map/ppermute | solution.py:50
  50.2 4.4 %collective-permute-start.14 = (f32[72,128]{1,0:T(8,128)S(1)}, f32[72,128]{1,0:T(8,128)S(1)}, u32[]{:S(2)}, u32[]{:S(2)}) collective-permute-start(f32[72,128]{1,0:T(8,128)S(1)} %get-tuple-element.67.refs_6_), channel_id=1, source_target_pairs={{0,4},{4,0},{8,12},{12,8},{16,20},{20,16},{24,28},{28,24},{1,5},{5... | collective-permute-start | bytes 110600 | tf_op jit(solution)/shard_map/ppermute | solution.py:50
  55.1 1.1 %volume.1 = (f32[9,20,256]{2,1,0:T(8,128)S(1)}, f32[8,128]{1,0:T(8,128)S(1)}) custom-call(f32[9,20,256]{2,1,0:T(8,128)S(1)} %get-tuple-element.59.refs_0_, f32[32,2304]{1,0:T(8,128)S(1)} %get-tuple-element.60.refs_1_, f32[9,9,3,256]{3,2,1,0:T(4,128)S(1)} %bitcast.12, f32[3,20,20]{2,1,0:T(8,128)S(1)} %copy-done.10, f32[3,8,16,128]{3,2,1,0:T(8,128)S(1)} %advection.4.refs_4_.refs_3_), custom_call_target="tpu_custom_call" | custom-call | flops 10000000 | bytes 921280 | tf_op jit(solution)/shard_map/volume/pallas_call | solution.py:31
  56.9 0.7 collective-permute-start.16
  57.5 4.8 %collective-permute-start.18 = (f32[264,128]{1,0:T(8,128)S(1)}, f32[264,128]{1,0:T(8,128)S(1)}, u32[]{:S(2)}, u32[]{:S(2)}) collective-permute-start(f32[264,128]{1,0:T(8,128)S(1)} %get-tuple-element.74.refs_10_), channel_id=1, source_target_pairs={{0,4},{4,0},{8,12},{12,8},{16,20},{20,16},{24,28},{28,24},{1,5},{5... | collective-permute-start | bytes 405512 | tf_op jit(solution)/shard_map/ppermute | solution.py:50
  63.0 1.7 %collective-permute-start.19 = (f32[4,8,4,128]{3,2,1,0:T(4,128)S(1)}, f32[4,8,4,128]{3,2,1,0:T(4,128)S(1)}, u32[]{:S(2)}, u32[]{:S(2)}) collective-permute-start(f32[4,8,4,128]{3,2,1,0:T(4,128)S(1)} %get-tuple-element.79), channel_id=1, source_target_pairs={{0,1},{1,0},{2,3},{3,2},{4,5},{5,4},{6,7},{7,6},{8,9},{9,8},{10,11... | collective-permute-start | bytes 196616 | tf_op jit(solution)/shard_map/ppermute | solution.py:50
  64.7 1.8 %flux.3 = (f32[9,20,256]{2,1,0:T(8,128)S(1)}, f32[8,128]{1,0:T(8,128)S(1)}) custom-call(f32[9,20,256]{2,1,0:T(8,128)S(1)} %get-tuple-element.68.refs_0_, f32[9,16,1024]{2,1,0:T(8,128)S(1)} %get-tuple-element.45.refs_0_.refs_1_, f32[9,16,128]{2,1,0:T(8,128)S(1)} %own_traces.1.refs_14_.refs_2_, f32[9,9,4,256]{3,2,1,0:T(4,128)S(1)} %bitcast.9, ...), custom_call_target="tpu_custom_call" | custom-call | flops 20000000 | bytes 1719424 | tf_op jit(solution)/shard_map/flux/pallas_call | solution.py:31
  68.3 3.1 %collective-permute-start.23 = (f32[72,128]{1,0:T(8,128)S(1)}, f32[72,128]{1,0:T(8,128)S(1)}, u32[]{:S(2)}, u32[]{:S(2)}) collective-permute-start(f32[72,128]{1,0:T(8,128)S(1)} %get-tuple-element.85), channel_id=1, source_target_pairs={{0,1},{1,0},{2,3},{3,2},{4,5},{5,4},{6,7},{7,6},{8,9},{9,8},{10,11... | collective-permute-start | bytes 110600 | tf_op jit(solution)/shard_map/ppermute | solution.py:50
  71.4 4.2 %collective-permute-start.22 = (f32[72,128]{1,0:T(8,128)S(1)}, f32[72,128]{1,0:T(8,128)S(1)}, u32[]{:S(2)}, u32[]{:S(2)}) collective-permute-start(f32[72,128]{1,0:T(8,128)S(1)} %get-tuple-element.81.refs_6_), channel_id=1, source_target_pairs={{0,4},{4,0},{8,12},{12,8},{16,20},{20,16},{24,28},{28,24},{1,5},{5... | collective-permute-start | bytes 110600 | tf_op jit(solution)/shard_map/ppermute | solution.py:50
  76.1 0.9 %replies.1 = f32[9,20,256]{2,1,0:T(8,128)} custom-call(f32[9,20,256]{2,1,0:T(8,128)S(1)} %get-tuple-element.75.refs_0_, f32[9,9,4,256]{3,2,1,0:T(4,128)S(1)} %bitcast.10, f32[10,4,20]{2,1,0:T(4,128)S(1)} %bitcast.16, s32[4,256]{1,0:T(4,128)S(1)} %copy-done.11, s32[5,3,8]{2,1,0:T(4,128)S(1)} %bitcast.20, f32[1,128]{1,0:T(1,128)S(1)} %get-tuple-element.65.refs_7_.refs_5_, ...), custom_call_target="tpu_custom_call" | custom-call | flops 1000000 | bytes 782432 | tf_op jit(solution)/shard_map/replies/pallas_call | solution.py:31
  77.5 1.0 %velocity.3 = f32[4,8,16,128]{3,2,1,0:T(8,128)} custom-call(f32[4,8,16,128]{3,2,1,0:T(8,128)S(1)} %get-tuple-element.76.refs_0_, f32[1,8,16,128]{3,2,1,0:T(8,128)S(1)} %get-tuple-element.82.refs_1_, f32[2,8,16,128]{3,2,1,0:T(8,128)S(1)} %copy-done.2, f32[3,8,16,128]{3,2,1,0:T(8,128)S(1)} %advection.5.refs_8_.refs_3_, ...), custom_call_target="tpu_custom_call" | custom-call | flops 1000000 | bytes 1064960 | tf_op jit(solution)/shard_map/velocity/pallas_call | solution.py:31
  (66 shorter events, 8.7 us)
Async XLA Ops:
  2.5 10.3 %copy-start.6 = (f32[3,9,9,256]{3,0,2,1:T(4,128)S(1)}, f32[3,9,9,256]{3,0,2,1:T(4,128)}, u32[]{:S(2)}) copy-start(f32[3,9,9,256]{3,0,2,1:T(4,128)} %param.14) | copy-start | bytes 746500
  2.5 10.3 %copy-start.10 = (f32[3,20,20]{2,1,0:T(8,128)S(1)}, f32[3,20,20]{2,1,0:T(8,128)}, u32[]{:S(2)}) copy-start(f32[3,20,20]{2,1,0:T(8,128)} %refs_3_.2) | copy-start | bytes 14404
  2.5 10.3 %copy-start.12 = (f32[4,10,20]{2,0,1:T(4,128)S(1)}, f32[4,10,20]{2,0,1:T(4,128)}, u32[]{:S(2)}) copy-start(f32[4,10,20]{2,0,1:T(4,128)} %param.17) | copy-start | bytes 9604
  2.6 13.6 %collective-permute-start.1 = (f32[7,8,4,128]{3,2,1,0:T(4,128)S(1)}, f32[7,8,4,128]{3,2,1,0:T(4,128)S(1)}, u32[]{:S(2)}, u32[]{:S(2)}) collective-permute-start(f32[7,8,4,128]{3,2,1,0:T(4,128)S(1)} %get-tuple-element.47), channel_id=1, source_target_pairs={{1,2},{2,1},{5,6},{6,5},{9,10},{10,9},{13,14},{14,13},{17,18},{18,... | collective-permute-start | bytes 344072 | tf_op jit(solution)/shard_map/ppermute | solution.py:50
  3.4 12.8 %collective-permute-start.3 = (f32[7,8,4,128]{3,2,1,0:T(4,128)S(1)}, f32[7,8,4,128]{3,2,1,0:T(4,128)S(1)}, u32[]{:S(2)}, u32[]{:S(2)}) collective-permute-start(f32[7,8,4,128]{3,2,1,0:T(4,128)S(1)} %get-tuple-element.49), channel_id=1, source_target_pairs={{0,1},{1,0},{2,3},{3,2},{4,5},{5,4},{6,7},{7,6},{8,9},{9,8},{10,11... | collective-permute-start | bytes 344072 | tf_op jit(solution)/shard_map/ppermute | solution.py:50
  7.8 14.9 %collective-permute-start = (f32[7,4,16,128]{3,2,1,0:T(8,128)S(1)}, f32[7,4,16,128]{3,2,1,0:T(8,128)S(1)}, u32[]{:S(2)}, u32[]{:S(2)}) collective-permute-start(f32[7,4,16,128]{3,2,1,0:T(8,128)S(1)} %get-tuple-element.46), channel_id=1, source_target_pairs={{4,8},{8,4},{12,16},{16,12},{20,24},{24,20},{5,9},{9,5},{13,17},{1... | collective-permute-start | bytes 688136 | tf_op jit(solution)/shard_map/ppermute | solution.py:50
  8.4 14.2 %collective-permute-start.2 = (f32[7,4,16,128]{3,2,1,0:T(8,128)S(1)}, f32[7,4,16,128]{3,2,1,0:T(8,128)S(1)}, u32[]{:S(2)}, u32[]{:S(2)}) collective-permute-start(f32[7,4,16,128]{3,2,1,0:T(8,128)S(1)} %get-tuple-element.48), channel_id=1, source_target_pairs={{0,4},{4,0},{8,12},{12,8},{16,20},{20,16},{24,28},{28,24},{1,5},{5... | collective-permute-start | bytes 688136 | tf_op jit(solution)/shard_map/ppermute | solution.py:50
  17.3 3.8 %copy-start.14 = (s32[4,128]{1,0:T(4,128)S(1)}, s32[4,128]{1,0:T(4,128)}, u32[]{:S(2)}) copy-start(s32[4,128]{1,0:T(4,128)} %refs_1_.10) | copy-start | bytes 6148
  17.3 17.2 %all-to-all-start = ((f32[32,8,128]{2,1,0:T(8,128)}), f32[32,8,128]{2,1,0:T(8,128)S(1)}, u32[]{:S(2)}, u32[]{:S(2)}) async-start(f32[32,8,128]{2,1,0:T(8,128)} %bitcast.6), calls=%async_computation | async-start | bytes 262144 | tf_op jit(solution)/shard_map/all_to_all | solution.py:649
  23.1 10.1 %collective-permute-start.4 = (f32[168,128]{1,0:T(8,128)S(1)}, f32[168,128]{1,0:T(8,128)S(1)}, u32[]{:S(2)}, u32[]{:S(2)}) collective-permute-start(f32[168,128]{1,0:T(8,128)S(1)} %get-tuple-element.55), channel_id=1, source_target_pairs={{4,8},{8,4},{12,16},{16,12},{20,24},{24,20},{5,9},{9,5},{13,17},{1... | collective-permute-start | bytes 258056 | tf_op jit(solution)/shard_map/ppermute | solution.py:50
  23.7 9.5 %collective-permute-start.5 = (f32[168,128]{1,0:T(8,128)S(1)}, f32[168,128]{1,0:T(8,128)S(1)}, u32[]{:S(2)}, u32[]{:S(2)}) collective-permute-start(f32[168,128]{1,0:T(8,128)S(1)} %get-tuple-element.56), channel_id=1, source_target_pairs={{1,2},{2,1},{5,6},{6,5},{9,10},{10,9},{13,14},{14,13},{17,18},{18,... | collective-permute-start | bytes 258056 | tf_op jit(solution)/shard_map/ppermute | solution.py:50
  24.4 8.8 %collective-permute-start.7 = (f32[168,128]{1,0:T(8,128)S(1)}, f32[168,128]{1,0:T(8,128)S(1)}, u32[]{:S(2)}, u32[]{:S(2)}) collective-permute-start(f32[168,128]{1,0:T(8,128)S(1)} %get-tuple-element.57), channel_id=1, source_target_pairs={{0,1},{1,0},{2,3},{3,2},{4,5},{5,4},{6,7},{7,6},{8,9},{9,8},{10,11... | collective-permute-start | bytes 258056 | tf_op jit(solution)/shard_map/ppermute | solution.py:50
  27.6 6.9 %collective-permute-start.6 = (f32[168,128]{1,0:T(8,128)S(1)}, f32[168,128]{1,0:T(8,128)S(1)}, u32[]{:S(2)}, u32[]{:S(2)}) collective-permute-start(f32[168,128]{1,0:T(8,128)S(1)} %get-tuple-element.54.refs_2_.refs_6_), channel_id=1, source_target_pairs={{0,4},{4,0},{8,12},{12,8},{16,20},{20,16},{24,28},{28,24},{1,5},{5... | collective-permute-start | bytes 258056 | tf_op jit(solution)/shard_map/ppermute | solution.py:50
  34.6 9.0 %copy-start.5 = (f32[4,9,9,256]{3,0,2,1:T(4,128)S(1)}, f32[4,9,9,256]{3,0,2,1:T(4,128)}, u32[]{:S(2)}) copy-start(f32[4,9,9,256]{3,0,2,1:T(4,128)} %param.15) | copy-start | bytes 995332
  34.6 9.0 %copy-start.8 = (f32[4,20,10]{1,0,2:T(4,128)S(1)}, f32[4,20,10]{1,0,2:T(4,128)}, u32[]{:S(2)}) copy-start(f32[4,20,10]{1,0,2:T(4,128)} %param.18) | copy-start | bytes 9604
  35.8 9.6 %collective-permute-start.8 = (f32[264,128]{1,0:T(8,128)S(1)}, f32[264,128]{1,0:T(8,128)S(1)}, u32[]{:S(2)}, u32[]{:S(2)}) collective-permute-start(f32[264,128]{1,0:T(8,128)S(1)} %get-tuple-element.62), channel_id=1, source_target_pairs={{4,8},{8,4},{12,16},{16,12},{20,24},{24,20},{5,9},{9,5},{13,17},{1... | collective-permute-start | bytes 405512 | tf_op jit(solution)/shard_map/ppermute | solution.py:50
  36.5 9.0 %collective-permute-start.10 = (f32[264,128]{1,0:T(8,128)S(1)}, f32[264,128]{1,0:T(8,128)S(1)}, u32[]{:S(2)}, u32[]{:S(2)}) collective-permute-start(f32[264,128]{1,0:T(8,128)S(1)} %get-tuple-element.58.refs_10_), channel_id=1, source_target_pairs={{0,4},{4,0},{8,12},{12,8},{16,20},{20,16},{24,28},{28,24},{1,5},{5... | collective-permute-start | bytes 405512 | tf_op jit(solution)/shard_map/ppermute | solution.py:50
  41.0 2.6 %copy-start.11 = (s32[4,256]{1,0:T(4,128)S(1)}, s32[4,256]{1,0:T(4,128)}, u32[]{:S(2)}) copy-start(s32[4,256]{1,0:T(4,128)} %refs_3_.3) | copy-start | bytes 12292
  41.0 4.4 %collective-permute-start.9 = (f32[4,8,4,128]{3,2,1,0:T(4,128)S(1)}, f32[4,8,4,128]{3,2,1,0:T(4,128)S(1)}, u32[]{:S(2)}, u32[]{:S(2)}) collective-permute-start(f32[4,8,4,128]{3,2,1,0:T(4,128)S(1)} %get-tuple-element.63), channel_id=1, source_target_pairs={{1,2},{2,1},{5,6},{6,5},{9,10},{10,9},{13,14},{14,13},{17,18},{18,... | collective-permute-start | bytes 196616 | tf_op jit(solution)/shard_map/ppermute | solution.py:50
  41.8 3.6 %collective-permute-start.11 = (f32[4,8,4,128]{3,2,1,0:T(4,128)S(1)}, f32[4,8,4,128]{3,2,1,0:T(4,128)S(1)}, u32[]{:S(2)}, u32[]{:S(2)}) collective-permute-start(f32[4,8,4,128]{3,2,1,0:T(4,128)S(1)} %get-tuple-element.64), channel_id=1, source_target_pairs={{0,1},{1,0},{2,3},{3,2},{4,5},{5,4},{6,7},{7,6},{8,9},{9,8},{10,11... | collective-permute-start | bytes 196616 | tf_op jit(solution)/shard_map/ppermute | solution.py:50
  45.9 10.4 %collective-permute-start.12 = (f32[72,128]{1,0:T(8,128)S(1)}, f32[72,128]{1,0:T(8,128)S(1)}, u32[]{:S(2)}, u32[]{:S(2)}) collective-permute-start(f32[72,128]{1,0:T(8,128)S(1)} %get-tuple-element.70), channel_id=1, source_target_pairs={{4,8},{8,4},{12,16},{16,12},{20,24},{24,20},{5,9},{9,5},{13,17},{1... | collective-permute-start | bytes 110600 | tf_op jit(solution)/shard_map/ppermute | solution.py:50
  46.5 9.7 %collective-permute-start.13 = (f32[72,128]{1,0:T(8,128)S(1)}, f32[72,128]{1,0:T(8,128)S(1)}, u32[]{:S(2)}, u32[]{:S(2)}) collective-permute-start(f32[72,128]{1,0:T(8,128)S(1)} %get-tuple-element.71), channel_id=1, source_target_pairs={{1,2},{2,1},{5,6},{6,5},{9,10},{10,9},{13,14},{14,13},{17,18},{18,... | collective-permute-start | bytes 110600 | tf_op jit(solution)/shard_map/ppermute | solution.py:50
  47.2 9.0 %collective-permute-start.15 = (f32[72,128]{1,0:T(8,128)S(1)}, f32[72,128]{1,0:T(8,128)S(1)}, u32[]{:S(2)}, u32[]{:S(2)}) collective-permute-start(f32[72,128]{1,0:T(8,128)S(1)} %get-tuple-element.72), channel_id=1, source_target_pairs={{0,1},{1,0},{2,3},{3,2},{4,5},{5,4},{6,7},{7,6},{8,9},{9,8},{10,11... | collective-permute-start | bytes 110600 | tf_op jit(solution)/shard_map/ppermute | solution.py:50
  50.2 6.3 %collective-permute-start.14 = (f32[72,128]{1,0:T(8,128)S(1)}, f32[72,128]{1,0:T(8,128)S(1)}, u32[]{:S(2)}, u32[]{:S(2)}) collective-permute-start(f32[72,128]{1,0:T(8,128)S(1)} %get-tuple-element.67.refs_6_), channel_id=1, source_target_pairs={{0,4},{4,0},{8,12},{12,8},{16,20},{20,16},{24,28},{28,24},{1,5},{5... | collective-permute-start | bytes 110600 | tf_op jit(solution)/shard_map/ppermute | solution.py:50
  56.9 9.7 %collective-permute-start.16 = (f32[264,128]{1,0:T(8,128)S(1)}, f32[264,128]{1,0:T(8,128)S(1)}, u32[]{:S(2)}, u32[]{:S(2)}) collective-permute-start(f32[264,128]{1,0:T(8,128)S(1)} %get-tuple-element.77), channel_id=1, source_target_pairs={{4,8},{8,4},{12,16},{16,12},{20,24},{24,20},{5,9},{9,5},{13,17},{1... | collective-permute-start | bytes 405512 | tf_op jit(solution)/shard_map/ppermute | solution.py:50
  57.5 9.0 %collective-permute-start.18 = (f32[264,128]{1,0:T(8,128)S(1)}, f32[264,128]{1,0:T(8,128)S(1)}, u32[]{:S(2)}, u32[]{:S(2)}) collective-permute-start(f32[264,128]{1,0:T(8,128)S(1)} %get-tuple-element.74.refs_10_), channel_id=1, source_target_pairs={{0,4},{4,0},{8,12},{12,8},{16,20},{20,16},{24,28},{28,24},{1,5},{5... | collective-permute-start | bytes 405512 | tf_op jit(solution)/shard_map/ppermute | solution.py:50
  62.3 4.2 %collective-permute-start.17 = (f32[4,8,4,128]{3,2,1,0:T(4,128)S(1)}, f32[4,8,4,128]{3,2,1,0:T(4,128)S(1)}, u32[]{:S(2)}, u32[]{:S(2)}) collective-permute-start(f32[4,8,4,128]{3,2,1,0:T(4,128)S(1)} %get-tuple-element.78), channel_id=1, source_target_pairs={{1,2},{2,1},{5,6},{6,5},{9,10},{10,9},{13,14},{14,13},{17,18},{18,... | collective-permute-start | bytes 196616 | tf_op jit(solution)/shard_map/ppermute | solution.py:50
  63.0 3.5 %collective-permute-start.19 = (f32[4,8,4,128]{3,2,1,0:T(4,128)S(1)}, f32[4,8,4,128]{3,2,1,0:T(4,128)S(1)}, u32[]{:S(2)}, u32[]{:S(2)}) collective-permute-start(f32[4,8,4,128]{3,2,1,0:T(4,128)S(1)} %get-tuple-element.79), channel_id=1, source_target_pairs={{0,1},{1,0},{2,3},{3,2},{4,5},{5,4},{6,7},{7,6},{8,9},{9,8},{10,11... | collective-permute-start | bytes 196616 | tf_op jit(solution)/shard_map/ppermute | solution.py:50
  66.9 10.0 %collective-permute-start.20 = (f32[72,128]{1,0:T(8,128)S(1)}, f32[72,128]{1,0:T(8,128)S(1)}, u32[]{:S(2)}, u32[]{:S(2)}) collective-permute-start(f32[72,128]{1,0:T(8,128)S(1)} %get-tuple-element.83), channel_id=1, source_target_pairs={{4,8},{8,4},{12,16},{16,12},{20,24},{24,20},{5,9},{9,5},{13,17},{1... | collective-permute-start | bytes 110600 | tf_op jit(solution)/shard_map/ppermute | solution.py:50
  67.6 9.4 %collective-permute-start.21 = (f32[72,128]{1,0:T(8,128)S(1)}, f32[72,128]{1,0:T(8,128)S(1)}, u32[]{:S(2)}, u32[]{:S(2)}) collective-permute-start(f32[72,128]{1,0:T(8,128)S(1)} %get-tuple-element.84), channel_id=1, source_target_pairs={{1,2},{2,1},{5,6},{6,5},{9,10},{10,9},{13,14},{14,13},{17,18},{18,... | collective-permute-start | bytes 110600 | tf_op jit(solution)/shard_map/ppermute | solution.py:50
  68.3 8.7 %collective-permute-start.23 = (f32[72,128]{1,0:T(8,128)S(1)}, f32[72,128]{1,0:T(8,128)S(1)}, u32[]{:S(2)}, u32[]{:S(2)}) collective-permute-start(f32[72,128]{1,0:T(8,128)S(1)} %get-tuple-element.85), channel_id=1, source_target_pairs={{0,1},{1,0},{2,3},{3,2},{4,5},{5,4},{6,7},{7,6},{8,9},{9,8},{10,11... | collective-permute-start | bytes 110600 | tf_op jit(solution)/shard_map/ppermute | solution.py:50
  71.4 6.1 %collective-permute-start.22 = (f32[72,128]{1,0:T(8,128)S(1)}, f32[72,128]{1,0:T(8,128)S(1)}, u32[]{:S(2)}, u32[]{:S(2)}) collective-permute-start(f32[72,128]{1,0:T(8,128)S(1)} %get-tuple-element.81.refs_6_), channel_id=1, source_target_pairs={{0,4},{4,0},{8,12},{12,8},{16,20},{20,16},{24,28},{28,24},{1,5},{5... | collective-permute-start | bytes 110600 | tf_op jit(solution)/shard_map/ppermute | solution.py:50
  (8 other events, 12.5 us)
